TPU v7x, 256 devices: a whole 4x4x8 slice. The times are simulated.
256 devices in a mesh: space: 16 (over y, z_hi, core), batch: 16 (over z_lo, x).
Axes of the slice: x: 4, y: 4, z: 8 (z_hi: 2, z_lo: 4; z = z_hi * 4 + z_lo), core: 2. Of those that a mesh axis runs over, the one named last changes fastest.
Arguments:
- activations: bfloat16 [16, 48, 16, 16, 128], P('batch', 'space'), may hold values from -6 to 6
- conv1_weight: bfloat16 [3, 3, 128, 128], replicated, may hold values from -0.1875 to 0.1875
- conv2_weight: bfloat16 [3, 3, 128, 128], replicated, may hold values from -0.1875 to 0.1875
- coarse_kernel_weight: bfloat16 [2, 2, 128, 128], replicated, may hold values from -0.25 to 0.25
- skip_cotangent: bfloat16 [16, 48, 16, 16, 128], P('batch', 'space'), may hold values from -6 to 6
- down_cotangent: bfloat16 [16, 48, 8, 8, 128], P('batch', 'space'), may hold values from -6 to 6
- face_neighbours: int32 [48, 4], replicated, may hold values from 0 to 47, as said below
- seam_codes: int32 [48, 4], replicated, may hold values from 0 to 7, as said below
- tile_slots: int32 [48], replicated, may hold values from 0 to 47, each once
Outputs:
- coarse_field: bfloat16 [16, 48, 8, 8, 128], P('batch', 'space')
- input_grad: bfloat16 [16, 48, 16, 16, 128], P('batch', 'space')
- conv1_grad: float32 [3, 3, 128, 128], replicated
- conv2_grad: float32 [3, 3, 128, 128], replicated
- down_grad: float32 [2, 2, 128, 128], replicated
Inputs may be any that keep to these rules, and one draw needn't show every extreme that they name: `face_neighbours`: sides pair up: if side s of tile t names tile u with code c, then side c // 2 of tile u names tile t with code 2 s + c % 2. Every tile is named by some side. `seam_codes`: c // 2 is the touching side of the named tile; c % 2 = 1 means its row runs the opposite way. `tile_slots`: each slot holds one tile.
All inputs are finite; a program needn't handle non-finite values.
Results may differ from a plain program's by a relative error of at most 0.009.
Values may be sent and summed in bfloat16 or wider, within the bound.
No kernel may reach another device: no remote copies, remote signals or barrier semaphores. Data moves between devices by JAX's collectives and lax.ppermute only.
A program may use at most 64 MiB of HBM per device.

v0:
```python
import math

import jax
import jax.numpy as jnp
from jax import lax
from jax.sharding import PartitionSpec as P


def edge_rows(value_entries):
    return jnp.stack(
        [
            value_entries[:, 0],
            value_entries[:, :, -1],
            value_entries[:, -1],
            value_entries[:, :, 0],
        ],
        axis=1,
    )


def orient(picked, reverse):
    return jnp.where(reverse[:, :, None, None] == 1, picked[:, :, ::-1], picked)


def attach(value_entries, seams):
    number = value_entries.shape[0]
    channels = value_entries.shape[-1]
    corner = jnp.zeros((number, 1, channels), value_entries.dtype)
    top_row = jnp.concatenate([corner, seams[:, 0], corner], axis=1)[:, None]
    bottom = jnp.concatenate([corner, seams[:, 2], corner], axis=1)[:, None]
    middle = jnp.concatenate(
        [seams[:, 3][:, :, None], value_entries, seams[:, 1][:, :, None]], axis=2
    )
    return jnp.concatenate([top_row, middle, bottom], axis=1)


def convolve(padded, weight_tensor):
    number = padded.shape[0]
    extent = padded.shape[1] - 2
    channels = weight_tensor.shape[-1]
    running = jnp.zeros((number * extent * extent, channels), jnp.float32)
    for a in range(3):
        for b in range(3):
            window = padded[:, a : a + extent, b : b + extent].reshape(-1, padded.shape[-1])
            running = running + jnp.dot(
                window, weight_tensor[a, b], preferred_element_type=jnp.float32
            )
    return running.reshape(number, extent, extent, channels)


def flipped(weight_tensor):
    return jnp.transpose(weight_tensor[::-1, ::-1], (0, 1, 3, 2))


def kernel_grad(padded, cotangent):
    extent = cotangent.shape[1]
    flattened = cotangent.reshape(-1, cotangent.shape[-1])
    kernel_rows = []
    for a in range(3):
        row_parts = []
        for b in range(3):
            window = padded[:, a : a + extent, b : b + extent].reshape(-1, padded.shape[-1])
            row_parts.append(
                lax.dot_general(
                    window, flattened, (((0,), (0,)), ((), ())), preferred_element_type=jnp.float32
                )
            )
        kernel_rows.append(jnp.stack(row_parts))
    return jnp.stack(kernel_rows)


def halve_resolution(value_entries, weight_tensor):
    number, extent, _, channels = value_entries.shape
    reduced = extent // 2
    blocks = value_entries.reshape(number, reduced, 2, reduced, 2, channels)
    running = jnp.zeros((number * reduced * reduced, channels), jnp.float32)
    for a in range(2):
        for b in range(2):
            running = running + jnp.dot(
                blocks[:, :, a, :, b].reshape(-1, channels),
                weight_tensor[a, b],
                preferred_element_type=jnp.float32,
            )
    return running.reshape(number, reduced, reduced, channels)


def down_back(cotangent, weight_tensor):
    number, reduced, _, channels = cotangent.shape
    flattened = cotangent.reshape(-1, channels)
    halves = []
    for a in range(2):
        parts_b = [
            jnp.dot(flattened, weight_tensor[a, b].T, preferred_element_type=jnp.float32).reshape(
                number, reduced, reduced, channels
            )
            for b in range(2)
        ]
        halves.append(jnp.stack(parts_b, axis=3))
    return jnp.stack(halves, axis=2).reshape(number, 2 * reduced, 2 * reduced, channels)


def down_kernel_grad(value_entries, cotangent):
    number, extent, _, channels = value_entries.shape
    reduced = extent // 2
    blocks = value_entries.reshape(number, reduced, 2, reduced, 2, channels)
    flattened = cotangent.reshape(-1, channels)
    kernel_rows = []
    for a in range(2):
        row_parts = []
        for b in range(2):
            window = blocks[:, :, a, :, b].reshape(-1, channels)
            row_parts.append(
                lax.dot_general(
                    window, flattened, (((0,), (0,)), ((), ())), preferred_element_type=jnp.float32
                )
            )
        kernel_rows.append(jnp.stack(row_parts))
    return jnp.stack(kernel_rows)


def gelu_back(preact, cotangent):
    return jax.vjp(jax.nn.gelu, preact)[1](cotangent)[0]


def add_sides(interior, returned_rows):
    interior = interior.at[:, 0].add(returned_rows[:, 0])
    interior = interior.at[:, :, -1].add(returned_rows[:, 1])
    interior = interior.at[:, -1].add(returned_rows[:, 2])
    return interior.at[:, :, 0].add(returned_rows[:, 3])


def side_kernels(weight_tensor):
    return [weight_tensor[0], weight_tensor[:, 2], weight_tensor[2], weight_tensor[:, 0]]


def edge_conv(border, triple):
    number, extent, channels = border.shape
    blank = jnp.zeros((number, 1, channels), border.dtype)
    leading = jnp.concatenate([border[:, 1:], blank], axis=1).reshape(-1, channels)
    trailing = jnp.concatenate([blank, border[:, :-1]], axis=1).reshape(-1, channels)
    running = jnp.dot(leading, triple[0].T, preferred_element_type=jnp.float32)
    running = running + jnp.dot(
        border.reshape(-1, channels), triple[1].T, preferred_element_type=jnp.float32
    )
    running = running + jnp.dot(trailing, triple[2].T, preferred_element_type=jnp.float32)
    return running.reshape(number, extent, channels)


def shards(
    activations,
    conv1_weight,
    conv2_weight,
    coarse_kernel_weight,
    skip_cotangent,
    down_cotangent,
    face_neighbours,
    seam_codes,
    tile_slots,
):
    value_entries = activations[0]
    tiles_here = value_entries.shape[0]
    extent = value_entries.shape[1]
    total_tiles = tile_slots.shape[0]
    first_slot = lax.axis_index("space") * tiles_here
    own_slots = first_slot + jnp.arange(tiles_here, dtype=jnp.int32)
    matches = tile_slots[None, :] == own_slots[:, None]
    own_tiles = jnp.sum(
        jnp.where(matches, jnp.arange(total_tiles, dtype=jnp.int32)[None, :], 0), axis=1
    )
    own_codes = seam_codes[own_tiles]
    source_slot = tile_slots[face_neighbours[own_tiles]]
    source_side = own_codes // 2
    reverse = own_codes % 2

    def seams_of(field_values):
        gathered = lax.all_gather(edge_rows(field_values), "space", axis=0, tiled=True)
        return orient(gathered[source_slot, source_side], reverse)

    def adjoint(cotangent, weight_tensor):
        narrow = jnp.pad(cotangent, ((0, 0), (1, 1), (1, 1), (0, 0)))
        interior = convolve(narrow, flipped(weight_tensor))
        triples = side_kernels(weight_tensor)
        own_edges = edge_rows(cotangent)
        rim_terms = jnp.stack(
            [edge_conv(own_edges[:, facing], triples[facing]) for facing in range(4)], axis=1
        )
        gathered = lax.all_gather(
            rim_terms.astype(jnp.bfloat16), "space", axis=0, tiled=True
        ).astype(rim_terms.dtype)
        returned_rows = orient(gathered[source_slot, source_side], reverse)
        return add_sides(interior, returned_rows)

    grad_scale = 1.0 / math.sqrt(
        lax.axis_size("batch") * lax.axis_size("space") * tiles_here * extent * extent
    )
    initial_padded_tile = attach(value_entries, seams_of(value_entries))
    first_pre = convolve(initial_padded_tile, conv1_weight)
    first_act = jax.nn.gelu(first_pre).astype(jnp.bfloat16)
    second_pad = attach(first_act, seams_of(first_act))
    second_pre = convolve(second_pad, conv2_weight)
    later_activation = jax.nn.gelu(second_pre).astype(jnp.bfloat16)
    coarse_field = halve_resolution(later_activation, coarse_kernel_weight).astype(jnp.bfloat16)
    down_part = down_cotangent[0]
    second_cot = skip_cotangent[0].astype(jnp.float32) + down_back(down_part, coarse_kernel_weight)
    second_delta = gelu_back(second_pre, second_cot).astype(jnp.bfloat16)
    down_grad = down_kernel_grad(later_activation, down_part) * grad_scale
    second_grad = kernel_grad(second_pad, second_delta) * grad_scale
    first_cot = adjoint(second_delta, conv2_weight)
    first_delta = gelu_back(first_pre, first_cot).astype(jnp.bfloat16)
    first_grad = kernel_grad(initial_padded_tile, first_delta) * grad_scale
    input_grad = adjoint(first_delta, conv1_weight).astype(jnp.bfloat16)
    first_grad, second_grad, down_grad = lax.psum(
        (first_grad, second_grad, down_grad), ("space", "batch")
    )
    return (coarse_field[None], input_grad[None], first_grad, second_grad, down_grad)


def solution(mesh):
    return jax.shard_map(
        shards,
        mesh=mesh,
        in_specs=(
            P("batch", "space", None, None, None),
            P(),
            P(),
            P(),
            P("batch", "space", None, None, None),
            P("batch", "space", None, None, None),
            P(),
            P(),
            P(),
        ),
        out_specs=(
            P("batch", "space", None, None, None),
            P("batch", "space", None, None, None),
            P(),
            P(),
            P(),
        ),
        check_vma=False,
    )
```

profile of v0, /device:TPU:1, one launch (start us, length us, event | category | flops | bytes accessed | tf_op | source)
XLA Modules:
  0.0 446.1 jit_solution(10252342259678449248)
XLA Ops:
  7.2 1.0 fusion.226
  8.2 0.7 fusion.225
  9.0 43.1 %all_gather.12 = bf16[48,4,16,128]{3,2,1,0:T(8,128)(2,1)S(1)} all-gather(bf16[3,4,16,128]{3,2,1,0:T(8,128)(2,1)S(1)} %pad_maximum_fusion.7), channel_id=1, replica_groups=mesh['space'=16,'batch'=16] {'space'}, dimensions={0}, use_global_device_ids=true | all-gather | bytes 835584 | tf_op jit(solution)/shard_map/all_gather | solution.py:176
  52.1 0.9 select_reduce_fusion
  53.0 0.8 copy.311
  53.8 0.8 copy.315
  54.6 0.6 gather_fusion
  55.1 0.6 gather_fusion.1
  55.8 0.7 gather_fusion.2
  56.7 0.6 gather_fusion.3
  58.4 0.5 copy-done.4
  61.9 30.4 %all_gather.13 = bf16[48,4,16,128]{3,2,0,1:T(8,128)(2,1)S(1)} all-gather(bf16[3,4,16,128]{3,2,0,1:T(8,128)(2,1)S(1)} %pad_maximum_fusion.8), channel_id=1, replica_groups=mesh['space'=16,'batch'=16] {'space'}, dimensions={0}, use_global_device_ids=true | all-gather | bytes 835584 | tf_op jit(solution)/shard_map/all_gather | solution.py:176
  92.3 0.6 gather_fusion.4
  94.1 0.5 copy-done.12
  96.7 1.2 fusion.22
  98.2 0.4 fusion.29
  98.6 0.9 convolution_bitcast_fusion.14
  99.5 0.9 convolution_bitcast_fusion.15
  100.3 0.9 convolution_bitcast_fusion.16
  101.2 0.9 convolution_bitcast_fusion.11
  102.1 0.9 convolution_bitcast_fusion.13
  103.0 0.9 convolution_bitcast_fusion.10
  103.8 0.9 convolution_bitcast_fusion.8
  104.7 0.9 convolution_bitcast_fusion.9
  105.8 1.1 pad_slice_fusion.8
  109.0 40.9 %all_gather.14 = bf16[48,4,16,128]{3,2,0,1:T(8,128)(2,1)S(1)} all-gather(bf16[3,4,16,128]{3,2,0,1:T(8,128)(2,1)S(1)} %pad_maximum_fusion.9), channel_id=1, replica_groups=mesh['space'=16,'batch'=16] {'space'}, dimensions={0}, use_global_device_ids=true | all-gather | bytes 835584 | tf_op jit(solution)/shard_map/all_gather | solution.py:187
  149.9 1.3 convert_element_type.95
  151.2 2.0 gather_fusion.5
  153.2 0.6 copy.370
  153.9 1.5 rev.21
  155.4 1.0 broadcast_select_fusion.1
  156.5 1.0 copy.355
  157.5 1.0 copy.356
  158.5 1.0 copy.357
  164.0 0.4 copy-done.18
  165.8 0.4 copy-done.20
  167.6 0.7 maximum_multiply_fusion.2
  168.8 0.9 maximum_multiply_fusion.1
  169.8 0.9 maximum_multiply_fusion
  170.8 1.0 pad_slice_fusion
  173.8 32.0 %all_gather.15 = bf16[48,4,16,128]{3,2,0,1:T(8,128)(2,1)S(1)} all-gather(bf16[3,4,16,128]{3,2,0,1:T(8,128)(2,1)S(1)} %pad_maximum_fusion.10), channel_id=1, replica_groups=mesh['space'=16,'batch'=16] {'space'}, dimensions={0}, use_global_device_ids=true | all-gather | bytes 835584 | tf_op jit(solution)/shard_map/all_gather | solution.py:187
  206.0 0.6 gather_fusion.6
  210.4 0.7 copy.424
  211.4 0.8 fusion
  212.2 223.5 %all-reduce.21.cloned.1.call-done = (f32[3,3,128,128]{3,2,1,0:T(8,128)}, f32[3,3,128,128]{3,2,1,0:T(8,128)}, f32[2,2,128,128]{3,2,1,0:T(8,128)}) async-done(((f32[3,3,128,128]{3,2,1,0:T(8,128)}, f32[3,3,128,128]{3,2,1,0:T(8,128)}, f32[2,2,128,128]{3,2,1,0:T(8,128)}), (f32[3,3,128,128]{3,2,1,0:T(8,128)}, f32[3,3,128,128]{3,2,1,0:T(8,128)}, f32[2,2,128,128]{3,2,1,0:T(8,128)})) %all-reduce.21.cloned.1.call-update) | async-done | bytes 1441808 | tf_op jit(solution)/shard_map/psum | solution.py:212
  435.7 2.0 copy.560
  437.7 0.8 copy.561
  438.5 0.7 copy.562
  (306 shorter events, 23.0 us)
Async XLA Ops:
  7.2 54.0 %copy-start = (bf16[1,3,8,8,128]{4,3,2,1,0:T(8,128)(2,1)S(1)}, bf16[1,3,8,8,128]{4,3,2,1,0:T(8,128)(2,1)}, u32[]{:S(2)}) copy-start(bf16[1,3,8,8,128]{4,3,2,1,0:T(8,128)(2,1)} %param.30) | copy-start | bytes 147460
  7.2 48.6 %copy-start.1 = (s32[48]{0:T(128)S(1)}, s32[48]{0:T(128)}, u32[]{:S(2)}) copy-start(s32[48]{0:T(128)} %param.33) | copy-start | bytes 580
  7.2 428.5 %all-reduce.21.cloned.1.call-start = ((), (), s32[]{:S(2)}) async-start(), calls=%async_computation | async-start | bytes 2883584 | tf_op jit(solution)/shard_map/psum | solution.py:212
  52.1 5.5 %copy-start.2 = (bf16[1,3,16,16,128]{4,3,2,1,0:T(8,128)(2,1)S(1)}, bf16[1,3,16,16,128]{4,3,2,1,0:T(8,128)(2,1)}, u32[]{:S(2)}) copy-start(bf16[1,3,16,16,128]{4,3,2,1,0:T(8,128)(2,1)} %param.25) | copy-start | bytes 589828
  57.8 1.7 copy-start.15
  57.8 2.1 copy-start.17
  57.9 1.1 copy-start.4
  60.3 0.9 copy-start.22
  60.8 34.8 %copy-start.13 = (bf16[768,128]{1,0:T(8,128)(2,1)}, bf16[768,128]{1,0:T(8,128)(2,1)S(1)}, u32[]{:S(2)}) copy-start(bf16[768,128]{1,0:T(8,128)(2,1)S(1)} %get-tuple-element.219) | copy-start | bytes 589828
  93.7 0.9 copy-start.12
  93.9 1.0 copy-start.3
  155.4 4.1 copy-start.11
  155.4 4.1 copy-start.10
  155.4 4.2 copy-start.8
  156.4 3.3 copy-start.32
  161.6 0.9 copy-start.33
  163.4 0.9 copy-start.18
  163.7 1.0 copy-start.16
  165.3 0.9 copy-start.20
  165.5 1.5 copy-start.19
  165.8 2.6 copy-start.14
  166.2 2.4 copy-start.24
  166.2 2.4 copy-start.26
  166.2 2.4 copy-start.28
  166.2 2.4 copy-start.30
  167.3 1.4 copy-start.35
  167.3 1.4 copy-start.36
  167.3 1.4 copy-start.37
  167.3 1.4 copy-start.38
  167.3 1.4 copy-start.40
  167.6 1.2 copy-start.39
  167.6 1.2 copy-start.41
  167.6 1.2 copy-start.42
  206.0 0.9 copy-start.9
  206.0 1.0 copy-start.7
  207.5 0.9 copy-start.6
  207.5 1.0 copy-start.5
  209.3 0.9 copy-start.23
  209.3 0.9 copy-start.27
  209.4 1.8 copy-start.31
  209.4 1.9 copy-start.29
  209.6 1.8 copy-start.25
  435.7 2.0 copy-start.21
  435.7 2.8 copy-start.34
Sparse Core Ops, SparseCore 0:
  170.8 264.8 all-reduce.20
where the time goes:
time: 448 us; the launch traced here: 446 us
  waiting for transfers between devices  224 us (50%)
  blocking collectives  146 us (33%)
  local copies, waits for them, and re-layouts  27.6 us (6%)
  matrix products  22.8 us (5%)
  between operations  15.9 us (4%)
  other arithmetic  9.75 us (2%)
    psum x1, waiting for transfers between devices, shards(): lax.psum((first_grad, second_grad, down_grad), ('space', 'batch'))  224 us
    all_gather x2, blocking collectives, seams_of(): lax.all_gather(edge_rows(field_values), 'space', axis=0, tiled=True)  73.6 us
    all_gather x2, blocking collectives, adjoint(): lax.all_gather(rim_terms.astype(jnp.bfloat16), 'space', axis=0, tiled=True)  72.9 us
    dot_general x18, matrix products, kernel_grad(): lax.dot_general(window, flattened, (((0,), (0,)), ((), ())), preferred_el...  9.58 us
  transfers between devices with their start and end apart: 1, of which 1 were waited for; matrix products, arithmetic and copies ran while one was open for 2% of the time, Pallas kernels for 0%

commit v1 on v0

--- a/solution.py
+++ b/solution.py
@@ -3,7 +3,12 @@
 import jax
 import jax.numpy as jnp
 from jax import lax
+from jax.sharding import Mesh
 from jax.sharding import PartitionSpec as P
+
+CHIPS = ("y", "z")
+PLANE = ("x", "y")
+DEPTH = ("z", "w")
 
 
 def edge_rows(value_entries):
@@ -144,6 +149,54 @@
     )
     running = running + jnp.dot(trailing, triple[2].T, preferred_element_type=jnp.float32)
     return running.reshape(number, extent, channels)
+
+
+def swap_core(block):
+    return lax.ppermute(block, "c", [(0, 1), (1, 0)])
+
+
+def spread(block, axes):
+    number = lax.axis_size(axes)
+    copies = jnp.broadcast_to(block[None], (number,) + block.shape)
+    return lax.all_to_all(copies, axes, 0, 0)
+
+
+def gather_space(block):
+    mine = spread(block, CHIPS)
+    both = jnp.stack([mine, swap_core(mine)])
+    return both.reshape((-1,) + block.shape[1:])
+
+
+def gathered_slot(slot, tiles_here):
+    chips = lax.axis_size(CHIPS)
+    owner = slot // tiles_here
+    other = (owner + lax.axis_index("c")) % 2
+    return (other * chips + owner // 2) * tiles_here + slot % tiles_here
+
+
+def total_sum(parts):
+    rows = jnp.concatenate([part.reshape(-1, part.shape[-1]) for part in parts])
+    half = rows.shape[0] // 2
+    core = lax.axis_index("c")
+    keep = lax.dynamic_slice_in_dim(rows, core * half, half)
+    give = lax.dynamic_slice_in_dim(rows, (1 - core) * half, half)
+    keep = keep + swap_core(give)
+    number = lax.axis_size(PLANE)
+    pieces = keep.astype(jnp.bfloat16).reshape(number, half // number, -1)
+    piece = jnp.sum(lax.all_to_all(pieces, PLANE, 0, 0).astype(jnp.float32), axis=0)
+    piece = jnp.sum(spread(piece, DEPTH), axis=0).astype(jnp.bfloat16)
+    mine = spread(piece, PLANE).reshape(half, -1)
+    other = swap_core(mine)
+    first = core == 0
+    rows = jnp.concatenate([jnp.where(first, mine, other), jnp.where(first, other, mine)])
+    rows = rows.astype(jnp.float32)
+    results = []
+    at = 0
+    for part in parts:
+        size = part.size // part.shape[-1]
+        results.append(rows[at : at + size].reshape(part.shape))
+        at += size
+    return results
 
 
 def shards(
@@ -161,19 +214,19 @@
     tiles_here = value_entries.shape[0]
     extent = value_entries.shape[1]
     total_tiles = tile_slots.shape[0]
-    first_slot = lax.axis_index("space") * tiles_here
+    first_slot = lax.axis_index(("y", "z", "c")) * tiles_here
     own_slots = first_slot + jnp.arange(tiles_here, dtype=jnp.int32)
     matches = tile_slots[None, :] == own_slots[:, None]
     own_tiles = jnp.sum(
         jnp.where(matches, jnp.arange(total_tiles, dtype=jnp.int32)[None, :], 0), axis=1
     )
     own_codes = seam_codes[own_tiles]
-    source_slot = tile_slots[face_neighbours[own_tiles]]
+    source_slot = gathered_slot(tile_slots[face_neighbours[own_tiles]], tiles_here)
     source_side = own_codes // 2
     reverse = own_codes % 2
 
     def seams_of(field_values):
-        gathered = lax.all_gather(edge_rows(field_values), "space", axis=0, tiled=True)
+        gathered = gather_space(edge_rows(field_values))
         return orient(gathered[source_slot, source_side], reverse)
 
     def adjoint(cotangent, weight_tensor):
@@ -184,14 +237,12 @@
         rim_terms = jnp.stack(
             [edge_conv(own_edges[:, facing], triples[facing]) for facing in range(4)], axis=1
         )
-        gathered = lax.all_gather(
-            rim_terms.astype(jnp.bfloat16), "space", axis=0, tiled=True
-        ).astype(rim_terms.dtype)
+        gathered = gather_space(rim_terms.astype(jnp.bfloat16)).astype(rim_terms.dtype)
         returned_rows = orient(gathered[source_slot, source_side], reverse)
         return add_sides(interior, returned_rows)
 
     grad_scale = 1.0 / math.sqrt(
-        lax.axis_size("batch") * lax.axis_size("space") * tiles_here * extent * extent
+        lax.axis_size(("w", "x")) * total_tiles * extent * extent
     )
     initial_padded_tile = attach(value_entries, seams_of(value_entries))
     first_pre = convolve(initial_padded_tile, conv1_weight)
@@ -209,33 +260,21 @@
     first_delta = gelu_back(first_pre, first_cot).astype(jnp.bfloat16)
     first_grad = kernel_grad(initial_padded_tile, first_delta) * grad_scale
     input_grad = adjoint(first_delta, conv1_weight).astype(jnp.bfloat16)
-    first_grad, second_grad, down_grad = lax.psum(
-        (first_grad, second_grad, down_grad), ("space", "batch")
-    )
+    first_grad, second_grad, down_grad = total_sum([first_grad, second_grad, down_grad])
     return (coarse_field[None], input_grad[None], first_grad, second_grad, down_grad)
 
 
 def solution(mesh):
+    batch = mesh.shape["batch"]
+    along_x = 4 if batch % 4 == 0 else 1
+    fine = Mesh(
+        mesh.devices.reshape(4, 2, 2, batch // along_x, along_x), ("y", "z", "c", "w", "x")
+    )
+    field = P(("w", "x"), ("y", "z", "c"), None, None, None)
     return jax.shard_map(
         shards,
-        mesh=mesh,
-        in_specs=(
-            P("batch", "space", None, None, None),
-            P(),
-            P(),
-            P(),
-            P("batch", "space", None, None, None),
-            P("batch", "space", None, None, None),
-            P(),
-            P(),
-            P(),
-        ),
-        out_specs=(
-            P("batch", "space", None, None, None),
-            P("batch", "space", None, None, None),
-            P(),
-            P(),
-            P(),
-        ),
+        mesh=fine,
+        in_specs=(field, P(), P(), P(), field, field, P(), P(), P()),
+        out_specs=(field, field, P(), P(), P()),
         check_vma=False,
     )

time: 448 us -> 192 us (0.43)
  waiting for transfers between devices: 224 us -> 56.3 us
  blocking collectives: 146 us -> 0 us
  starting transfers between devices: 0.04 us -> 54.4 us
  between operations: 15.9 us -> 2.52 us
  other arithmetic: 9.75 us -> 16.8 us
  matrix products: 22.8 us -> 29.4 us
    psum x1 -> x0, waiting for transfers between devices: 224 us -> none  [shards(): lax.psum((first_grad, second_grad, down_grad), ('space', 'batch'))]
    all_gather x4 -> x0, blocking collectives: 146 us -> none  [the longest x2 73.6 us: seams_of(): lax.all_gather(edge_rows(field_values), 'space', axis=0, tiled=True)]
    all_to_all x0 -> x7, waiting for transfers between devices: none -> 54.6 us  [the longest x6 46.5 us: spread(): return lax.all_to_all(copies, axes, 0, 0)]
    all_to_all x0 -> x7, starting transfers between devices: none -> 42.5 us  [the longest x6 35.4 us: spread(): return lax.all_to_all(copies, axes, 0, 0)]
    ppermute x0 -> x6, starting transfers between devices: none -> 11.9 us  [swap_core(): return lax.ppermute(block, 'c', [(0, 1), (1, 0)])]
    unnamed x96 -> x103, local copies, waits for them, and re-layouts: 8.72 us -> 2.54 us
    broadcast_in_dim x0 -> x6, local copies, waits for them, and re-layouts: none -> 4.87 us  [spread(): copies = jnp.broadcast_to(block[None], (number,) + block.shape)]
  transfers between devices with their start and end apart: 1 -> 13, of which waited for: 1 -> 9; matrix products, arithmetic and copies ran while one was open for 2% -> 16% of each run, Pallas kernels for 0% -> 0%
where the time goes in v1:
time: 192 us; the launch traced here: 191 us
  waiting for transfers between devices  56.3 us (29%)
  starting transfers between devices  54.4 us (28%)
  local copies, waits for them, and re-layouts  31.5 us (16%)
  matrix products  29.4 us (15%)
  other arithmetic  16.8 us (9%)
  between operations  2.52 us (1%)
    all_to_all x6, waiting for transfers between devices, spread(): return lax.all_to_all(copies, axes, 0, 0)  46.5 us
    all_to_all x6, starting transfers between devices, spread(): return lax.all_to_all(copies, axes, 0, 0)  35.4 us
    ppermute x6, starting transfers between devices, swap_core(): return lax.ppermute(block, 'c', [(0, 1), (1, 0)])  11.9 us
    dot_general x18, matrix products, kernel_grad(): lax.dot_general(window, flattened, (((0,), (0,)), ((), ())), preferred_el...  10.2 us
    slice x29, local copies, waits for them, and re-layouts, convolve(): window = padded[:, a:a + extent, b:b + extent].reshape(-1, padded.shape[-1])  9.35 us
    all_to_all x1, waiting for transfers between devices, total_sum(): lax.all_to_all(pieces, PLANE, 0, 0).astype(jnp.float32)  8.18 us
    dot_general x36, matrix products, convolve(): jnp.dot(window, weight_tensor[a, b], preferred_element_type=jnp.float32)  7.95 us
    all_to_all x1, starting transfers between devices, total_sum(): lax.all_to_all(pieces, PLANE, 0, 0).astype(jnp.float32)  7.05 us
  transfers between devices with their start and end apart: 13, of which 9 were waited for; matrix products, arithmetic and copies ran while one was open for 16% of the time, Pallas kernels for 0%

profile of v1, /device:TPU:1, one launch (start us, length us, event | category | flops | bytes accessed | tf_op | source)
XLA Modules:
  0.0 190.9 jit_solution(14223293651996827919)
XLA Ops:
  1.4 1.0 fusion.232
  3.3 11.8 %all-to-all-start = ((bf16[8,3,4,16,128]{4,3,2,1,0:T(8,128)(2,1)}), bf16[8,3,4,16,128]{4,3,2,1,0:T(8,128)(2,1)S(1)}, u32[]{:S(2)}, u32[]{:S(2)}) async-start(bf16[8,3,4,16,128]{4,3,2,1,0:T(8,128)(2,1)} %broadcast_in_dim.57), calls=%async_computation | async-start | bytes 786432 | tf_op jit(solution)/shard_map/all_to_all | solution.py:161
  17.6 9.3 %all-to-all-done = bf16[8,3,4,16,128]{4,3,2,1,0:T(8,128)(2,1)S(1)} async-done(((bf16[8,3,4,16,128]{4,3,2,1,0:T(8,128)(2,1)}), bf16[8,3,4,16,128]{4,3,2,1,0:T(8,128)(2,1)S(1)}, u32[]{:S(2)}, u32[]{:S(2)}) %all-to-all-start) | async-done | bytes 393248 | tf_op jit(solution)/shard_map/all_to_all | solution.py:161
  26.9 2.9 %collective-permute-start = (bf16[8,3,4,16,128]{4,3,2,1,0:T(8,128)(2,1)S(1)}, bf16[8,3,4,16,128]{4,3,2,1,0:T(8,128)(2,1)S(1)}, u32[]{:S(2)}, u32[]{:S(2)}) collective-permute-start(bf16[8,3,4,16,128]{4,3,2,1,0:T(8,128)(2,1)S(1)} %all-to-all-done), channel_id=1, source_target_pairs={{0,16},{16,0},{1,17},{17,1},{2,18},{18,2},{3,19},{19,3},{4,20},{20... | collective-permute-start | bytes 1179656 | tf_op jit(solution)/shard_map/ppermute | solution.py:155
  30.1 1.1 collective-permute-done
  35.0 1.0 fusion.44
  37.2 3.5 %all-to-all-start.1 = ((bf16[8,3,4,16,128]{4,3,2,1,0:T(8,128)(2,1)}), bf16[8,3,4,16,128]{4,3,2,1,0:T(8,128)(2,1)S(1)}, u32[]{:S(2)}, u32[]{:S(2)}) async-start(bf16[8,3,4,16,128]{4,3,2,1,0:T(8,128)(2,1)} %broadcast_in_dim.60), calls=%async_computation.1 | async-start | bytes 786432 | tf_op jit(solution)/shard_map/all_to_all | solution.py:161
  42.5 10.3 %all-to-all-done.1 = bf16[8,3,4,16,128]{4,3,2,1,0:T(8,128)(2,1)S(1)} async-done(((bf16[8,3,4,16,128]{4,3,2,1,0:T(8,128)(2,1)}), bf16[8,3,4,16,128]{4,3,2,1,0:T(8,128)(2,1)S(1)}, u32[]{:S(2)}, u32[]{:S(2)}) %all-to-all-start.1) | async-done | bytes 393248 | tf_op jit(solution)/shard_map/all_to_all | solution.py:161
  52.8 1.4 collective-permute-start.1
  56.6 1.7 maximum_bitcast_fusion
  58.3 2.0 %pad_maximum_fusion.2 = bf16[2,8,3,4,16,128]{5,4,3,2,1,0:T(8,128)(2,1)} fusion(bf16[1,8,3,4,16,128]{5,4,3,2,1,0:T(8,128)(2,1)} %bitcast.40, bf16[1,8,3,4,16,128]{5,4,3,2,1,0:T(8,128)(2,1)S(1)} %bitcast.682), kind=kLoop, calls=%fused_computation.95 | loop fusion | flops 393216 | bytes 1572864 | tf_op jit(solution)/shard_map/stack | solution.py:166
  60.2 1.8 gather_fusion.4
  65.7 1.1 fusion.22
  67.5 0.9 convolution_bitcast_fusion.13
  68.4 0.9 convolution_bitcast_fusion.11
  70.2 0.9 convolution_bitcast_fusion.9
  71.0 0.9 convolution_bitcast_fusion.16
  71.9 0.9 convolution_bitcast_fusion.15
  72.8 0.9 convolution_bitcast_fusion.14
  74.7 1.2 pad_slice_fusion.8
  82.5 4.5 %all-to-all-start.2 = ((bf16[8,3,4,16,128]{4,3,2,1,0:T(8,128)(2,1)}), bf16[8,3,4,16,128]{4,3,2,1,0:T(8,128)(2,1)S(1)}, u32[]{:S(2)}, u32[]{:S(2)}) async-start(bf16[8,3,4,16,128]{4,3,2,1,0:T(8,128)(2,1)} %broadcast_in_dim.63), calls=%async_computation.2 | async-start | bytes 786432 | tf_op jit(solution)/shard_map/all_to_all | solution.py:161
  87.1 1.0 copy.248
  88.1 1.0 copy.249
  89.1 1.0 copy.250
  90.1 1.0 copy.253
  91.1 1.0 copy.254
  97.5 1.8 all-to-all-done.2
  99.3 1.5 collective-permute-start.2
  100.9 1.1 maximum_multiply_fusion.1
  102.0 1.5 fusion
  103.6 1.4 bitcast_convert_fusion.1
  105.0 2.0 %gather_fusion.5 = f32[12,16,128]{2,1,0:T(8,128)S(1)} fusion(f32[48,4,16,128]{3,2,1,0:T(8,128)} %bitcast_convert_fusion.1, s32[12]{0:T(128)S(1)} %reshape.1055), kind=kCustom, calls=%fused_computation.5 | custom fusion | bytes 196704 | tf_op jit(solution)/shard_map/gather | solution.py:241
  109.0 0.9 convolution_bitcast_fusion.17
  110.8 1.1 pad_slice_fusion
  115.0 6.6 %all-to-all-start.3 = ((bf16[8,3,4,16,128]{4,3,2,1,0:T(8,128)(2,1)}), bf16[8,3,4,16,128]{4,3,2,1,0:T(8,128)(2,1)S(1)}, u32[]{:S(2)}, u32[]{:S(2)}) async-start(bf16[8,3,4,16,128]{4,3,2,1,0:T(8,128)(2,1)} %broadcast_in_dim.64), calls=%async_computation.3 | async-start | bytes 786432 | tf_op jit(solution)/shard_map/all_to_all | solution.py:161
  121.9 0.9 constant_dynamic-slice_fusion
  125.8 7.9 %all-to-all-done.3 = bf16[8,3,4,16,128]{4,3,2,1,0:T(8,128)(2,1)S(1)} async-done(((bf16[8,3,4,16,128]{4,3,2,1,0:T(8,128)(2,1)}), bf16[8,3,4,16,128]{4,3,2,1,0:T(8,128)(2,1)S(1)}, u32[]{:S(2)}, u32[]{:S(2)}) %all-to-all-start.3) | async-done | bytes 393248 | tf_op jit(solution)/shard_map/all_to_all | solution.py:161
  133.7 1.5 collective-permute-start.3
  135.2 1.9 %add_convert_fusion = bf16[1408,128]{1,0:T(8,128)(2,1)} fusion(f32[1408,128]{1,0:T(8,128)} %collective-permute-done.4, f32[2816,128]{1,0:T(8,128)S(1)} %pad_maximum_fusion, s32[]{:T(128)S(6)} %select_n.164), kind=kLoop, calls=%fused_computation.102 | loop fusion | flops 360448 | bytes 1802244 | tf_op jit(solution)/shard_map/convert_element_type | solution.py:185
  137.1 7.1 %all-to-all-start.4 = ((bf16[16,88,128]{2,1,0:T(8,128)(2,1)}), bf16[16,88,128]{2,1,0:T(8,128)(2,1)S(1)}, u32[]{:S(2)}, u32[]{:S(2)}) async-start(bf16[16,88,128]{2,1,0:T(8,128)(2,1)} %bitcast.260), calls=%async_computation.4 | async-start | bytes 720896 | tf_op jit(solution)/shard_map/all_to_all | solution.py:186
  144.8 8.2 %all-to-all-done.4 = bf16[16,88,128]{2,1,0:T(8,128)(2,1)S(1)} async-done(((bf16[16,88,128]{2,1,0:T(8,128)(2,1)}), bf16[16,88,128]{2,1,0:T(8,128)(2,1)S(1)}, u32[]{:S(2)}, u32[]{:S(2)}) %all-to-all-start.4) | async-done | bytes 360480 | tf_op jit(solution)/shard_map/all_to_all | solution.py:186
  153.8 4.9 %all-to-all-start.5 = ((f32[8,88,128]{2,1,0:T(8,128)}), f32[8,88,128]{2,1,0:T(8,128)S(1)}, u32[]{:S(2)}, u32[]{:S(2)}) async-start(f32[8,88,128]{2,1,0:T(8,128)} %broadcast_in_dim.66), calls=%async_computation.5 | async-start | bytes 720896 | tf_op jit(solution)/shard_map/all_to_all | solution.py:161
  158.7 1.1 pad_maximum_fusion.4
  160.9 9.5 %all-to-all-done.5 = f32[8,88,128]{2,1,0:T(8,128)S(1)} async-done(((f32[8,88,128]{2,1,0:T(8,128)}), f32[8,88,128]{2,1,0:T(8,128)S(1)}, u32[]{:S(2)}, u32[]{:S(2)}) %all-to-all-start.5) | async-done | bytes 360480 | tf_op jit(solution)/shard_map/all_to_all | solution.py:161
  171.2 4.2 %all-to-all-start.6 = ((bf16[16,88,128]{2,1,0:T(8,128)(2,1)}), bf16[16,88,128]{2,1,0:T(8,128)(2,1)S(1)}, u32[]{:S(2)}, u32[]{:S(2)}) async-start(bf16[16,88,128]{2,1,0:T(8,128)(2,1)} %broadcast_in_dim.67), calls=%async_computation.6 | async-start | bytes 720896 | tf_op jit(solution)/shard_map/all_to_all | solution.py:161
  175.6 7.7 %all-to-all-done.6 = bf16[16,88,128]{2,1,0:T(8,128)(2,1)S(1)} async-done(((bf16[16,88,128]{2,1,0:T(8,128)(2,1)}), bf16[16,88,128]{2,1,0:T(8,128)(2,1)S(1)}, u32[]{:S(2)}, u32[]{:S(2)}) %all-to-all-start.6) | async-done | bytes 360480 | tf_op jit(solution)/shard_map/all_to_all | solution.py:161
  183.3 4.3 %collective-permute-start.5 = (bf16[1408,128]{1,0:T(8,128)(2,1)S(1)}, bf16[1408,128]{1,0:T(8,128)(2,1)S(1)}, u32[]{:S(2)}, u32[]{:S(2)}) collective-permute-start(bf16[1408,128]{1,0:T(8,128)(2,1)S(1)} %bitcast.685), channel_id=1, source_target_pairs={{0,16},{16,0},{1,17},{17,1},{2,18},{18,2},{3,19},{19,3},{4,20},{20... | collective-permute-start | bytes 1081352 | tf_op jit(solution)/shard_map/ppermute | solution.py:155
  189.8 1.1 fusion.220
  (358 shorter events, 45.7 us)
Async XLA Ops:
  0.6 40.0 %copy-start = (bf16[1,3,8,8,128]{4,3,2,1,0:T(8,128)(2,1)S(1)}, bf16[1,3,8,8,128]{4,3,2,1,0:T(8,128)(2,1)}, u32[]{:S(2)}) copy-start(bf16[1,3,8,8,128]{4,3,2,1,0:T(8,128)(2,1)} %param.30) | copy-start | bytes 147460
  0.6 14.4 %copy-start.1 = (s32[48]{0:T(128)S(1)}, s32[48]{0:T(128)}, u32[]{:S(2)}) copy-start(s32[48]{0:T(128)} %param.33) | copy-start | bytes 580
  0.7 14.6 %copy-start.46 = (s32[48,4]{0,1:T(4,128)S(1)}, s32[48,4]{0,1:T(4,128)}, u32[]{:S(2)}) copy-start(s32[48,4]{0,1:T(4,128)} %param.31) | copy-start | bytes 2308
  3.3 13.7 %copy-start.47 = (s32[48,4]{0,1:T(4,128)S(1)}, s32[48,4]{0,1:T(4,128)}, u32[]{:S(2)}) copy-start(s32[48,4]{0,1:T(4,128)} %param.32) | copy-start | bytes 2308
  3.3 23.6 %all-to-all-start = ((bf16[8,3,4,16,128]{4,3,2,1,0:T(8,128)(2,1)}), bf16[8,3,4,16,128]{4,3,2,1,0:T(8,128)(2,1)S(1)}, u32[]{:S(2)}, u32[]{:S(2)}) async-start(bf16[8,3,4,16,128]{4,3,2,1,0:T(8,128)(2,1)} %broadcast_in_dim.57), calls=%async_computation | async-start | bytes 786432 | tf_op jit(solution)/shard_map/all_to_all | solution.py:161
  16.7 15.4 %copy-start.2 = (bf16[1,3,16,16,128]{4,3,2,1,0:T(8,128)(2,1)S(1)}, bf16[1,3,16,16,128]{4,3,2,1,0:T(8,128)(2,1)}, u32[]{:S(2)}) copy-start(bf16[1,3,16,16,128]{4,3,2,1,0:T(8,128)(2,1)} %param.25) | copy-start | bytes 589828
  26.9 4.2 %collective-permute-start = (bf16[8,3,4,16,128]{4,3,2,1,0:T(8,128)(2,1)S(1)}, bf16[8,3,4,16,128]{4,3,2,1,0:T(8,128)(2,1)S(1)}, u32[]{:S(2)}, u32[]{:S(2)}) collective-permute-start(bf16[8,3,4,16,128]{4,3,2,1,0:T(8,128)(2,1)S(1)} %all-to-all-done), channel_id=1, source_target_pairs={{0,16},{16,0},{1,17},{17,1},{2,18},{18,2},{3,19},{19,3},{4,20},{20... | collective-permute-start | bytes 1179656 | tf_op jit(solution)/shard_map/ppermute | solution.py:155
  32.3 1.7 copy-start.24
  32.3 2.1 %copy-start.22 = (bf16[3,16,16,128]{3,2,1,0:T(8,128)(2,1)}, bf16[3,16,16,128]{3,2,1,0:T(8,128)(2,1)S(1)}, u32[]{:S(2)}) copy-start(bf16[3,16,16,128]{3,2,1,0:T(8,128)(2,1)S(1)} %get-tuple-element.177) | copy-start | bytes 589828
  35.0 5.6 %copy-start.29 = (bf16[2,2,128,128]{3,2,1,0:T(8,128)(2,1)S(1)}, bf16[2,2,128,128]{3,2,1,0:T(8,128)(2,1)}, u32[]{:S(2)}) copy-start(bf16[2,2,128,128]{3,2,1,0:T(8,128)(2,1)} %param.28) | copy-start | bytes 393220
  36.0 6.4 %copy-start.17 = (bf16[1,3,16,16,128]{4,3,2,1,0:T(8,128)(2,1)S(1)}, bf16[1,3,16,16,128]{4,3,2,1,0:T(8,128)(2,1)}, u32[]{:S(2)}) copy-start(bf16[1,3,16,16,128]{4,3,2,1,0:T(8,128)(2,1)} %param.29) | copy-start | bytes 589828
  37.2 15.6 %all-to-all-start.1 = ((bf16[8,3,4,16,128]{4,3,2,1,0:T(8,128)(2,1)}), bf16[8,3,4,16,128]{4,3,2,1,0:T(8,128)(2,1)S(1)}, u32[]{:S(2)}, u32[]{:S(2)}) async-start(bf16[8,3,4,16,128]{4,3,2,1,0:T(8,128)(2,1)} %broadcast_in_dim.60), calls=%async_computation.1 | async-start | bytes 786432 | tf_op jit(solution)/shard_map/all_to_all | solution.py:161
  40.6 15.2 %copy-start.3 = (bf16[3,3,128,128]{3,2,1,0:T(8,128)(2,1)S(1)}, bf16[3,3,128,128]{3,2,1,0:T(8,128)(2,1)}, u32[]{:S(2)}) copy-start(bf16[3,3,128,128]{3,2,1,0:T(8,128)(2,1)} %param.27) | copy-start | bytes 884740
  42.5 14.1 %copy-start.32 = (f32[3,8,8,1,128]{4,2,1,0,3:T(8,128)S(1)}, f32[3,8,8,1,128]{4,2,1,0,3:T(8,128)}, u32[]{:S(2)}) copy-start(f32[3,8,8,1,128]{4,2,1,0,3:T(8,128)} %convolution_bitcast_fusion.1) | copy-start | bytes 294916
  42.5 14.1 %copy-start.33 = (f32[3,8,8,1,128]{4,2,1,0,3:T(8,128)S(1)}, f32[3,8,8,1,128]{4,2,1,0,3:T(8,128)}, u32[]{:S(2)}) copy-start(f32[3,8,8,1,128]{4,2,1,0,3:T(8,128)} %convolution_bitcast_fusion) | copy-start | bytes 294916
  52.8 5.5 %collective-permute-start.1 = (bf16[8,3,4,16,128]{4,3,2,1,0:T(8,128)(2,1)S(1)}, bf16[8,3,4,16,128]{4,3,2,1,0:T(8,128)(2,1)}, u32[]{:S(2)}, u32[]{:S(2)}) collective-permute-start(bf16[8,3,4,16,128]{4,3,2,1,0:T(8,128)(2,1)S(1)} %all-to-all-done.1), channel_id=1, source_target_pairs={{0,16},{16,0},{1,17},{17,1},{2,18},{18,2},{3,19},{19,3},{4,20},{20... | collective-permute-start | bytes 1179656 | tf_op jit(solution)/shard_map/ppermute | solution.py:155
  65.3 1.8 copy-start.18
  74.5 1.4 copy-start.30
  82.5 9.5 %copy-start.16 = (bf16[3,16,16,128]{3,1,0,2:T(8,128)(2,1)S(1)}, bf16[3,16,16,128]{3,1,0,2:T(8,128)(2,1)}, u32[]{:S(2)}) copy-start(bf16[3,16,16,128]{3,1,0,2:T(8,128)(2,1)} %get-tuple-element.166) | copy-start | bytes 589828
  82.5 9.6 %copy-start.35 = (f32[1,128,128]{2,1,0:T(8,128)S(1)}, f32[1,128,128]{2,1,0:T(8,128)}, u32[]{:S(2)}) copy-start(f32[1,128,128]{2,1,0:T(8,128)} %convolution_bitcast_fusion.5) | copy-start | bytes 196612
  82.5 16.7 %all-to-all-start.2 = ((bf16[8,3,4,16,128]{4,3,2,1,0:T(8,128)(2,1)}), bf16[8,3,4,16,128]{4,3,2,1,0:T(8,128)(2,1)S(1)}, u32[]{:S(2)}, u32[]{:S(2)}) async-start(bf16[8,3,4,16,128]{4,3,2,1,0:T(8,128)(2,1)} %broadcast_in_dim.63), calls=%async_computation.2 | async-start | bytes 786432 | tf_op jit(solution)/shard_map/all_to_all | solution.py:161
  87.1 5.1 %copy-start.36 = (f32[1,128,128]{2,1,0:T(8,128)S(1)}, f32[1,128,128]{2,1,0:T(8,128)}, u32[]{:S(2)}) copy-start(f32[1,128,128]{2,1,0:T(8,128)} %convolution_bitcast_fusion.4) | copy-start | bytes 196612
  87.1 5.1 %copy-start.34 = (f32[1,128,128]{2,1,0:T(8,128)S(1)}, f32[1,128,128]{2,1,0:T(8,128)}, u32[]{:S(2)}) copy-start(f32[1,128,128]{2,1,0:T(8,128)} %convolution_bitcast_fusion.6) | copy-start | bytes 196612
  94.3 2.0 %copy-start.26 = (bf16[3,8,2,8,2,128]{5,3,1,0,4,2:T(8,128)(2,1)S(1)}, bf16[3,8,2,8,2,128]{5,3,1,0,4,2:T(8,128)(2,1)}, u32[]{:S(2)}) copy-start(bf16[3,8,2,8,2,128]{5,3,1,0,4,2:T(8,128)(2,1)} %get-tuple-element.120) | copy-start | bytes 589828
  94.4 2.2 %copy-start.9 = (bf16[3,16,16,128]{3,1,0,2:T(8,128)(2,1)S(1)}, bf16[3,16,16,128]{3,1,0,2:T(8,128)(2,1)}, u32[]{:S(2)}) copy-start(bf16[3,16,16,128]{3,1,0,2:T(8,128)(2,1)} %get-tuple-element.159) | copy-start | bytes 589828
  94.6 2.1 %copy-start.8 = (bf16[3,16,16,128]{3,1,0,2:T(8,128)(2,1)S(1)}, bf16[3,16,16,128]{3,1,0,2:T(8,128)(2,1)}, u32[]{:S(2)}) copy-start(bf16[3,16,16,128]{3,1,0,2:T(8,128)(2,1)} %get-tuple-element.165) | copy-start | bytes 589828
  94.6 2.2 %copy-start.20 = (bf16[768,128]{1,0:T(8,128)(2,1)S(1)}, bf16[768,128]{1,0:T(8,128)(2,1)}, u32[]{:S(2)}) copy-start(bf16[768,128]{1,0:T(8,128)(2,1)} %get-tuple-element.217) | copy-start | bytes 589828
  96.7 4.0 %copy-start.37 = (f32[1,128,128]{2,1,0:T(8,128)S(1)}, f32[1,128,128]{2,1,0:T(8,128)}, u32[]{:S(2)}) copy-start(f32[1,128,128]{2,1,0:T(8,128)} %convolution_bitcast_fusion.13) | copy-start | bytes 196612
  96.8 4.0 %copy-start.38 = (f32[1,128,128]{2,1,0:T(8,128)S(1)}, f32[1,128,128]{2,1,0:T(8,128)}, u32[]{:S(2)}) copy-start(f32[1,128,128]{2,1,0:T(8,128)} %convolution_bitcast_fusion.11) | copy-start | bytes 196612
  97.2 4.7 %copy-start.31 = (f32[192,128]{1,0:T(8,128)S(1)}, f32[192,128]{1,0:T(8,128)}, u32[]{:S(2)}) copy-start(f32[192,128]{1,0:T(8,128)} %convolution_add_fusion.33) | copy-start | bytes 294916
  99.3 4.2 %collective-permute-start.2 = (bf16[8,3,4,16,128]{4,3,2,1,0:T(8,128)(2,1)S(1)}, bf16[8,3,4,16,128]{4,3,2,1,0:T(8,128)(2,1)S(1)}, u32[]{:S(2)}, u32[]{:S(2)}) collective-permute-start(bf16[8,3,4,16,128]{4,3,2,1,0:T(8,128)(2,1)S(1)} %all-to-all-done.2), channel_id=1, source_target_pairs={{0,16},{16,0},{1,17},{17,1},{2,18},{18,2},{3,19},{19,3},{4,20},{20... | collective-permute-start | bytes 1179656 | tf_op jit(solution)/shard_map/ppermute | solution.py:155
  105.0 2.9 %copy-start.25 = (bf16[3,16,16,128]{3,2,1,0:T(8,128)(2,1)S(1)}, bf16[3,16,16,128]{3,2,1,0:T(8,128)(2,1)}, u32[]{:S(2)}) copy-start(bf16[3,16,16,128]{3,2,1,0:T(8,128)(2,1)} %copy-done.24) | copy-start | bytes 589828
  112.2 9.3 %copy-start.45 = (f32[1,128,128]{2,1,0:T(8,128)S(1)}, f32[1,128,128]{2,1,0:T(8,128)}, u32[]{:S(2)}) copy-start(f32[1,128,128]{2,1,0:T(8,128)} %convolution_bitcast_fusion.17) | copy-start | bytes 196612
  115.0 6.7 %copy-start.7 = (f32[2,2,128,128]{3,2,1,0:T(8,128)S(1)}, f32[2,2,128,128]{3,2,1,0:T(8,128)}, u32[]{:S(2)}) copy-start(f32[2,2,128,128]{3,2,1,0:T(8,128)} %maximum_multiply_fusion.2) | copy-start | bytes 786436
  115.0 18.7 %all-to-all-start.3 = ((bf16[8,3,4,16,128]{4,3,2,1,0:T(8,128)(2,1)}), bf16[8,3,4,16,128]{4,3,2,1,0:T(8,128)(2,1)S(1)}, u32[]{:S(2)}, u32[]{:S(2)}) async-start(bf16[8,3,4,16,128]{4,3,2,1,0:T(8,128)(2,1)} %broadcast_in_dim.64), calls=%async_computation.3 | async-start | bytes 786432 | tf_op jit(solution)/shard_map/all_to_all | solution.py:161
  121.8 1.4 copy-start.14
  121.8 1.4 copy-start.13
  121.9 1.5 copy-start.12
  121.9 1.6 copy-start.11
  121.9 1.6 copy-start.10
  122.8 1.5 copy-start.5
  122.8 12.4 %collective-permute-start.4 = (f32[1408,128]{1,0:T(8,128)}, f32[1408,128]{1,0:T(8,128)}, u32[]{:S(2)}, u32[]{:S(2)}) collective-permute-start(f32[1408,128]{1,0:T(8,128)} %constant_dynamic-slice_fusion), channel_id=1, source_target_pairs={{0,16},{16,0},{1,17},{17,1},{2,18},{18,2},{3,19},{19,3},{4,20},{20... | collective-permute-start | bytes 2162696 | tf_op jit(solution)/shard_map/ppermute | solution.py:155
  125.8 18.4 %copy-start.21 = (bf16[3,16,16,128]{3,2,1,0:T(8,128)(2,1)S(1)}, bf16[3,16,16,128]{3,2,1,0:T(8,128)(2,1)}, u32[]{:S(2)}) copy-start(bf16[3,16,16,128]{3,2,1,0:T(8,128)(2,1)} %copy.276) | copy-start | bytes 589828
  133.7 25.0 %collective-permute-start.3 = (bf16[8,3,4,16,128]{4,3,2,1,0:T(8,128)(2,1)S(1)}, bf16[8,3,4,16,128]{4,3,2,1,0:T(8,128)(2,1)}, u32[]{:S(2)}, u32[]{:S(2)}) collective-permute-start(bf16[8,3,4,16,128]{4,3,2,1,0:T(8,128)(2,1)S(1)} %all-to-all-done.3), channel_id=1, source_target_pairs={{0,16},{16,0},{1,17},{17,1},{2,18},{18,2},{3,19},{19,3},{4,20},{20... | collective-permute-start | bytes 1179656 | tf_op jit(solution)/shard_map/ppermute | solution.py:155
  137.1 15.9 %all-to-all-start.4 = ((bf16[16,88,128]{2,1,0:T(8,128)(2,1)}), bf16[16,88,128]{2,1,0:T(8,128)(2,1)S(1)}, u32[]{:S(2)}, u32[]{:S(2)}) async-start(bf16[16,88,128]{2,1,0:T(8,128)(2,1)} %bitcast.260), calls=%async_computation.4 | async-start | bytes 720896 | tf_op jit(solution)/shard_map/all_to_all | solution.py:186
  153.8 16.6 %all-to-all-start.5 = ((f32[8,88,128]{2,1,0:T(8,128)}), f32[8,88,128]{2,1,0:T(8,128)S(1)}, u32[]{:S(2)}, u32[]{:S(2)}) async-start(f32[8,88,128]{2,1,0:T(8,128)} %broadcast_in_dim.66), calls=%async_computation.5 | async-start | bytes 720896 | tf_op jit(solution)/shard_map/all_to_all | solution.py:161
  171.2 12.1 %all-to-all-start.6 = ((bf16[16,88,128]{2,1,0:T(8,128)(2,1)}), bf16[16,88,128]{2,1,0:T(8,128)(2,1)S(1)}, u32[]{:S(2)}, u32[]{:S(2)}) async-start(bf16[16,88,128]{2,1,0:T(8,128)(2,1)} %broadcast_in_dim.67), calls=%async_computation.6 | async-start | bytes 720896 | tf_op jit(solution)/shard_map/all_to_all | solution.py:161
  183.3 5.6 %collective-permute-start.5 = (bf16[1408,128]{1,0:T(8,128)(2,1)S(1)}, bf16[1408,128]{1,0:T(8,128)(2,1)S(1)}, u32[]{:S(2)}, u32[]{:S(2)}) collective-permute-start(bf16[1408,128]{1,0:T(8,128)(2,1)S(1)} %bitcast.685), channel_id=1, source_target_pairs={{0,16},{16,0},{1,17},{17,1},{2,18},{18,2},{3,19},{19,3},{4,20},{20... | collective-permute-start | bytes 1081352 | tf_op jit(solution)/shard_map/ppermute | solution.py:155
  (13 other events, 14.0 us)

commit v2 on v0

v2 whole, which is shorter than its diff:
```python
import functools
import math

import jax
import jax.numpy as jnp
from jax import lax
from jax.experimental import pallas as pl
from jax.experimental.pallas import tpu as pltpu
from jax.sharding import Mesh
from jax.sharding import PartitionSpec as P

CHIPS = ("y", "z")
PLANE = ("x", "y")
DEPTH = ("z", "w")
SLOPE = math.sqrt(2.0 / math.pi)
CUBIC = 0.044715
BF16 = jnp.bfloat16
F32 = jnp.float32
EDGE = 16
CH = 128


def swap_core(block):
    return lax.ppermute(block, "c", [(0, 1), (1, 0)])


def spread(block, axes):
    number = lax.axis_size(axes)
    copies = jnp.broadcast_to(block[None], (number,) + block.shape)
    return lax.all_to_all(copies, axes, 0, 0)


def swap_apart(block, axis, apart):
    number = lax.axis_size(axis)
    return lax.ppermute(block, axis, [(i, i ^ apart) for i in range(number)])


def rings(field_values):
    return jnp.stack(
        [
            field_values[:, :2],
            jnp.swapaxes(field_values[:, :, :-3:-1], 1, 2),
            field_values[:, :-3:-1],
            jnp.swapaxes(field_values[:, :, :2], 1, 2),
        ],
        axis=1,
    )


def side_frames(weight_tensor):
    turned = jnp.swapaxes(weight_tensor, 0, 1)
    return jnp.stack([weight_tensor, turned[::-1], weight_tensor[::-1], turned])


def flipped(weight_tensor):
    return jnp.transpose(weight_tensor[::-1, ::-1], (0, 1, 3, 2))


def frame_adjoint(frames):
    return jnp.transpose(frames, (1, 2, 4, 0, 3)).reshape(-1, 4 * CH)


def gelu(v):
    return 0.5 * v * (1.0 + jnp.tanh(SLOPE * (v + CUBIC * v * v * v)))


def gelu_slope(v):
    t = jnp.tanh(SLOPE * (v + CUBIC * v * v * v))
    return 0.5 * (1.0 + t) + (0.5 * SLOPE) * v * (1.0 - t * t) * (1.0 + (3.0 * CUBIC) * v * v)


def dot(left, right):
    return jnp.dot(left, right, preferred_element_type=F32)


def dot_rows(left, right):
    return lax.dot_general(left, right, (((0,), (0,)), ((), ())), preferred_element_type=F32)


def turned(turn, rows):
    high = rows.astype(BF16)
    low = (rows - high.astype(F32)).astype(BF16)
    return dot(turn, high) + dot(turn, low)


def as_rows(block):
    return block.reshape(-1, CH)


def windows(pad_ref, cols_ref):
    for a in range(3):
        for b in range(3):
            part = pad_ref[:, a : a + EDGE, b : b + EDGE, :].astype(BF16)
            cols_ref[:, (3 * a + b) * CH : (3 * a + b + 1) * CH] = as_rows(part)


def triples(line_ref, cols_ref):
    for at in range(3):
        part = line_ref[:, 2 - at : 2 - at + EDGE, :].astype(BF16)
        cols_ref[0 : line_ref.shape[0] * EDGE, at * CH : (at + 1) * CH] = as_rows(part)


def pick(rows_ref, at, count, side, base=0):
    lanes = pl.ds(pl.multiple_of(base + side * CH, CH), CH)
    return rows_ref[pl.ds(at, count), lanes]


def pad_place(side):
    return {0: 0, 1: EDGE + 1, 2: EDGE + 1, 3: 0}[side]


def edge_place(side):
    return {0: 1, 1: EDGE, 2: EDGE, 3: 1}[side]


def put_side(pad_ref, tile, side, place, rows, add=False):
    if side % 2 == 0:
        if add:
            rows = rows + pad_ref[tile, place, 1 : EDGE + 1, :]
        pad_ref[tile, place, 1 : EDGE + 1, :] = rows
        return
    for i in range(EDGE):
        row = rows[i : i + 1]
        if add:
            row = row + pad_ref[tile, 1 + i, place : place + 1, :]
        pad_ref[tile, 1 + i, place : place + 1, :] = row


def get_side(pad_ref, tile, side, place):
    if side % 2 == 0:
        return pad_ref[tile, place, 1 : EDGE + 1, :]
    rows = [pad_ref[tile, 1 + i, place : place + 1, :] for i in range(EDGE)]
    return jnp.concatenate(rows, axis=0)


def near_at(n):
    return 8 * n


def lateral_at(j):
    return 96 + 8 * j


def table_kernel(near_ref, code_ref, slot_ref, index_ref, turn_ref):
    total = slot_ref.shape[0]
    tiles = 3
    core = lax.axis_index("c")
    at_y = lax.axis_index("y")
    at_z = lax.axis_index("z")
    first = ((at_y * 2 + at_z) * 2 + core) * tiles

    def look(i, found):
        here = slot_ref[i]
        return tuple(jnp.where(here == first + k, i, found[k]) for k in range(tiles))

    own = lax.fori_loop(0, total, look, (jnp.int32(0),) * tiles)

    def place(tile):
        slot = slot_ref[tile]
        owner = slot // tiles
        chip = ((owner // 4) ^ at_y) * 2 + ((owner // 2) % 2 ^ at_z)
        local = slot % tiles
        return (owner + core) % 2, (owner // 2) * tiles + local, chip * tiles + local

    column = lax.broadcasted_iota(jnp.int32, (EDGE, 12 * EDGE), 1)
    row = lax.broadcasted_iota(jnp.int32, (EDGE, 12 * EDGE), 0)
    for side in range(4):
        for k in range(tiles):
            n = side * tiles + k
            near = near_ref[own[k], side]
            code = code_ref[own[k], side]
            near_side = code // 2
            reverse = code % 2
            other, slot, crossed = place(near)
            index_ref[near_at(n)] = other
            index_ref[near_at(n) + 1] = slot
            index_ref[near_at(n) + 4] = crossed
            index_ref[near_at(n) + 2] = near_side
            index_ref[near_at(n) + 3] = reverse
            source = jnp.where(reverse == 1, EDGE - 1 - row, row) + n * EDGE
            turn_ref[n * EDGE : (n + 1) * EDGE, :] = (
                jnp.where(column == source, 1.0, 0.0).astype(F32).astype(BF16)
            )
            upright = near_side % 2
            far = jnp.where((near_side == 1) | (near_side == 2), 1, 0)
            for h in range(2):
                lateral = jnp.where(upright == 1, (0, 2)[h], (3, 1)[h])
                tile = near_ref[near, lateral]
                lateral_code = code_ref[near, lateral]
                other, slot, crossed = place(tile)
                at = lateral_at(2 * n + h)
                index_ref[at] = other
                index_ref[at + 1] = slot
                index_ref[at + 4] = crossed
                index_ref[at + 2] = lateral_code // 2
                index_ref[at + 3] = (far + lateral_code) % 2


def table_row(mine_ref, other_ref, index_ref, at, depth, crossed=False):
    slot = index_ref[at + (4 if crossed else 1)]
    side = index_ref[at + 2]
    mine = mine_ref[slot, side, depth]
    other = other_ref[slot, side, depth]
    return jnp.where(index_ref[at] == 0, mine.astype(F32), other.astype(F32))


def end_rows(mine_ref, other_ref, index_ref, j, crossed=False):
    row = table_row(mine_ref, other_ref, index_ref, lateral_at(j), 0, crossed)
    far = index_ref[lateral_at(j) + 3] == 1
    last = EDGE - 1
    return far, jnp.where(far, row[last:], row[:1]), jnp.where(far, row[last - 1 : last], row[1:2])


def forward_kernel(
    index_ref, turn_ref, x_ref, ring_ref, mine_ref, other_ref, skip_ref, down_ref,
    w1_ref, w1_sides_ref, w2_ref, w2_back_ref, w2_adjoint_ref, wc_ref, wc_back_ref,
    coarse_ref, delta_ring_ref, grad_ref, pre_ref, inner_ref, strip_pre_ref, sent_ref,
    pad_ref, pad2_ref, patch_ref, cols_ref, cols2_ref, strip_ref, wide_ref, split_ref,
    line_ref, line_cols_ref, fine_ref, down_cols_ref,
):
    tiles = x_ref.shape[0]
    patch_ref[...] = jnp.zeros_like(patch_ref)
    pad_ref[...] = jnp.zeros_like(pad_ref)
    pad2_ref[...] = jnp.zeros_like(pad2_ref)
    line_ref[...] = jnp.zeros_like(line_ref)
    split_ref[...] = jnp.zeros_like(split_ref)
    turn = turn_ref[...]

    pad_ref[:, 1 : EDGE + 1, 1 : EDGE + 1, :] = x_ref[...].astype(F32)
    near = []
    own = []
    for n in range(12):
        side, k = n // tiles, n % tiles
        own.append(ring_ref[k, side, 0])
        edge = table_row(mine_ref, other_ref, index_ref, near_at(n), 0)
        near.append(edge)
        patch_ref[n, 1, 1 : EDGE + 1, :] = edge
        patch_ref[n, 2, 1 : EDGE + 1, :] = table_row(
            mine_ref, other_ref, index_ref, near_at(n), 1
        )
        for h in range(2):
            _, outer, inner = end_rows(mine_ref, other_ref, index_ref, 2 * n + h)
            at = (0, EDGE + 1)[h]
            patch_ref[n, 1, at : at + 1, :] = outer
            patch_ref[n, 2, at : at + 1, :] = inner
    seams = dot(turn, jnp.concatenate(near, axis=0).astype(BF16))
    own_turned = dot(turn, jnp.concatenate(own, axis=0))
    patch_ref[:, 0, 1 : EDGE + 1, :] = own_turned.reshape(12, EDGE, CH)
    for n in range(12):
        side, k = n // tiles, n % tiles
        put_side(pad_ref, k, side, pad_place(side), seams[n * EDGE : (n + 1) * EDGE])
    for r in range(3):
        for b in range(3):
            part = patch_ref[:, r, b : b + EDGE, :].astype(BF16)
            strip_ref[:, (3 * r + b) * CH : (3 * r + b + 1) * CH] = as_rows(part)
    wide_ref[...] = dot(strip_ref[...], w1_sides_ref[...])
    for n in range(12):
        strip_pre_ref[n * EDGE : (n + 1) * EDGE, :] = pick(
            wide_ref, n * EDGE, EDGE, index_ref[near_at(n) + 2]
        )
    windows(pad_ref, cols_ref)
    pre_ref[...] = dot(cols_ref[...], w1_ref[...])
    first_act = gelu(pre_ref[...]).astype(BF16).astype(F32)
    pad2_ref[:, 1 : EDGE + 1, 1 : EDGE + 1, :] = first_act.reshape(tiles, EDGE, EDGE, CH)
    strip_act = dot(turn, gelu(strip_pre_ref[...]).astype(BF16))
    for n in range(12):
        side, k = n // tiles, n % tiles
        put_side(pad2_ref, k, side, pad_place(side), strip_act[n * EDGE : (n + 1) * EDGE])
    windows(pad2_ref, cols2_ref)
    second_pre = dot(cols2_ref[...], w2_ref[...])
    second_act = gelu(second_pre).astype(BF16).astype(F32)
    fine_ref[...] = second_act.reshape(tiles, EDGE, EDGE, CH)
    half = EDGE // 2
    for a in range(2):
        for b in range(2):
            part = fine_ref[:, pl.ds(a, half, 2), pl.ds(b, half, 2), :]
            down_cols_ref[:, (2 * a + b) * CH : (2 * a + b + 1) * CH] = as_rows(part).astype(BF16)
    coarse_ref[...] = dot(down_cols_ref[...], wc_ref[...]).astype(BF16)
    down = down_ref[...]
    spread_down = dot(down, wc_back_ref[...])
    for a in range(2):
        for b in range(2):
            part = spread_down[:, (2 * a + b) * CH : (2 * a + b + 1) * CH]
            fine_ref[:, pl.ds(a, half, 2), pl.ds(b, half, 2), :] = part.reshape(
                tiles, half, half, CH
            )
    second_cot = skip_ref[...].astype(F32) + fine_ref[...]
    delta = (gelu_slope(second_pre) * as_rows(second_cot)).astype(BF16)
    pad_ref[...] = jnp.zeros_like(pad_ref)
    pad_ref[:, 1 : EDGE + 1, 1 : EDGE + 1, :] = delta.astype(F32).reshape(tiles, EDGE, EDGE, CH)
    for side in range(4):
        step = (1, -1, -1, 1)[side]
        for k in range(tiles):
            for depth in range(2):
                rows = get_side(pad_ref, k, side, edge_place(side) + step * depth)
                delta_ring_ref[k, side, depth] = rows.astype(BF16)
                if depth == 0:
                    line_ref[side * tiles + k, 1 : EDGE + 1, :] = rows
    core = lax.axis_index("c")

    def put_grad(at, block):
        half = at // 11
        rows = slice(at % 11 * CH, (at % 11 + 1) * CH)
        grad_ref[jnp.where(core == half, 0, 1), rows, :] = block

    down_grad = dot_rows(down_cols_ref[...], down)
    for at in range(4):
        put_grad(18 + at, down_grad[at * CH : (at + 1) * CH])
    second_grad = dot_rows(cols2_ref[...], delta)
    for at in range(9):
        put_grad(9 + at, second_grad[at * CH : (at + 1) * CH])

    windows(pad_ref, cols2_ref)
    inner = dot(cols2_ref[...], w2_back_ref[...])
    inner_ref[...] = inner
    inner_delta = (gelu_slope(pre_ref[...]) * inner).astype(BF16)
    triples(line_ref, line_cols_ref)
    rims = []
    for side in range(4):
        rows = slice(side * tiles * EDGE, (side + 1) * tiles * EDGE)
        lanes = slice(side * CH, (side + 1) * CH)
        rims.append(dot(line_cols_ref[rows, :], w2_adjoint_ref[: 3 * CH, lanes]))
    sent = turned(turn, jnp.concatenate(rims, axis=0))
    sent_ref[...] = sent
    sent_delta = (gelu_slope(strip_pre_ref[...]) * sent).astype(BF16)
    for n in range(12):
        lanes = pl.ds(pl.multiple_of(index_ref[near_at(n) + 2] * CH, CH), CH)
        rows = slice(n * EDGE, (n + 1) * EDGE)
        split_ref[rows, lanes] = sent_delta[rows]
    sent_grad = dot_rows(strip_ref[...], split_ref[...])
    first_grad = dot_rows(cols_ref[...], inner_delta)
    for a in range(3):
        for b in range(3):
            at = (3 * a + b) * CH
            block = first_grad[at : at + CH]
            for side, r, k in ((0, a, b), (1, 2 - b, a), (2, 2 - a, b), (3, b, a)):
                source = (3 * r + k) * CH
                block = block + sent_grad[source : source + CH, side * CH : (side + 1) * CH]
            put_grad(3 * a + b, block)


def backward_kernel(
    index_ref, turn_ref, mine_ref, other_ref, pre_ref, inner_ref, strip_pre_ref, sent_ref,
    w1_back_ref, w1_adjoint_ref, w2_adjoint_ref,
    out_ref,
    pad_ref, cols_ref, line_ref, deep_ref, line_cols_ref, deep_cols_ref, ends_ref, wide_ref,
    strip_wide_ref, cot_ref,
):
    tiles = out_ref.shape[0]
    turn = turn_ref[...]
    line_ref[...] = jnp.zeros_like(line_ref)
    deep_ref[...] = jnp.zeros_like(deep_ref)
    ends_ref[...] = jnp.zeros_like(ends_ref)
    pad_ref[...] = jnp.zeros_like(pad_ref)
    for n in range(12):
        for depth, rows_ref in ((0, line_ref), (1, deep_ref)):
            rows_ref[n, 1 : EDGE + 1, :] = table_row(
                mine_ref, other_ref, index_ref, near_at(n), depth, True
            )
    for j in range(24):
        far, outer, inner = end_rows(mine_ref, other_ref, index_ref, j, True)
        blank = jnp.zeros_like(inner)
        ends_ref[j : j + 1, :CH] = jnp.where(far, blank, inner)
        ends_ref[j : j + 1, CH : 2 * CH] = outer
        ends_ref[j : j + 1, 2 * CH :] = jnp.where(far, inner, blank)
    strip_rows = 12 * EDGE
    triples(line_ref, line_cols_ref)
    line_cols_ref[strip_rows:, :] = ends_ref[...].astype(BF16)
    triples(deep_ref, deep_cols_ref)
    wide_ref[...] = dot(line_cols_ref[...], w2_adjoint_ref[: 3 * CH])
    strip_wide_ref[...] = dot(deep_cols_ref[...], w2_adjoint_ref[: 3 * CH]) + dot(
        line_cols_ref[:strip_rows, :], w2_adjoint_ref[3 * CH :]
    )
    cot_ref[...] = sent_ref[...]
    rims = []
    for n in range(12):
        side = index_ref[near_at(n) + 2]
        rows = slice(n * EDGE, (n + 1) * EDGE)
        rims.append(pick(wide_ref, n * EDGE, EDGE, side))
        cot_ref[rows, :] += pick(strip_wide_ref, n * EDGE, EDGE, side)
        for h in range(2):
            j = 2 * n + h
            at = n * EDGE + (0, EDGE - 1)[h]
            cot_ref[at : at + 1, :] += pick(
                wide_ref, strip_rows + j, 1, index_ref[lateral_at(j) + 2]
            )
    rims = turned(turn, jnp.concatenate(rims, axis=0))
    pad_ref[:, 1 : EDGE + 1, 1 : EDGE + 1, :] = inner_ref[...].reshape(tiles, EDGE, EDGE, CH)
    for n in range(12):
        side, k = n // tiles, n % tiles
        rows = rims[n * EDGE : (n + 1) * EDGE]
        put_side(pad_ref, k, side, edge_place(side), rows, add=True)
    middle = pad_ref[:, 1 : EDGE + 1, 1 : EDGE + 1, :]
    delta = gelu_slope(pre_ref[...]) * as_rows(middle)
    delta = delta.astype(BF16).astype(F32)
    pad_ref[:, 1 : EDGE + 1, 1 : EDGE + 1, :] = delta.reshape(tiles, EDGE, EDGE, CH)
    windows(pad_ref, cols_ref)
    strip_delta = (gelu_slope(strip_pre_ref[...]) * cot_ref[...]).astype(BF16).astype(F32)
    line_ref[:, 1 : EDGE + 1, :] = strip_delta.reshape(12, EDGE, CH)
    triples(line_ref, deep_cols_ref)
    strip_wide_ref[...] = dot(deep_cols_ref[...], w1_adjoint_ref[...])
    rims = []
    for n in range(12):
        rims.append(pick(strip_wide_ref, n * EDGE, EDGE, index_ref[near_at(n) + 2]))
    rims = turned(turn, jnp.concatenate(rims, axis=0))
    grad = dot(cols_ref[...], w1_back_ref[...])
    pad_ref[:, 1 : EDGE + 1, 1 : EDGE + 1, :] = grad.reshape(tiles, EDGE, EDGE, CH)
    for n in range(12):
        side, k = n // tiles, n % tiles
        rows = rims[n * EDGE : (n + 1) * EDGE]
        put_side(pad_ref, k, side, edge_place(side), rows, add=True)
    out_ref[...] = pad_ref[:, 1 : EDGE + 1, 1 : EDGE + 1, :].astype(BF16)


def pin_kernel(*refs):
    pass


def first_sum_kernel(pieces_ref, own_ref, across_ref, copies_ref, pair_ref):
    total = jnp.sum(pieces_ref[...].astype(F32), axis=0)
    for at in range(copies_ref.shape[0]):
        copies_ref[at] = total
    pair_ref[0] = own_ref[...]
    pair_ref[1] = across_ref[...]


def second_sum_kernel(pieces_ref, own_ref, one_ref, two_ref, three_ref, copies_ref, table_ref):
    total = jnp.sum(pieces_ref[...], axis=0).astype(BF16)
    for at in range(copies_ref.shape[0]):
        copies_ref[at] = total
    for at, part_ref in enumerate((own_ref, one_ref, two_ref, three_ref)):
        table_ref[at] = part_ref[...]


def finish_kernel(scale, mine_ref, other_ref, first_ref, second_ref, down_ref):
    core = lax.axis_index("c")
    for at in range(22):
        half = at // 11
        rows = slice(at % 11 * CH, (at % 11 + 1) * CH)
        block = jnp.where(core == half, mine_ref[rows, :], other_ref[rows, :])
        out_ref, base = ((first_ref, 0), (second_ref, 9), (down_ref, 18))[at // 9]
        out_ref[at - base] = block.astype(F32) * scale


def whole(space):
    return pl.BlockSpec(memory_space=space)


def shards(
    activations,
    conv1_weight,
    conv2_weight,
    coarse_kernel_weight,
    skip_cotangent,
    down_cotangent,
    face_neighbours,
    seam_codes,
    tile_slots,
):
    value_entries = activations[0]
    tiles = value_entries.shape[0]
    total_tiles = tile_slots.shape[0]
    cells = tiles * EDGE * EDGE
    strips = 4 * tiles * EDGE
    half = EDGE // 2
    smem, vmem = whole(pltpu.SMEM), whole(pltpu.VMEM)
    shape = jax.ShapeDtypeStruct
    params = pltpu.CompilerParams(vmem_limit_bytes=40 * 1024 * 1024)

    own_rings = rings(value_entries)
    mine = spread(own_rings, CHIPS)

    index, turn = pl.pallas_call(
        table_kernel,
        out_shape=(shape((288,), jnp.int32), shape((strips, strips), BF16)),
        in_specs=[smem] * 3,
        out_specs=(smem, vmem),
        compiler_params=params,
    )(face_neighbours, seam_codes, tile_slots)
    frames1 = side_frames(conv1_weight)
    frames2 = side_frames(conv2_weight)
    w1_sides = jnp.transpose(frames1, (1, 2, 3, 0, 4)).reshape(9 * CH, 4 * CH)
    w1_adjoint = frame_adjoint(frames1[:, :1])
    w2_adjoint = frame_adjoint(frames2[:, :2])
    w1_back = flipped(conv1_weight).reshape(9 * CH, CH)
    w2_back = flipped(conv2_weight).reshape(9 * CH, CH)
    wc_back = jnp.transpose(coarse_kernel_weight, (3, 0, 1, 2)).reshape(CH, 4 * CH)

    ready = [index, turn, w1_sides, w1_adjoint, w2_adjoint, w1_back, w2_back, wc_back]
    anywhere = whole(pl.ANY)
    mine = pl.pallas_call(
        pin_kernel,
        out_shape=shape(mine.shape, BF16),
        in_specs=[anywhere] * (1 + len(ready)),
        out_specs=anywhere,
        input_output_aliases={0: 0},
    )(mine, *ready)
    other = swap_core(mine)

    def table(block):
        return block.reshape((-1,) + own_rings.shape[1:])

    coarse, delta_rings, grads, pre, inner, strip_pre, sent = pl.pallas_call(
        forward_kernel,
        out_shape=(
            shape((tiles * half * half, CH), BF16),
            shape(own_rings.shape, BF16),
            shape((2, 11 * CH, CH), F32),
            shape((cells, CH), F32),
            shape((cells, CH), F32),
            shape((strips, CH), F32),
            shape((strips, CH), F32),
        ),
        in_specs=[smem] + [vmem] * 14,
        out_specs=(vmem,) * 7,
        scratch_shapes=[
            pltpu.VMEM((tiles, EDGE + 2, EDGE + 8, CH), F32),
            pltpu.VMEM((tiles, EDGE + 2, EDGE + 8, CH), F32),
            pltpu.VMEM((4 * tiles, 3, EDGE + 8, CH), F32),
            pltpu.VMEM((cells, 9 * CH), BF16),
            pltpu.VMEM((cells, 9 * CH), BF16),
            pltpu.VMEM((strips, 9 * CH), BF16),
            pltpu.VMEM((strips, 4 * CH), F32),
            pltpu.VMEM((strips, 4 * CH), BF16),
            pltpu.VMEM((4 * tiles, EDGE + 8, CH), F32),
            pltpu.VMEM((strips, 3 * CH), BF16),
            pltpu.VMEM((tiles, EDGE, EDGE, CH), F32),
            pltpu.VMEM((tiles * half * half, 4 * CH), BF16),
        ],
        compiler_params=params,
    )(
        index, turn, value_entries, own_rings, table(mine), table(other), skip_cotangent[0],
        down_cotangent.reshape(-1, CH), conv1_weight.reshape(9 * CH, CH), w1_sides,
        conv2_weight.reshape(9 * CH, CH), w2_back, w2_adjoint,
        coarse_kernel_weight.reshape(4 * CH, CH), wc_back,
    )
    across = swap_apart(delta_rings, "z", 1)
    kept = (grads[0] + swap_core(grads[1])).astype(BF16)
    plane = lax.axis_size(PLANE)
    part = kept.shape[0] // plane
    pieces = lax.all_to_all(kept.reshape(plane, part, CH), PLANE, 0, 0)
    deep = lax.axis_size(DEPTH)
    copies, pair = pl.pallas_call(
        first_sum_kernel,
        out_shape=(shape((deep, part, CH), F32), shape((2,) + delta_rings.shape, BF16)),
        in_specs=[vmem] * 3,
        out_specs=(vmem,) * 2,
        compiler_params=params,
    )(pieces, delta_rings, across)
    along = [swap_apart(pair, "y", apart) for apart in (1, 2, 3)]
    pieces = lax.all_to_all(copies, DEPTH, 0, 0)
    copies, mine = pl.pallas_call(
        second_sum_kernel,
        out_shape=(shape((plane, part, CH), BF16), shape((4,) + pair.shape, BF16)),
        in_specs=[vmem] * 5,
        out_specs=(vmem,) * 2,
        compiler_params=params,
    )(pieces, pair, *along)
    other = swap_core(mine)
    summed = lax.all_to_all(copies, PLANE, 0, 0).reshape(-1, CH)
    summed_other = swap_core(summed)
    input_grad = pl.pallas_call(
        backward_kernel,
        out_shape=shape(value_entries.shape, BF16),
        in_specs=[smem] + [vmem] * 10,
        out_specs=vmem,
        scratch_shapes=[
            pltpu.VMEM((tiles, EDGE + 2, EDGE + 8, CH), F32),
            pltpu.VMEM((cells, 9 * CH), BF16),
            pltpu.VMEM((4 * tiles, EDGE + 8, CH), F32),
            pltpu.VMEM((4 * tiles, EDGE + 8, CH), F32),
            pltpu.VMEM((strips + 32, 3 * CH), BF16),
            pltpu.VMEM((strips, 3 * CH), BF16),
            pltpu.VMEM((32, 3 * CH), F32),
            pltpu.VMEM((strips + 32, 4 * CH), F32),
            pltpu.VMEM((strips, 4 * CH), F32),
            pltpu.VMEM((strips, CH), F32),
        ],
        compiler_params=params,
    )(
        index, turn, table(mine), table(other), pre, inner, strip_pre, sent,
        w1_back, w1_adjoint, w2_adjoint,
    )
    scale = 1.0 / math.sqrt(lax.axis_size(("w", "x")) * total_tiles * EDGE * EDGE)
    first_grad, second_grad, down_grad = pl.pallas_call(
        functools.partial(finish_kernel, scale),
        out_shape=tuple(shape((count, CH, CH), F32) for count in (9, 9, 4)),
        in_specs=[vmem] * 2,
        out_specs=(vmem,) * 3,
        compiler_params=params,
    )(summed, summed_other)
    return (
        coarse.reshape((1, tiles, half, half, CH)),
        input_grad[None],
        first_grad.reshape(conv1_weight.shape),
        second_grad.reshape(conv2_weight.shape),
        down_grad.reshape(coarse_kernel_weight.shape),
    )


def solution(mesh):
    batch = mesh.shape["batch"]
    along_x = 4 if batch % 4 == 0 else 1
    fine = Mesh(
        mesh.devices.reshape(4, 2, 2, batch // along_x, along_x), ("y", "z", "c", "w", "x")
    )
    field = P(("w", "x"), ("y", "z", "c"), None, None, None)
    return jax.shard_map(
        shards,
        mesh=fine,
        in_specs=(field, P(), P(), P(), field, field, P(), P(), P()),
        out_specs=(field, field, P(), P(), P()),
        check_vma=False,
    )
```

time: 448 us -> 117 us (0.26)
  waiting for transfers between devices: 224 us -> 21 us
  blocking collectives: 146 us -> 15.1 us
  starting transfers between devices: 0.04 us -> 38.8 us
  matrix products: 22.8 us -> 0 us
  Pallas kernels: 0 us -> 15.4 us
  between operations: 15.9 us -> 1.05 us
  other arithmetic: 9.75 us -> 2.03 us
  local copies, waits for them, and re-layouts: 27.6 us -> 22.7 us
    psum x1 -> x0, waiting for transfers between devices: 224 us -> none  [shards(): lax.psum((first_grad, second_grad, down_grad), ('space', 'batch'))]
    all_gather x4 -> x0, blocking collectives: 146 us -> none  [the longest x2 73.6 us: seams_of(): lax.all_gather(edge_rows(field_values), 'space', axis=0, tiled=True)]
    all_to_all x0 -> x3, starting transfers between devices: none -> 25.4 us  [the longest x1 11.8 us: spread(): return lax.all_to_all(copies, axes, 0, 0)]
    dot_general x90 -> x0, matrix products: 22.8 us -> none  [the longest x18 9.58 us: kernel_grad(): lax.dot_general(window, flattened, (((0,), (0,)), ((), ())), preferred_el...]
    ppermute x0 -> x8, waiting for transfers between devices: none -> 18.5 us  [the longest x4 13.3 us: swap_apart(): return lax.ppermute(block, axis, [(i, i ^ apart) for i in range(number)])]
    pallas_call x0 -> x7, Pallas kernels: none -> 15.4 us  [the longest x1 6.37 us: shards(): pl.pallas_call(forward_kernel, out_shape=(shape((tiles * half * half, CH)...]
    all_to_all x0 -> x1, blocking collectives: none -> 15.1 us  [shards(): summed = lax.all_to_all(copies, PLANE, 0, 0).reshape(-1, CH)]
    ppermute x0 -> x8, starting transfers between devices: none -> 13.4 us  [the longest x4 8.17 us: swap_core(): return lax.ppermute(block, 'c', [(0, 1), (1, 0)])]
  transfers between devices with their start and end apart: 1 -> 11, of which waited for: 1 -> 8; matrix products, arithmetic and copies ran while one was open for 2% -> 11% of each run, Pallas kernels for 0% -> 4%
where the time goes in v2:
time: 117 us; the launch traced here: 116 us
  starting transfers between devices  38.8 us (33%)
  local copies, waits for them, and re-layouts  22.7 us (19%)
  waiting for transfers between devices  21 us (18%)
  Pallas kernels  15.4 us (13%)
  blocking collectives  15.1 us (13%)
  other arithmetic  2.03 us (2%)
    all_to_all x1, blocking collectives, shards(): summed = lax.all_to_all(copies, PLANE, 0, 0).reshape(-1, CH)  15.1 us
    unnamed x80, local copies, waits for them, and re-layouts  14.4 us
    ppermute x4, waiting for transfers between devices, swap_apart(): return lax.ppermute(block, axis, [(i, i ^ apart) for i in range(number)])  13.3 us
    all_to_all x1, starting transfers between devices, spread(): return lax.all_to_all(copies, axes, 0, 0)  11.8 us
    ppermute x4, starting transfers between devices, swap_core(): return lax.ppermute(block, 'c', [(0, 1), (1, 0)])  8.17 us
    all_to_all x1, starting transfers between devices, shards(): pieces = lax.all_to_all(kept.reshape(plane, part, CH), PLANE, 0, 0)  8.11 us
    pallas_call x1, Pallas kernels, shards(): pl.pallas_call(forward_kernel, out_shape=(shape((tiles * half * half, CH)...  6.37 us
    all_to_all x1, starting transfers between devices, shards(): pieces = lax.all_to_all(copies, DEPTH, 0, 0)  5.49 us
  transfers between devices with their start and end apart: 11, of which 8 were waited for; matrix products, arithmetic and copies ran while one was open for 11% of the time, Pallas kernels for 4%

profile of v2, /device:TPU:1, one launch (start us, length us, event | category | flops | bytes accessed | tf_op | source)
XLA Modules:
  0.0 116.1 jit_solution(11615898405447471157)
XLA Ops:
  0.6 1.0 copy.48
  1.9 1.1 broadcast_in_dim.4
  3.0 11.8 %all-to-all-start = ((bf16[8,3,4,2,16,128]{5,4,3,2,1,0:T(8,128)(2,1)}), bf16[8,3,4,2,16,128]{5,4,3,2,1,0:T(8,128)(2,1)S(1)}, u32[]{:S(2)}, u32[]{:S(2)}) async-start(bf16[8,3,4,2,16,128]{5,4,3,2,1,0:T(8,128)(2,1)} %broadcast_in_dim.4), calls=%async_computation | async-start | bytes 1572864 | tf_op jit(solution)/shard_map/all_to_all | solution.py:30
  15.0 0.8 copy.31.refs_8_.wc_back_ref
  15.8 0.8 reverse_bitcast_fusion.1
  16.6 0.9 copy.26
  17.6 0.9 copy.27
  18.6 1.0 fusion
  19.6 1.5 %copy.25 = bf16[2,3,128,4,128]{4,3,2,1,0:T(4,128)(2,1)S(1)} copy(bf16[2,3,128,4,128]{2,4,1,0,3:T(8,128)(2,1)} %fusion) | data formatting | bytes 1572864 | tf_op jit(solution)/shard_map/transpose | solution.py:60
  21.1 1.0 copy.44
  22.4 1.0 copy.23
  23.4 1.8 %copy.45 = bf16[48,8,4,128]{3,1,2,0:T(8,128)(2,1)} copy(bf16[48,8,4,128]{3,2,1,0:T(4,128)(2,1)} %bitcast.123) | data formatting | bytes 786432
  25.2 0.9 copy.22
  26.1 1.3 %copy.43 = bf16[144,8,4,128]{3,1,2,0:T(8,128)(2,1)} copy(bf16[144,8,4,128]{3,2,1,0:T(4,128)(2,1)S(1)} %bitcast.117) | data formatting | bytes 2359296
  27.4 3.7 %shard_map.128 = (s32[288]{0:T(512)S(1)}, bf16[192,192]{1,0:T(8,128)(2,1)S(1)}) custom-call(s32[48,4]{1,0:T(8,128)S(1)} %copy.15.near_ref, s32[48,4]{1,0:T(8,128)S(1)} %copy.16.code_ref, s32[48]{0:T(128)S(1)} %copy-done.32), custom_call_target="tpu_custom_call" | custom-call | tf_op jit(solution)/shard_map/pallas_call | solution.py:473
  31.1 0.6 copy-done.12
  31.7 0.6 copy-done.30
  32.6 3.3 %collective-permute-start = (bf16[8,3,4,2,16,128]{5,4,3,2,1,0:T(8,128)(2,1)}, bf16[8,3,4,2,16,128]{5,4,3,2,1,0:T(8,128)(2,1)S(1)}, u32[]{:S(2)}, u32[]{:S(2)}) collective-permute-start(bf16[8,3,4,2,16,128]{5,4,3,2,1,0:T(8,128)(2,1)} %shard_map.129), channel_id=1, source_target_pairs={{0,16},{16,0},{1,17},{17,1},{2,18},{18,2},{3,19},{19,3},{4,20},{20... | collective-permute-start | bytes 2359304 | tf_op jit(solution)/shard_map/ppermute | solution.py:24
  35.9 2.1 %collective-permute-done = bf16[8,3,4,2,16,128]{5,4,3,2,1,0:T(8,128)(2,1)S(1)} collective-permute-done((bf16[8,3,4,2,16,128]{5,4,3,2,1,0:T(8,128)(2,1)}, bf16[8,3,4,2,16,128]{5,4,3,2,1,0:T(8,128)(2,1)S(1)}, u32[]{:S(2)}, u32[]{:S(2)}) %collective-permute-start) | collective-permute-done | bytes 786464 | tf_op jit(solution)/shard_map/ppermute | solution.py:24
  38.0 1.1 copy-done.3
  39.2 1.0 copy-done.7
  40.1 0.9 copy-done.11
  41.0 0.9 copy-done.13
  41.9 0.9 copy-done.15
  42.9 0.9 copy-done.17
  43.8 0.9 copy-done.22
  44.7 6.4 %shard_map.130 = (bf16[192,128]{1,0:T(8,128)(2,1)}, bf16[3,4,2,16,128]{4,3,2,1,0:T(8,128)(2,1)S(1)}, f32[2,1408,128]{2,1,0:T(8,128)S(1)}, f32[768,128]{1,0:T(8,1...) custom-call(s32[288]{0:T(512)S(1)} %copy-done.31, ...), custom_call_target="tpu_custom_call" | custom-call | tf_op jit(solution)/shard_map/pallas_call | solution.py:503
  51.2 0.5 collective-permute-start.1
  51.6 1.8 %collective-permute-done.1 = f32[1408,128]{1,0:T(8,128)S(1)} collective-permute-done((f32[1408,128]{1,0:T(8,128)S(1)}, f32[1408,128]{1,0:T(8,128)S(1)}, u32[]{:S(2)}, u32[]{:S(2)}) %collective-permute-start.1) | collective-permute-done | bytes 720928 | tf_op jit(solution)/shard_map/ppermute | solution.py:24
  53.5 0.8 fusion.1
  54.3 8.1 %all-to-all-start.1 = ((bf16[16,88,128]{2,1,0:T(8,128)(2,1)}), bf16[16,88,128]{2,1,0:T(8,128)(2,1)S(1)}, u32[]{:S(2)}, u32[]{:S(2)}) async-start(bf16[16,88,128]{2,1,0:T(8,128)(2,1)} %bitcast.38), calls=%async_computation.1 | async-start | bytes 720896 | tf_op jit(solution)/shard_map/all_to_all | solution.py:541
  62.4 1.9 %collective-permute-start.2 = (bf16[3,4,2,16,128]{4,3,2,1,0:T(8,128)(2,1)S(1)}, bf16[3,4,2,16,128]{4,3,2,1,0:T(8,128)(2,1)S(1)}, u32[]{:S(2)}, u32[]{:S(2)}) collective-permute-start(bf16[3,4,2,16,128]{4,3,2,1,0:T(8,128)(2,1)S(1)} %get-tuple-element.25.own_ref), channel_id=1, source_target_pairs={{0,32},{32,0},{1,33},{33,1},{2,34},{34,2},{3,35},{35,3},{4,36},{36... | collective-permute-start | bytes 294920 | tf_op jit(solution)/shard_map/ppermute | solution.py:35
  64.3 5.5 %collective-permute-done.2.across_ref = bf16[3,4,2,16,128]{4,3,2,1,0:T(8,128)(2,1)S(1)} collective-permute-done((bf16[3,4,2,16,128]{4,3,2,1,0:T(8,128)(2,1)S(1)}, bf16[3,4,2,16,128]{4,3,2,1,0:T(8,128)(2,1)S(1)}, u32[]{:S(2)}, u32[]{:S(2)}) %collective-permute-start.2) | collective-permute-done | bytes 98336 | tf_op jit(solution)/shard_map/ppermute | solution.py:35
  69.9 1.4 %all-to-all-done.1.pieces_ref = bf16[16,88,128]{2,1,0:T(8,128)(2,1)S(1)} async-done(((bf16[16,88,128]{2,1,0:T(8,128)(2,1)}), bf16[16,88,128]{2,1,0:T(8,128)(2,1)S(1)}, u32[]{:S(2)}, u32[]{:S(2)}) %all-to-all-start.1) | async-done | bytes 360480 | tf_op jit(solution)/shard_map/all_to_all | solution.py:541
  71.3 0.9 copy-done.24
  72.2 0.8 shard_map.131
  73.0 5.5 %all-to-all-start.2 = ((f32[8,88,128]{2,1,0:T(8,128)}), f32[8,88,128]{2,1,0:T(8,128)S(1)}, u32[]{:S(2)}, u32[]{:S(2)}) async-start(f32[8,88,128]{2,1,0:T(8,128)} %get-tuple-element.26), calls=%async_computation.2 | async-start | bytes 720896 | tf_op jit(solution)/shard_map/all_to_all | solution.py:551
  78.5 2.5 %collective-permute-start.5 = (bf16[2,3,4,2,16,128]{5,4,3,2,1,0:T(8,128)(2,1)S(1)}, bf16[2,3,4,2,16,128]{5,4,3,2,1,0:T(8,128)(2,1)S(1)}, u32[]{:S(2)}, u32[]{:S(2)}) collective-permute-start(bf16[2,3,4,2,16,128]{5,4,3,2,1,0:T(8,128)(2,1)S(1)} %get-tuple-element.27.own_ref), channel_id=1, source_target_pairs={{0,192},{64,128},{128,64},{192,0},{1,193},{65,129},{129,65},{193,1... | collective-permute-start | bytes 589832 | tf_op jit(solution)/shard_map/ppermute | solution.py:35
  80.9 0.6 collective-permute-start.4
  81.8 7.1 %collective-permute-done.5.three_ref = bf16[2,3,4,2,16,128]{5,4,3,2,1,0:T(8,128)(2,1)S(1)} collective-permute-done((bf16[2,3,4,2,16,128]{5,4,3,2,1,0:T(8,128)(2,1)S(1)}, bf16[2,3,4,2,16,128]{5,4,3,2,1,0:T(8,128)(2,1)S(1)}, u32[]{:S(2)}, u32[]{:S(2)}) %collective-permute-start.5) | collective-permute-done | bytes 196640 | tf_op jit(solution)/shard_map/ppermute | solution.py:35
  89.0 0.6 collective-permute-done.3.one_ref
  89.5 1.1 all-to-all-done.2.pieces_ref
  90.7 2.8 %collective-permute-start.6 = (bf16[4,2,3,4,2,16,128]{6,5,4,3,2,1,0:T(8,128)(2,1)S(1)}, bf16[4,2,3,4,2,16,128]{6,5,4,3,2,1,0:T(8,128)(2,1)S(1)}, u32[]{:S(2)}, u32[]{:S(2)}) collective-permute-start(bf16[4,2,3,4,2,16,128]{6,5,4,3,2,1,0:T(8,128)(2,1)S(1)} %get-tuple-element.28), channel_id=1, source_target_pairs={{0,16},{16,0},{1,17},{17,1},{2,18},{18,2},{3,19},{19,3},{4,20},{20... | collective-permute-start | bytes 2359304 | tf_op jit(solution)/shard_map/ppermute | solution.py:24
  93.6 15.1 %all_to_all.20 = bf16[16,88,128]{2,1,0:T(8,128)(2,1)S(1)} all-to-all(bf16[16,88,128]{2,1,0:T(8,128)(2,1)S(1)} %get-tuple-element.33), channel_id=1, replica_groups=mesh['y'=4,'z'=2,'c'=2,'w'=4,'x'=4] {'x','y'}, dimensions={0} | all-to-all | bytes 720896 | tf_op jit(solution)/shard_map/all_to_all | solution.py:560
  108.6 1.6 %collective-permute-start.7 = (bf16[1408,128]{1,0:T(8,128)(2,1)S(1)}, bf16[1408,128]{1,0:T(8,128)(2,1)S(1)}, u32[]{:S(2)}, u32[]{:S(2)}) collective-permute-start(bf16[1408,128]{1,0:T(8,128)(2,1)S(1)} %bitcast.107), channel_id=1, source_target_pairs={{0,16},{16,0},{1,17},{17,1},{2,18},{18,2},{3,19},{19,3},{4,20},{20... | collective-permute-start | bytes 1081352 | tf_op jit(solution)/shard_map/ppermute | solution.py:24
  110.2 1.3 %collective-permute-done.7.other_ref = bf16[1408,128]{1,0:T(8,128)(2,1)S(1)} collective-permute-done((bf16[1408,128]{1,0:T(8,128)(2,1)S(1)}, bf16[1408,128]{1,0:T(8,128)(2,1)S(1)}, u32[]{:S(2)}, u32[]{:S(2)}) %collective-permute-start.7) | collective-permute-done | bytes 360480 | tf_op jit(solution)/shard_map/ppermute | solution.py:24
  111.5 1.3 %shard_map.134 = (f32[9,128,128]{2,1,0:T(8,128)}, f32[9,128,128]{2,1,0:T(8,128)}, f32[4,128,128]{2,1,0:T(8,128)}) custom-call(bf16[1408,128]{1,0:T(8,128)(2,1)S(1)} %bitcast.108, bf16[1408,128]{1,0:T(8,128)(2,1)S(1)} %collective-permute-done.7.other_ref), custom_call_target="tpu_custom_call" | custom-call | tf_op jit(solution)/shard_map/pallas_call | solution.py:585
  112.9 3.2 %shard_map.133 = bf16[3,16,16,128]{3,2,1,0:T(8,128)(2,1)} custom-call(s32[288]{0:T(512)S(1)} %copy-done.31, bf16[192,192]{1,0:T(8,128)(2,1)S(1)} %copy-done.14, bf16[24,4,2,16,128]{4,3,2,1,0:T(8,128)(2,1)S(1)} %bitcast.111, bf16[24,4,2,16,128]{4,3,2,1,0:T(8,128)(2,1)S(1)} %bitcast.112, f32[768,128]{1,0:T(8,128)S(1)} %copy-done.19, ...), custom_call_target="tpu_custom_call" | custom-call | tf_op jit(solution)/shard_map/pallas_call | solution.py:562
  (85 shorter events, 1.7 us)
Async XLA Ops:
  1.9 1.1 copy-start.10
  1.9 12.9 %copy-start.34 = (s32[48,4]{0,1:T(4,128)S(1)}, s32[48,4]{0,1:T(4,128)}, u32[]{:S(2)}) copy-start(s32[48,4]{0,1:T(4,128)} %param.15) | copy-start | bytes 2308
  1.9 13.0 %copy-start.35 = (s32[48,4]{0,1:T(4,128)S(1)}, s32[48,4]{0,1:T(4,128)}, u32[]{:S(2)}) copy-start(s32[48,4]{0,1:T(4,128)} %param.16) | copy-start | bytes 2308
  1.9 13.1 %copy-start.16 = (bf16[2,2,128,128]{3,2,1,0:T(8,128)(2,1)S(1)}, bf16[2,2,128,128]{3,2,1,0:T(8,128)(2,1)}, u32[]{:S(2)}) copy-start(bf16[2,2,128,128]{3,2,1,0:T(8,128)(2,1)} %param.12) | copy-start | bytes 393220
  1.9 13.8 %copy-start.4 = (bf16[3,3,128,128]{3,2,1,0:T(8,128)(2,1)S(1)}, bf16[3,3,128,128]{3,2,1,0:T(8,128)(2,1)}, u32[]{:S(2)}) copy-start(bf16[3,3,128,128]{3,2,1,0:T(8,128)(2,1)} %param.10) | copy-start | bytes 884740
  3.0 12.8 %copy-start.5 = (bf16[3,3,128,128]{3,2,1,0:T(8,128)(2,1)S(1)}, bf16[3,3,128,128]{3,2,1,0:T(8,128)(2,1)}, u32[]{:S(2)}) copy-start(bf16[3,3,128,128]{3,2,1,0:T(8,128)(2,1)} %param.11) | copy-start | bytes 884740
  3.0 28.7 %all-to-all-start = ((bf16[8,3,4,2,16,128]{5,4,3,2,1,0:T(8,128)(2,1)}), bf16[8,3,4,2,16,128]{5,4,3,2,1,0:T(8,128)(2,1)S(1)}, u32[]{:S(2)}, u32[]{:S(2)}) async-start(bf16[8,3,4,2,16,128]{5,4,3,2,1,0:T(8,128)(2,1)} %broadcast_in_dim.4), calls=%async_computation | async-start | bytes 1572864 | tf_op jit(solution)/shard_map/all_to_all | solution.py:30
  21.1 1.1 copy-start.33
  26.1 1.3 %copy-start.32 = (s32[48]{0:T(128)S(1)}, s32[48]{0:T(128)}, u32[]{:S(2)}) copy-start(s32[48]{0:T(128)} %slot_ref.1) | copy-start | bytes 580
  31.0 0.6 copy-start.12
  31.7 0.6 copy-start.30
  31.7 0.9 copy-start.2
  32.6 5.4 %copy-start = (bf16[96,8,4,128]{3,1,2,0:T(8,128)(2,1)S(1)}, bf16[96,8,4,128]{3,1,2,0:T(8,128)(2,1)}, u32[]{:S(2)}) copy-start(bf16[96,8,4,128]{3,1,2,0:T(8,128)(2,1)} %copy.44) | copy-start | bytes 2359300
  32.6 5.4 %copy-start.1 = (bf16[144,8,4,128]{3,1,2,0:T(8,128)(2,1)S(1)}, bf16[144,8,4,128]{3,1,2,0:T(8,128)(2,1)}, u32[]{:S(2)}) copy-start(bf16[144,8,4,128]{3,1,2,0:T(8,128)(2,1)} %copy.43) | copy-start | bytes 3538948
  32.6 5.4 %copy-start.9 = (bf16[128,512]{1,0:T(8,128)(2,1)S(1)}, bf16[128,512]{1,0:T(8,128)(2,1)}, u32[]{:S(2)}) copy-start(bf16[128,512]{1,0:T(8,128)(2,1)} %copy.31.refs_8_.wc_back_ref) | copy-start | bytes 393220
  32.6 5.4 %copy-start.29 = (bf16[1,3,8,8,128]{4,3,2,1,0:T(8,128)(2,1)S(1)}, bf16[1,3,8,8,128]{4,3,2,1,0:T(8,128)(2,1)}, u32[]{:S(2)}) copy-start(bf16[1,3,8,8,128]{4,3,2,1,0:T(8,128)(2,1)} %param.14) | copy-start | bytes 147460
  32.6 5.4 %copy-start.31 = (s32[288]{0:T(512)S(1)}, s32[288]{0:T(512)}, u32[]{:S(2)}) copy-start(s32[288]{0:T(512)} %copy-done.30) | copy-start | bytes 3460
  32.6 5.4 %collective-permute-start = (bf16[8,3,4,2,16,128]{5,4,3,2,1,0:T(8,128)(2,1)}, bf16[8,3,4,2,16,128]{5,4,3,2,1,0:T(8,128)(2,1)S(1)}, u32[]{:S(2)}, u32[]{:S(2)}) collective-permute-start(bf16[8,3,4,2,16,128]{5,4,3,2,1,0:T(8,128)(2,1)} %shard_map.129), channel_id=1, source_target_pairs={{0,16},{16,0},{1,17},{17,1},{2,18},{18,2},{3,19},{19,3},{4,20},{20... | collective-permute-start | bytes 2359304 | tf_op jit(solution)/shard_map/ppermute | solution.py:24
  38.0 1.1 copy-start.3
  39.2 1.0 copy-start.7
  40.1 0.9 copy-start.11
  41.0 0.9 copy-start.13
  41.9 0.9 copy-start.15
  42.8 0.9 copy-start.17
  43.8 0.9 copy-start.22
  51.1 3.2 %copy-start.18 = (f32[768,128]{1,0:T(8,128)}, f32[768,128]{1,0:T(8,128)S(1)}, u32[]{:S(2)}) copy-start(f32[768,128]{1,0:T(8,128)S(1)} %get-tuple-element.29.pre_ref) | copy-start | bytes 1179652
  51.1 3.2 %copy-start.20 = (f32[768,128]{1,0:T(8,128)}, f32[768,128]{1,0:T(8,128)S(1)}, u32[]{:S(2)}) copy-start(f32[768,128]{1,0:T(8,128)S(1)} %get-tuple-element.30.inner_ref) | copy-start | bytes 1179652
  51.1 3.2 %copy-start.25 = (f32[192,128]{1,0:T(8,128)}, f32[192,128]{1,0:T(8,128)S(1)}, u32[]{:S(2)}) copy-start(f32[192,128]{1,0:T(8,128)S(1)} %get-tuple-element.31.strip_pre_ref) | copy-start | bytes 294916
  51.1 3.2 %copy-start.27 = (f32[192,128]{1,0:T(8,128)}, f32[192,128]{1,0:T(8,128)S(1)}, u32[]{:S(2)}) copy-start(f32[192,128]{1,0:T(8,128)S(1)} %get-tuple-element.32.sent_ref) | copy-start | bytes 294916
  51.1 11.3 %copy-start.23 = (bf16[3,4,2,16,128]{4,3,2,1,0:T(8,128)(2,1)}, bf16[3,4,2,16,128]{4,3,2,1,0:T(8,128)(2,1)S(1)}, u32[]{:S(2)}) copy-start(bf16[3,4,2,16,128]{4,3,2,1,0:T(8,128)(2,1)S(1)} %get-tuple-element.25.own_ref) | copy-start | bytes 294916
  51.2 2.3 %collective-permute-start.1 = (f32[1408,128]{1,0:T(8,128)S(1)}, f32[1408,128]{1,0:T(8,128)S(1)}, u32[]{:S(2)}, u32[]{:S(2)}) collective-permute-start(f32[1408,128]{1,0:T(8,128)S(1)} %slice_bitcast_fusion), channel_id=1, source_target_pairs={{0,16},{16,0},{1,17},{17,1},{2,18},{18,2},{3,19},{19,3},{4,20},{20... | collective-permute-start | bytes 2162696 | tf_op jit(solution)/shard_map/ppermute | solution.py:24
  54.3 17.0 %all-to-all-start.1 = ((bf16[16,88,128]{2,1,0:T(8,128)(2,1)}), bf16[16,88,128]{2,1,0:T(8,128)(2,1)S(1)}, u32[]{:S(2)}, u32[]{:S(2)}) async-start(bf16[16,88,128]{2,1,0:T(8,128)(2,1)} %bitcast.38), calls=%async_computation.1 | async-start | bytes 720896 | tf_op jit(solution)/shard_map/all_to_all | solution.py:541
  62.4 7.5 %collective-permute-start.2 = (bf16[3,4,2,16,128]{4,3,2,1,0:T(8,128)(2,1)S(1)}, bf16[3,4,2,16,128]{4,3,2,1,0:T(8,128)(2,1)S(1)}, u32[]{:S(2)}, u32[]{:S(2)}) collective-permute-start(bf16[3,4,2,16,128]{4,3,2,1,0:T(8,128)(2,1)S(1)} %get-tuple-element.25.own_ref), channel_id=1, source_target_pairs={{0,32},{32,0},{1,33},{33,1},{2,34},{34,2},{3,35},{35,3},{4,36},{36... | collective-permute-start | bytes 294920 | tf_op jit(solution)/shard_map/ppermute | solution.py:35
  71.3 0.9 copy-start.24
  73.0 17.7 %all-to-all-start.2 = ((f32[8,88,128]{2,1,0:T(8,128)}), f32[8,88,128]{2,1,0:T(8,128)S(1)}, u32[]{:S(2)}, u32[]{:S(2)}) async-start(f32[8,88,128]{2,1,0:T(8,128)} %get-tuple-element.26), calls=%async_computation.2 | async-start | bytes 720896 | tf_op jit(solution)/shard_map/all_to_all | solution.py:551
  78.4 34.4 %copy-start.6 = (bf16[48,8,4,128]{3,1,2,0:T(8,128)(2,1)S(1)}, bf16[48,8,4,128]{3,1,2,0:T(8,128)(2,1)}, u32[]{:S(2)}) copy-start(bf16[48,8,4,128]{3,1,2,0:T(8,128)(2,1)} %copy.45) | copy-start | bytes 1179652
  78.5 34.4 %copy-start.8 = (bf16[3,3,128,128]{3,2,1,0:T(8,128)(2,1)S(1)}, bf16[3,3,128,128]{3,2,1,0:T(8,128)(2,1)}, u32[]{:S(2)}) copy-start(bf16[3,3,128,128]{3,2,1,0:T(8,128)(2,1)} %copy.26) | copy-start | bytes 884740
  78.5 34.4 %copy-start.14 = (bf16[192,192]{1,0:T(8,128)(2,1)S(1)}, bf16[192,192]{1,0:T(8,128)(2,1)}, u32[]{:S(2)}) copy-start(bf16[192,192]{1,0:T(8,128)(2,1)} %copy-done.12) | copy-start | bytes 221188
  78.5 34.4 %copy-start.19 = (f32[768,128]{1,0:T(8,128)S(1)}, f32[768,128]{1,0:T(8,128)}, u32[]{:S(2)}) copy-start(f32[768,128]{1,0:T(8,128)} %copy-done.18) | copy-start | bytes 1179652
  78.5 34.4 %copy-start.21 = (f32[768,128]{1,0:T(8,128)S(1)}, f32[768,128]{1,0:T(8,128)}, u32[]{:S(2)}) copy-start(f32[768,128]{1,0:T(8,128)} %copy-done.20) | copy-start | bytes 1179652
  78.5 10.5 %collective-permute-start.5 = (bf16[2,3,4,2,16,128]{5,4,3,2,1,0:T(8,128)(2,1)S(1)}, bf16[2,3,4,2,16,128]{5,4,3,2,1,0:T(8,128)(2,1)S(1)}, u32[]{:S(2)}, u32[]{:S(2)}) collective-permute-start(bf16[2,3,4,2,16,128]{5,4,3,2,1,0:T(8,128)(2,1)S(1)} %get-tuple-element.27.own_ref), channel_id=1, source_target_pairs={{0,192},{64,128},{128,64},{192,0},{1,193},{65,129},{129,65},{193,1... | collective-permute-start | bytes 589832 | tf_op jit(solution)/shard_map/ppermute | solution.py:35
  80.9 8.0 %collective-permute-start.4 = (bf16[2,3,4,2,16,128]{5,4,3,2,1,0:T(8,128)(2,1)S(1)}, bf16[2,3,4,2,16,128]{5,4,3,2,1,0:T(8,128)(2,1)S(1)}, u32[]{:S(2)}, u32[]{:S(2)}) collective-permute-start(bf16[2,3,4,2,16,128]{5,4,3,2,1,0:T(8,128)(2,1)S(1)} %get-tuple-element.27.own_ref), channel_id=1, source_target_pairs={{0,128},{64,192},{128,0},{192,64},{1,129},{65,193},{129,1},{193,65... | collective-permute-start | bytes 589832 | tf_op jit(solution)/shard_map/ppermute | solution.py:35
  81.5 8.0 %collective-permute-start.3 = (bf16[2,3,4,2,16,128]{5,4,3,2,1,0:T(8,128)(2,1)S(1)}, bf16[2,3,4,2,16,128]{5,4,3,2,1,0:T(8,128)(2,1)S(1)}, u32[]{:S(2)}, u32[]{:S(2)}) collective-permute-start(bf16[2,3,4,2,16,128]{5,4,3,2,1,0:T(8,128)(2,1)S(1)} %get-tuple-element.27.own_ref), channel_id=1, source_target_pairs={{0,64},{64,0},{128,192},{192,128},{1,65},{65,1},{129,193},{193,129... | collective-permute-start | bytes 589832 | tf_op jit(solution)/shard_map/ppermute | solution.py:35
  90.6 22.3 %copy-start.26 = (f32[192,128]{1,0:T(8,128)S(1)}, f32[192,128]{1,0:T(8,128)}, u32[]{:S(2)}) copy-start(f32[192,128]{1,0:T(8,128)} %copy-done.25) | copy-start | bytes 294916
  90.6 22.3 %copy-start.28 = (f32[192,128]{1,0:T(8,128)S(1)}, f32[192,128]{1,0:T(8,128)}, u32[]{:S(2)}) copy-start(f32[192,128]{1,0:T(8,128)} %copy-done.27) | copy-start | bytes 294916
  90.7 22.1 %collective-permute-start.6 = (bf16[4,2,3,4,2,16,128]{6,5,4,3,2,1,0:T(8,128)(2,1)S(1)}, bf16[4,2,3,4,2,16,128]{6,5,4,3,2,1,0:T(8,128)(2,1)S(1)}, u32[]{:S(2)}, u32[]{:S(2)}) collective-permute-start(bf16[4,2,3,4,2,16,128]{6,5,4,3,2,1,0:T(8,128)(2,1)S(1)} %get-tuple-element.28), channel_id=1, source_target_pairs={{0,16},{16,0},{1,17},{17,1},{2,18},{18,2},{3,19},{19,3},{4,20},{20... | collective-permute-start | bytes 2359304 | tf_op jit(solution)/shard_map/ppermute | solution.py:24
  108.6 2.9 %collective-permute-start.7 = (bf16[1408,128]{1,0:T(8,128)(2,1)S(1)}, bf16[1408,128]{1,0:T(8,128)(2,1)S(1)}, u32[]{:S(2)}, u32[]{:S(2)}) collective-permute-start(bf16[1408,128]{1,0:T(8,128)(2,1)S(1)} %bitcast.107), channel_id=1, source_target_pairs={{0,16},{16,0},{1,17},{17,1},{2,18},{18,2},{3,19},{19,3},{4,20},{20... | collective-permute-start | bytes 1081352 | tf_op jit(solution)/shard_map/ppermute | solution.py:24

commit v3 on v2

v3 whole, which is shorter than its diff:
```python
import functools
import math

import jax
import jax.numpy as jnp
from jax import lax
from jax.experimental import pallas as pl
from jax.experimental.pallas import tpu as pltpu
from jax.sharding import Mesh
from jax.sharding import PartitionSpec as P

PLANE = ("x", "y")
DEPTH = ("z", "w")
SLOPE = math.sqrt(2.0 / math.pi)
CUBIC = 0.044715
BF16 = jnp.bfloat16
F32 = jnp.float32
EDGE = 16
CH = 128


def swap_core(block):
    return lax.ppermute(block, "c", [(0, 1), (1, 0)])


def swap_apart(block, axis, apart):
    number = lax.axis_size(axis)
    return lax.ppermute(block, axis, [(i, i ^ apart) for i in range(number)])


def fetch(sources, targets, sems):
    copies = []
    for at, (source, target) in enumerate(zip(sources, targets)):
        copies.append(pltpu.make_async_copy(source, target, sems.at[at]))
        copies[-1].start()
    return copies


def finish(copies):
    for copy in copies:
        copy.wait()


def gelu(v):
    return 0.5 * v * (1.0 + jnp.tanh(SLOPE * (v + CUBIC * v * v * v)))


def gelu_slope(v):
    t = jnp.tanh(SLOPE * (v + CUBIC * v * v * v))
    return 0.5 * (1.0 + t) + (0.5 * SLOPE) * v * (1.0 - t * t) * (1.0 + (3.0 * CUBIC) * v * v)


def dot(left, right):
    return jnp.dot(left, right, preferred_element_type=F32)


def dot_rows(left, right):
    return lax.dot_general(left, right, (((0,), (0,)), ((), ())), preferred_element_type=F32)


def turned(turn, rows):
    high = rows.astype(BF16)
    low = (rows - high.astype(F32)).astype(BF16)
    return dot(turn, high) + dot(turn, low)


def as_rows(block):
    return block.reshape(-1, CH)


def lanes(at, count=1):
    return slice(at * CH, (at + count) * CH)


def strip(n):
    return slice(n * EDGE, (n + 1) * EDGE)


def as_cells(rows):
    return rows.reshape(-1, EDGE, EDGE, CH)


def fill_pad(pad_ref, rows):
    pad_ref[:, 1 : EDGE + 1, 1 : EDGE + 1, :] = as_cells(rows)


def windows(pad_ref, cols_ref):
    for a in range(3):
        for b in range(3):
            part = pad_ref[:, a : a + EDGE, b : b + EDGE, :].astype(BF16)
            cols_ref[:, lanes(3 * a + b)] = as_rows(part)


def triples(line_ref, cols_ref, order):
    for at, start in enumerate(order):
        part = line_ref[:, start : start + EDGE, :].astype(BF16)
        cols_ref[0 : line_ref.shape[0] * EDGE, lanes(at)] = as_rows(part)


def pick(rows_ref, at, count, side):
    chosen = pl.ds(pl.multiple_of(side * CH, CH), CH)
    return rows_ref[pl.ds(at, count), chosen]


def side_cells(tile, side, depth=0):
    near = (depth, EDGE - 1 - depth)[side in (1, 2)]
    if side % 2 == 0:
        return pl.ds(tile * EDGE * EDGE + near * EDGE, EDGE)
    return pl.ds(tile * EDGE * EDGE + near, EDGE, EDGE)


def add_sides(cells_ref, rows):
    for n in range(12):
        cells = side_cells(n % 3, n // 3)
        cells_ref[cells, :] = cells_ref[cells, :] + rows[strip(n)]


def put_seams(pad_ref, rows):
    for n in range(12):
        side, k = n // 3, n % 3
        place = (0, EDGE + 1, EDGE + 1, 0)[side]
        seam = rows[strip(n)]
        if side % 2 == 0:
            pad_ref[k, place, 1 : EDGE + 1, :] = seam
        else:
            for i in range(EDGE):
                pad_ref[k, 1 + i, place : place + 1, :] = seam[i : i + 1]


def near_at(n):
    return 8 * n


def lateral_at(j):
    return 96 + 8 * j


def frame_source(side, r, k):
    return ((r, k), (k, 2 - r), (2 - r, k), (k, r))[side]


def ring_kernel(x_ref, ring_ref, cells_ref):
    cells_ref[...] = as_rows(x_ref[...]).astype(F32)
    for n in range(12):
        for depth in range(2):
            rows = cells_ref[side_cells(n % 3, n // 3, depth), :].astype(BF16)
            ring_ref[n % 3, n // 3, depth] = rows


W1_SIDES, W2, TAIL, X = (slice(0, 512), slice(512, 640), slice(640, 768), slice(768, 896))
W2_BACK, W1_BACK, ADJOINT = slice(0, 128), slice(128, 256), slice(256, 768)


def stage_kernel(
    near_ref, code_ref, slot_ref, x_hbm, skip_hbm, down_hbm, w1_hbm, w2_hbm, wc_hbm,
    index_ref, turn_hbm, early_hbm, late_hbm, cells_hbm,
    x_ref, skip_ref, down_ref, w1_ref, w2_ref, wc_ref,
    turn_ref, early_ref, late_ref, cells_ref,
    pad_ref, cot_ref, cols_ref, wc_back_ref, in_sems, out_sems,
):
    arrivals = fetch(
        (w1_hbm, w2_hbm, wc_hbm, x_hbm, down_hbm, skip_hbm),
        (w1_ref, w2_ref, wc_ref, x_ref, down_ref, skip_ref),
        in_sems,
    )
    pad_ref[...] = jnp.zeros_like(pad_ref)
    early_ref[704:, TAIL] = jnp.zeros_like(early_ref[704:, TAIL])
    early_ref[768:, X] = jnp.zeros_like(early_ref[768:, X])
    total = slot_ref.shape[0]
    tiles = 3
    core = lax.axis_index("c")
    at_y = lax.axis_index("y")
    at_z = lax.axis_index("z")
    first = ((at_y * 2 + at_z) * 2 + core) * tiles

    def look(i, found):
        here = slot_ref[i]
        return tuple(jnp.where(here == first + k, i, found[k]) for k in range(tiles))

    own = lax.fori_loop(0, total, look, (jnp.int32(0),) * tiles)

    def place(at, tile):
        slot = slot_ref[tile]
        owner = slot // tiles
        local = slot % tiles
        chip = ((owner // 4) ^ at_y) * 2 + ((owner // 2) % 2 ^ at_z)
        index_ref[at] = (owner + core) % 2
        index_ref[at + 1] = chip * tiles + local

    column = lax.broadcasted_iota(jnp.int32, (EDGE, 12 * EDGE), 1)
    row = lax.broadcasted_iota(jnp.int32, (EDGE, 12 * EDGE), 0)
    for n in range(12):
        side, k = n // tiles, n % tiles
        near = near_ref[side, own[k]]
        code = code_ref[side, own[k]]
        near_side = code // 2
        reverse = code % 2
        place(near_at(n), near)
        index_ref[near_at(n) + 2] = near_side
        source = jnp.where(reverse == 1, EDGE - 1 - row, row) + n * EDGE
        turn_ref[strip(n), :] = jnp.where(column == source, 1.0, 0.0).astype(F32).astype(BF16)
        upright = near_side % 2
        far = jnp.where((near_side == 1) | (near_side == 2), 1, 0)
        for h in range(2):
            lateral = jnp.where(upright == 1, (0, 2)[h], (3, 1)[h])
            at = lateral_at(2 * n + h)
            place(at, near_ref[lateral, near])
            lateral_code = code_ref[lateral, near]
            index_ref[at + 2] = lateral_code // 2
            index_ref[at + 3] = (far + lateral_code) % 2

    finish(arrivals)

    def flip(block):
        return jnp.transpose(block.astype(F32)).astype(BF16)

    for a in range(3):
        for b in range(3):
            block = w1_ref[lanes(3 * a + b), :]
            first_flip = flip(block)
            second_flip = flip(w2_ref[lanes(3 * a + b), :])
            back = lanes(8 - 3 * a - b)
            late_ref[back, W1_BACK] = first_flip
            late_ref[back, W2_BACK] = second_flip
            for side in range(4):
                for r in range(3):
                    for k in range(3):
                        if frame_source(side, r, k) != (a, b):
                            continue
                        early_ref[lanes(3 * r + k), lanes(side)] = block
                        if r == 0:
                            late_ref[lanes(6 + k), lanes(2 + side)] = first_flip
                        if r <= 1:
                            late_ref[lanes(3 * r + k), lanes(2 + side)] = second_flip
    early_ref[:, W2] = w2_ref[...]
    early_ref[:512, TAIL] = wc_ref[...]
    down = down_ref[...]
    early_ref[512:704, TAIL] = down
    x_rows = as_rows(x_ref[...])
    early_ref[:768, X] = x_rows
    departures = fetch(
        (early_ref, late_ref, turn_ref), (early_hbm, late_hbm, turn_hbm), out_sems
    )
    for at in range(4):
        wc_back_ref[:, lanes(at)] = flip(wc_ref[lanes(at), :])
    spread_down = dot(down, wc_back_ref[...])
    half = EDGE // 2
    for a in range(2):
        for b in range(2):
            part = spread_down[:, lanes(2 * a + b)].reshape(tiles, half, half, CH)
            cot_ref[:, pl.ds(a, half, 2), pl.ds(b, half, 2), :] = part
    cells_ref[:, lanes(1)] = as_rows(cot_ref[...] + skip_ref[...].astype(F32))
    fill_pad(pad_ref, x_rows.astype(F32))
    windows(pad_ref, cols_ref)
    cells_ref[:, lanes(0)] = dot(cols_ref[...], w1_ref[...])
    last = pltpu.make_async_copy(cells_ref, cells_hbm, out_sems.at[3])
    last.start()
    finish(departures + [last])


def table_row(mine_ref, other_ref, index_ref, at, depth):
    slot = index_ref[at + 1]
    side = index_ref[at + 2]
    mine = mine_ref[slot, side, depth]
    other = other_ref[slot, side, depth]
    return jnp.where(index_ref[at] == 0, mine.astype(F32), other.astype(F32))


def end_rows(mine_ref, other_ref, index_ref, j):
    row = table_row(mine_ref, other_ref, index_ref, lateral_at(j), 0)
    far = index_ref[lateral_at(j) + 3] == 1
    last = EDGE - 1
    return far, jnp.where(far, row[last:], row[:1]), jnp.where(far, row[last - 1 : last], row[1:2])


def forward_kernel(
    index_ref, turn_ref, mine_ref, other_ref, early_ref, staged_ref,
    coarse_ref, delta_ring_ref, pre_ref, strip_pre_ref, seam_ref, cols2_ref, strip_ref,
    down_cols_ref, delta_ref, line_ref,
    pad_ref, patch_ref, wide_ref, fine_ref, cells_ref, line_cols_ref,
):
    tiles = 3
    patch_ref[...] = jnp.zeros_like(patch_ref)
    pad_ref[...] = jnp.zeros_like(pad_ref)
    line_ref[...] = jnp.zeros_like(line_ref)
    turn = turn_ref[...]
    near = []
    own = []
    for n in range(12):
        own.append(mine_ref[n % tiles, n // tiles, 0])
        edge = table_row(mine_ref, other_ref, index_ref, near_at(n), 0)
        near.append(edge)
        patch_ref[n, 1, 1 : EDGE + 1, :] = edge
        patch_ref[n, 2, 1 : EDGE + 1, :] = table_row(
            mine_ref, other_ref, index_ref, near_at(n), 1
        )
        for h in range(2):
            _, outer, inner = end_rows(mine_ref, other_ref, index_ref, 2 * n + h)
            at = (0, EDGE + 1)[h]
            patch_ref[n, 1, at : at + 1, :] = outer
            patch_ref[n, 2, at : at + 1, :] = inner
    seams = dot(turn, jnp.concatenate(near, axis=0).astype(BF16))
    seam_ref[...] = seams
    own_turned = dot(turn, jnp.concatenate(own, axis=0))
    patch_ref[:, 0, 1 : EDGE + 1, :] = own_turned.reshape(12, EDGE, CH)
    for r in range(3):
        for b in range(3):
            part = patch_ref[:, r, b : b + EDGE, :].astype(BF16)
            strip_ref[:, lanes(3 * r + b)] = as_rows(part)
    wide_ref[...] = dot(strip_ref[...], early_ref[:, W1_SIDES])
    for n in range(12):
        strip_pre_ref[strip(n), :] = pick(wide_ref, n * EDGE, EDGE, index_ref[near_at(n) + 2])
    line_ref[:, 1 : EDGE + 1, :] = seams.reshape(12, EDGE, CH)
    triples(line_ref, line_cols_ref, (0, 1, 2))
    pre_ref[...] = staged_ref[:, lanes(0)]
    parts = []
    for side in range(4):
        rows = slice(side * tiles * EDGE, (side + 1) * tiles * EDGE)
        parts.append(dot(line_cols_ref[rows, :], early_ref[: 3 * CH, lanes(side)]))
    add_sides(pre_ref, jnp.concatenate(parts, axis=0))
    fill_pad(pad_ref, gelu(pre_ref[...]).astype(BF16).astype(F32))
    put_seams(pad_ref, dot(turn, gelu(strip_pre_ref[...]).astype(BF16)))
    windows(pad_ref, cols2_ref)
    second_pre = dot(cols2_ref[...], early_ref[:, W2])
    delta = (gelu_slope(second_pre) * staged_ref[:, lanes(1)]).astype(BF16)
    delta_ref[...] = delta
    cells_ref[...] = delta.astype(F32)
    for n in range(12):
        for depth in range(2):
            rows = cells_ref[side_cells(n % tiles, n // tiles, depth), :]
            delta_ring_ref[n % tiles, n // tiles, depth] = rows.astype(BF16)
            if depth == 0:
                line_ref[n, 1 : EDGE + 1, :] = rows
    fine_ref[...] = as_cells(gelu(second_pre).astype(BF16).astype(F32))
    half = EDGE // 2
    for a in range(2):
        for b in range(2):
            part = fine_ref[:, pl.ds(a, half, 2), pl.ds(b, half, 2), :]
            down_cols_ref[:, lanes(2 * a + b)] = as_rows(part).astype(BF16)
    coarse_ref[...] = dot(down_cols_ref[...], early_ref[:512, TAIL]).astype(BF16)


def gradient_kernel(
    index_ref, turn_ref, early_ref, late_ref, pre_ref, strip_pre_ref, seam_ref, cols2_ref, strip_ref, down_cols_ref, delta_ref, line_ref,
    grad_ref, rest_ref,
    pad_ref, cols_ref, cols3_ref, split_ref, line_cols_ref,
):
    tiles = 3
    core = lax.axis_index("c")

    def put_grad(at, block):
        half = at // 11
        grad_ref[jnp.where(core == half, 0, 1), lanes(at % 11), :] = block

    split_ref[...] = jnp.zeros_like(split_ref)
    turn = turn_ref[...]
    down_grad = dot_rows(down_cols_ref[...], early_ref[512:704, TAIL])
    for at in range(4):
        put_grad(18 + at, down_grad[lanes(at)])
    delta = delta_ref[...]
    second_grad = dot_rows(cols2_ref[...], delta)
    for at in range(9):
        put_grad(9 + at, second_grad[lanes(at)])
    pad_ref[...] = jnp.zeros_like(pad_ref)
    fill_pad(pad_ref, delta.astype(F32))
    windows(pad_ref, cols3_ref)
    inner = dot(cols3_ref[...], late_ref[:, W2_BACK])
    rest_ref[:768, lanes(0)] = pre_ref[...]
    rest_ref[:768, lanes(1)] = inner
    inner_delta = (gelu_slope(pre_ref[...]) * inner).astype(BF16)
    triples(line_ref, line_cols_ref, (2, 1, 0))
    rims = []
    for side in range(4):
        rows = slice(side * tiles * EDGE, (side + 1) * tiles * EDGE)
        rims.append(dot(line_cols_ref[rows, :], late_ref[: 3 * CH, lanes(2 + side)]))
    sent = turned(turn, jnp.concatenate(rims, axis=0))
    rest_ref[768:, lanes(0)] = strip_pre_ref[...]
    rest_ref[768:, lanes(1)] = sent
    sent_delta = (gelu_slope(strip_pre_ref[...]) * sent).astype(BF16)
    for n in range(12):
        chosen = pl.ds(pl.multiple_of(index_ref[near_at(n) + 2] * CH, CH), CH)
        split_ref[strip(n), chosen] = sent_delta[strip(n)]
    sent_grad = dot_rows(strip_ref[...], split_ref[...])
    fill_pad(pad_ref, early_ref[:768, X].astype(F32))
    put_seams(pad_ref, seam_ref[...])
    windows(pad_ref, cols_ref)
    first_grad = dot_rows(cols_ref[...], inner_delta)
    for a in range(3):
        for b in range(3):
            block = first_grad[lanes(3 * a + b)]
            for side in range(4):
                for r in range(3):
                    for k in range(3):
                        if frame_source(side, r, k) == (a, b):
                            block = block + sent_grad[lanes(3 * r + k), lanes(side)]
            put_grad(3 * a + b, block)


def backward_kernel(
    index_ref, turn_ref, mine_ref, other_ref, late_ref, rest_ref,
    out_ref, flag_ref,
    pad_ref, cols_ref, line_ref, deep_ref, line_cols_ref, deep_cols_ref, ends_ref, wide_ref,
    strip_wide_ref, cot_ref, cells_ref,
):
    flag_ref[...] = jnp.zeros_like(flag_ref)
    turn = turn_ref[...]
    line_ref[...] = jnp.zeros_like(line_ref)
    deep_ref[...] = jnp.zeros_like(deep_ref)
    ends_ref[...] = jnp.zeros_like(ends_ref)
    pad_ref[...] = jnp.zeros_like(pad_ref)
    for n in range(12):
        for depth, rows_ref in ((0, line_ref), (1, deep_ref)):
            rows_ref[n, 1 : EDGE + 1, :] = table_row(
                mine_ref, other_ref, index_ref, near_at(n), depth
            )
    for j in range(24):
        far, outer, inner = end_rows(mine_ref, other_ref, index_ref, j)
        blank = jnp.zeros_like(inner)
        ends_ref[j : j + 1, lanes(0)] = jnp.where(far, blank, inner)
        ends_ref[j : j + 1, lanes(1)] = outer
        ends_ref[j : j + 1, lanes(2)] = jnp.where(far, inner, blank)
    strip_rows = 12 * EDGE
    triples(line_ref, line_cols_ref, (2, 1, 0))
    line_cols_ref[strip_rows:, :] = ends_ref[...].astype(BF16)
    triples(deep_ref, deep_cols_ref, (2, 1, 0))
    wide_ref[...] = dot(line_cols_ref[...], late_ref[: 3 * CH, ADJOINT])
    strip_wide_ref[...] = dot(deep_cols_ref[...], late_ref[: 3 * CH, ADJOINT]) + dot(
        line_cols_ref[:strip_rows, :], late_ref[3 * CH : 6 * CH, ADJOINT]
    )
    cot_ref[...] = rest_ref[768:, lanes(1)]
    rims = []
    for n in range(12):
        side = index_ref[near_at(n) + 2]
        rims.append(pick(wide_ref, n * EDGE, EDGE, side))
        cot_ref[strip(n), :] += pick(strip_wide_ref, n * EDGE, EDGE, side)
        for h in range(2):
            j = 2 * n + h
            at = n * EDGE + (0, EDGE - 1)[h]
            cot_ref[at : at + 1, :] += pick(
                wide_ref, strip_rows + j, 1, index_ref[lateral_at(j) + 2]
            )
    cells_ref[...] = rest_ref[:768, lanes(1)]
    add_sides(cells_ref, turned(turn, jnp.concatenate(rims, axis=0)))
    delta = gelu_slope(rest_ref[:768, lanes(0)]) * cells_ref[...]
    fill_pad(pad_ref, delta.astype(BF16).astype(F32))
    windows(pad_ref, cols_ref)
    strip_delta = (gelu_slope(rest_ref[768:, lanes(0)]) * cot_ref[...]).astype(BF16).astype(F32)
    line_ref[:, 1 : EDGE + 1, :] = strip_delta.reshape(12, EDGE, CH)
    triples(line_ref, deep_cols_ref, (2, 1, 0))
    strip_wide_ref[...] = dot(deep_cols_ref[...], late_ref[6 * CH :, ADJOINT])
    rims = []
    for n in range(12):
        rims.append(pick(strip_wide_ref, n * EDGE, EDGE, index_ref[near_at(n) + 2]))
    cells_ref[...] = dot(cols_ref[...], late_ref[:, W1_BACK])
    add_sides(cells_ref, turned(turn, jnp.concatenate(rims, axis=0)))
    out_ref[...] = as_cells(cells_ref[...]).astype(BF16)


def first_pair_kernel(own_ref, across_ref, pair_ref):
    pair_ref[0] = own_ref[...]
    pair_ref[1] = across_ref[...]


def first_table_kernel(own_ref, one_ref, two_ref, three_ref, index_ref, table_ref):
    for at, part_ref in enumerate((own_ref, one_ref, two_ref, three_ref)):
        table_ref[at] = part_ref[...]


def pair_kernel(own_ref, across_ref, grads_ref, pair_ref, give_ref):
    pair_ref[0] = own_ref[...]
    pair_ref[1] = across_ref[...]
    give_ref[...] = grads_ref[1]


def table_kernel(own_ref, one_ref, two_ref, three_ref, table_ref):
    for at, part_ref in enumerate((own_ref, one_ref, two_ref, three_ref)):
        table_ref[at] = part_ref[...]


def spread_sum(pieces_ref, copies_ref):
    total = jnp.sum(pieces_ref[...].astype(F32), axis=0).astype(BF16)
    for at in range(copies_ref.shape[0]):
        copies_ref[at] = total


def first_sum_kernel(pieces_ref, table_ref, copies_ref, out_ref):
    spread_sum(pieces_ref, copies_ref)
    out_ref[...] = table_ref[...]


def second_sum_kernel(pieces_ref, flag_ref, copies_ref):
    spread_sum(pieces_ref, copies_ref)


def finish_kernel(scale, mine_ref, other_ref, first_ref, second_ref, down_ref):
    core = lax.axis_index("c")
    for at in range(22):
        half = at // 11
        rows = slice(at % 11 * CH, (at % 11 + 1) * CH)
        block = jnp.where(core == half, mine_ref[rows, :], other_ref[rows, :])
        out_ref, base = ((first_ref, 0), (second_ref, 9), (down_ref, 18))[at // 9]
        out_ref[at - base] = block.astype(F32) * scale


def whole(space):
    return pl.BlockSpec(memory_space=space)


def shards(
    activations,
    conv1_weight,
    conv2_weight,
    coarse_kernel_weight,
    skip_cotangent,
    down_cotangent,
    face_neighbours,
    seam_codes,
    tile_slots,
):
    x = activations[0]
    tiles = x.shape[0]
    total_tiles = tile_slots.shape[0]
    cells = tiles * EDGE * EDGE
    strips = 4 * tiles * EDGE
    half = EDGE // 2
    quarter = tiles * half * half
    smem, vmem, hbm = whole(pltpu.SMEM), whole(pltpu.VMEM), whole(pltpu.HBM)
    shape = jax.ShapeDtypeStruct
    plane = lax.axis_size(PLANE)
    deep = lax.axis_size(DEPTH)
    pad = shape((tiles, EDGE + 2, EDGE + 8, CH), F32)
    line = shape((4 * tiles, EDGE + 8, CH), F32)
    ring = shape((tiles, 4, 2, EDGE, CH), BF16)

    def call(
        kernel, outs, operands, scratch=(), sems=(), specs=None, out_specs=None, cost=1, room=24
    ):
        single = not isinstance(outs, tuple)
        scratch = [pltpu.VMEM(one.shape, one.dtype) for one in scratch]
        scratch += [pltpu.SemaphoreType.DMA((count,)) for count in sems]
        return pl.pallas_call(
            kernel,
            out_shape=outs,
            in_specs=specs or [vmem] * len(operands),
            out_specs=out_specs or (vmem if single else (vmem,) * len(outs)),
            scratch_shapes=scratch,
            compiler_params=pltpu.CompilerParams(vmem_limit_bytes=room * 1024 * 1024),
            cost_estimate=pl.CostEstimate(
                flops=cost * cells * 18 * CH * CH, bytes_accessed=2 * 1024 * 1024, transcendentals=0
            ),
        )(*operands)

    wide = shape((strips, 4 * CH), F32)
    all_cols = shape((cells, 9 * CH), BF16)
    cell_rows = shape((cells, CH), F32)
    strip_rows = shape((strips, CH), F32)
    flag = shape((8, CH), F32)
    own_ring = call(ring_kernel, ring, [x], [cell_rows])
    across = swap_apart(own_ring, "z", 1)
    operands = [
        x,
        skip_cotangent[0],
        down_cotangent.reshape(-1, CH),
        conv1_weight.reshape(9 * CH, CH),
        conv2_weight.reshape(9 * CH, CH),
        coarse_kernel_weight.reshape(4 * CH, CH),
    ]
    staged = (
        shape((strips, strips), BF16),
        shape((9 * CH, 7 * CH), BF16),
        shape((9 * CH, 6 * CH), BF16),
        shape((cells, 2 * CH), F32),
    )
    index, turn, early, late, staged_cells = call(
        stage_kernel,
        (shape((296,), jnp.int32),) + staged,
        [face_neighbours.T, seam_codes.T, tile_slots] + operands,
        tuple(operands) + staged
        + (pad, shape(x.shape, F32), all_cols, shape((CH, 4 * CH), BF16)),
        (len(operands), len(staged)),
        specs=[smem] * 3 + [hbm] * 6,
        out_specs=(smem,) + (hbm,) * 4,
        cost=4,
        room=60,
    )
    pair = call(first_pair_kernel, shape((2,) + ring.shape, BF16), [own_ring, across])
    along = [swap_apart(pair, "y", apart) for apart in (1, 2, 3)]
    mine = call(
        first_table_kernel,
        shape((4,) + pair.shape, BF16),
        [pair] + along + [index],
        specs=[vmem] * 4 + [smem],
    )
    other = swap_core(mine)

    def table(block):
        return block.reshape((-1,) + ring.shape[1:])

    (
        coarse, delta_ring, pre, strip_pre, seam, cols2, strip_cols, down_cols, delta, line_rows,
    ) = call(
        forward_kernel,
        (
            shape((quarter, CH), BF16),
            ring,
            cell_rows,
            strip_rows,
            strip_rows,
            all_cols,
            shape((strips, 9 * CH), BF16),
            shape((quarter, 4 * CH), BF16),
            shape((cells, CH), BF16),
            line,
        ),
        [index, turn, table(mine), table(other), early, staged_cells],
        [
            pad,
            shape((4 * tiles, 3, EDGE + 8, CH), F32),
            wide,
            shape(x.shape, F32),
            cell_rows,
            shape((strips, 3 * CH), BF16),
        ],
        specs=[smem] + [vmem] * 5,
        cost=2,
    )
    across = swap_apart(delta_ring, "z", 1)
    grads, rest = call(
        gradient_kernel,
        (shape((2, 11 * CH, CH), F32), shape((cells + strips, 2 * CH), F32)),
        [
            index, turn, early, late, pre, strip_pre, seam, cols2, strip_cols, down_cols, delta,
            line_rows,
        ],
        [
            pad,
            all_cols,
            all_cols,
            shape((strips, 4 * CH), BF16),
            shape((strips, 3 * CH), BF16),
        ],
        specs=[smem] + [vmem] * 11,
        cost=4,
    )
    pair, give = call(
        pair_kernel,
        (shape((2,) + ring.shape, BF16), shape(grads.shape[1:], F32)),
        [delta_ring, across, grads],
    )
    kept = (grads[0] + swap_core(give)).astype(BF16)
    along = [swap_apart(pair, "y", apart) for apart in (1, 2, 3)]
    part = kept.shape[0] // plane
    pieces = lax.all_to_all(kept.reshape(plane, part, CH), PLANE, 0, 0)
    mine = call(table_kernel, shape((4,) + pair.shape, BF16), [pair] + along, cost=100)
    copies, mine = call(
        first_sum_kernel,
        (shape((deep, part, CH), BF16), shape(mine.shape, BF16)),
        [pieces, mine],
    )
    other = swap_core(mine)
    pieces = lax.all_to_all(copies, DEPTH, 0, 0)
    input_grad, done = call(
        backward_kernel,
        (shape(x.shape, BF16), flag),
        [index, turn, table(mine), table(other), late, rest],
        [
            pad,
            all_cols,
            line,
            line,
            shape((strips + 32, 3 * CH), BF16),
            shape((strips, 3 * CH), BF16),
            shape((32, 3 * CH), F32),
            shape((strips + 32, 4 * CH), F32),
            wide,
            strip_rows,
            cell_rows,
        ],
        specs=[smem] + [vmem] * 5,
        cost=4,
    )
    copies = call(second_sum_kernel, shape((plane, part, CH), BF16), [pieces, done])
    summed = lax.all_to_all(copies, PLANE, 0, 0).reshape(-1, CH)
    scale = 1.0 / math.sqrt(lax.axis_size(("w", "x")) * total_tiles * EDGE * EDGE)
    first_grad, second_grad, down_grad = call(
        functools.partial(finish_kernel, scale),
        tuple(shape((count, CH, CH), F32) for count in (9, 9, 4)),
        [summed, swap_core(summed)],
    )
    return (
        coarse.reshape((1, tiles, half, half, CH)),
        input_grad[None],
        first_grad.reshape(conv1_weight.shape),
        second_grad.reshape(conv2_weight.shape),
        down_grad.reshape(coarse_kernel_weight.shape),
    )


def solution(mesh):
    batch = mesh.shape["batch"]
    along_x = 4 if batch % 4 == 0 else 1
    fine = Mesh(
        mesh.devices.reshape(4, 2, 2, batch // along_x, along_x), ("y", "z", "c", "w", "x")
    )
    field = P(("w", "x"), ("y", "z", "c"), None, None, None)
    return jax.shard_map(
        shards,
        mesh=fine,
        in_specs=(field, P(), P(), P(), field, field, P(), P(), P()),
        out_specs=(field, field, P(), P(), P()),
        check_vma=False,
    )
```

time: 117 us -> 107 us (0.915)
  local copies, waits for them, and re-layouts: 22.7 us -> 6.12 us
  Pallas kernels: 15.4 us -> 21.8 us
  starting transfers between devices: 38.8 us -> 40.6 us
  other arithmetic: 2.03 us -> 0.81 us
  blocking collectives: 15.1 us -> 13.9 us
    ppermute x4 -> x8, starting transfers between devices: 5.27 us -> 20.7 us  [swap_apart(): return lax.ppermute(block, axis, [(i, i ^ apart) for i in range(number)])]
    all_to_all x1 -> x0, starting transfers between devices: 11.8 us -> none  [spread(): return lax.all_to_all(copies, axes, 0, 0)]
    unnamed x80 -> x20, local copies, waits for them, and re-layouts: 14.4 us -> 6.12 us
    pallas_call x7 -> x12, Pallas kernels: 15.4 us -> 21.8 us  [call(): pl.pallas_call(kernel, out_shape=outs, in_specs=specs or [vmem] * len(ope...]
    transpose x8 -> x0, local copies, waits for them, and re-layouts: 6.17 us -> none  [the longest x4 2.73 us: flipped(): return jnp.transpose(weight_tensor[::-1, ::-1], (0, 1, 3, 2))]
    all_to_all x1, waiting for transfers between devices: 1.09 us -> 6 us  [shards(): pieces = lax.all_to_all(copies, DEPTH, 0, 0)]
    all_to_all x1, starting transfers between devices: 8.11 us -> 5.09 us  [shards(): pieces = lax.all_to_all(kept.reshape(plane, part, CH), PLANE, 0, 0)]
    ppermute x4 -> x8, waiting for transfers between devices: 13.3 us -> 10.7 us  [swap_apart(): return lax.ppermute(block, axis, [(i, i ^ apart) for i in range(number)])]
  transfers between devices with their start and end apart: 11 -> 14, of which waited for: 8 -> 9; matrix products, arithmetic and copies ran while one was open for 11% -> 1% of each run, Pallas kernels for 4% -> 15%
where the time goes in v3:
time: 107 us; the launch traced here: 106 us
  starting transfers between devices  40.6 us (38%)
  waiting for transfers between devices  21.9 us (20%)
  Pallas kernels  21.8 us (20%)
  blocking collectives  13.9 us (13%)
  local copies, waits for them, and re-layouts  6.12 us (6%)
    pallas_call x12, Pallas kernels, call(): pl.pallas_call(kernel, out_shape=outs, in_specs=specs or [vmem] * len(ope...  21.8 us
    ppermute x8, starting transfers between devices, swap_apart(): return lax.ppermute(block, axis, [(i, i ^ apart) for i in range(number)])  20.7 us
    all_to_all x1, blocking collectives, shards(): summed = lax.all_to_all(copies, PLANE, 0, 0).reshape(-1, CH)  13.9 us
    ppermute x8, waiting for transfers between devices, swap_apart(): return lax.ppermute(block, axis, [(i, i ^ apart) for i in range(number)])  10.7 us
    all_to_all x1, starting transfers between devices, shards(): pieces = lax.all_to_all(copies, DEPTH, 0, 0)  7.62 us
    ppermute x4, starting transfers between devices, swap_core(): return lax.ppermute(block, 'c', [(0, 1), (1, 0)])  7.27 us
    unnamed x20, local copies, waits for them, and re-layouts  6.12 us
    all_to_all x1, waiting for transfers between devices, shards(): pieces = lax.all_to_all(copies, DEPTH, 0, 0)  6 us
  transfers between devices with their start and end apart: 14, of which 9 were waited for; matrix products, arithmetic and copies ran while one was open for 1% of the time, Pallas kernels for 15%

profile of v3, /device:TPU:1, one launch (start us, length us, event | category | flops | bytes accessed | tf_op | source)
XLA Modules:
  0.0 106.0 jit_solution(18081519605626559075)
XLA Ops:
  0.6 0.0 copy-start.9
  0.6 0.9 copy-done.9
  1.6 0.1 shard_map.129.own_ref
  1.6 7.8 %collective-permute-start = (bf16[3,4,2,16,128]{4,3,2,1,0:T(8,128)(2,1)S(1)}, bf16[3,4,2,16,128]{4,3,2,1,0:T(8,128)(2,1)S(1)}, u32[]{:S(2)}, u32[]{:S(2)}) collective-permute-start(bf16[3,4,2,16,128]{4,3,2,1,0:T(8,128)(2,1)S(1)} %shard_map.129.own_ref), channel_id=1, source_target_pairs={{0,32},{32,0},{1,33},{33,1},{2,34},{34,2},{3,35},{35,3},{4,36},{36... | collective-permute-start | bytes 294920 | tf_op jit(solution)/shard_map/ppermute | solution.py:28
  9.4 2.1 %collective-permute-done.across_ref = bf16[3,4,2,16,128]{4,3,2,1,0:T(8,128)(2,1)S(1)} collective-permute-done((bf16[3,4,2,16,128]{4,3,2,1,0:T(8,128)(2,1)S(1)}, bf16[3,4,2,16,128]{4,3,2,1,0:T(8,128)(2,1)S(1)}, u32[]{:S(2)}, u32[]{:S(2)}) %collective-permute-start) | collective-permute-done | bytes 98336 | tf_op jit(solution)/shard_map/ppermute | solution.py:28
  11.6 1.8 %collective-permute-start.1 = (bf16[2,3,4,2,16,128]{5,4,3,2,1,0:T(8,128)(2,1)S(1)}, bf16[2,3,4,2,16,128]{5,4,3,2,1,0:T(8,128)(2,1)S(1)}, u32[]{:S(2)}, u32[]{:S(2)}) collective-permute-start(bf16[2,3,4,2,16,128]{5,4,3,2,1,0:T(8,128)(2,1)S(1)} %shard_map.130.own_ref), channel_id=1, source_target_pairs={{0,64},{64,0},{128,192},{192,128},{1,65},{65,1},{129,193},{193,129... | collective-permute-start | bytes 589832 | tf_op jit(solution)/shard_map/ppermute | solution.py:28
  13.4 2.6 %collective-permute-start.2 = (bf16[2,3,4,2,16,128]{5,4,3,2,1,0:T(8,128)(2,1)S(1)}, bf16[2,3,4,2,16,128]{5,4,3,2,1,0:T(8,128)(2,1)S(1)}, u32[]{:S(2)}, u32[]{:S(2)}) collective-permute-start(bf16[2,3,4,2,16,128]{5,4,3,2,1,0:T(8,128)(2,1)S(1)} %shard_map.130.own_ref), channel_id=1, source_target_pairs={{0,128},{64,192},{128,0},{192,64},{1,129},{65,193},{129,1},{193,65... | collective-permute-start | bytes 589832 | tf_op jit(solution)/shard_map/ppermute | solution.py:28
  16.0 0.0 collective-permute-start.3
  16.0 6.3 %shard_map.128 = (s32[296]{0:T(512)}, bf16[192,192]{1,0:T(8,128)(2,1)}, bf16[1152,896]{1,0:T(8,128)(2,1)}, bf16[1152,768]{1,0:T(8,128)(2,1)}, f32[768,256]{1,0:T(8,128)}) custom-call(s32[4,48]{1,0:T(4,128)} %bitcast.37, s32[4,48]{1,0:T(4,128)} %bitcast.38, s32[48]{0:T(128)} %slot_ref.1, bf16[3,16,16,128]{3,2,1,0:T(8,128)(2,1)} %bitcast.27, ...), custom_call_target="tpu_custom_call" | custom-call | flops 905969664 | bytes 2097152 | tf_op jit(solution)/shard_map/pallas_call | solution.py:541
  22.3 0.0 collective-permute-done.1.one_ref
  22.4 1.4 %collective-permute-done.2.two_ref = bf16[2,3,4,2,16,128]{5,4,3,2,1,0:T(8,128)(2,1)S(1)} collective-permute-done((bf16[2,3,4,2,16,128]{5,4,3,2,1,0:T(8,128)(2,1)S(1)}, bf16[2,3,4,2,16,128]{5,4,3,2,1,0:T(8,128)(2,1)S(1)}, u32[]{:S(2)}, u32[]{:S(2)}) %collective-permute-start.2) | collective-permute-done | bytes 196640 | tf_op jit(solution)/shard_map/ppermute | solution.py:28
  23.8 3.1 %collective-permute-done.3.three_ref = bf16[2,3,4,2,16,128]{5,4,3,2,1,0:T(8,128)(2,1)S(1)} collective-permute-done((bf16[2,3,4,2,16,128]{5,4,3,2,1,0:T(8,128)(2,1)S(1)}, bf16[2,3,4,2,16,128]{5,4,3,2,1,0:T(8,128)(2,1)S(1)}, u32[]{:S(2)}, u32[]{:S(2)}) %collective-permute-start.3) | collective-permute-done | bytes 196640 | tf_op jit(solution)/shard_map/ppermute | solution.py:28
  26.9 0.7 copy-done.7
  27.6 0.6 shard_map.131
  28.2 1.7 %collective-permute-start.4 = (bf16[4,2,3,4,2,16,128]{6,5,4,3,2,1,0:T(8,128)(2,1)S(1)}, bf16[4,2,3,4,2,16,128]{6,5,4,3,2,1,0:T(8,128)(2,1)S(1)}, u32[]{:S(2)}, u32[]{:S(2)}) collective-permute-start(bf16[4,2,3,4,2,16,128]{6,5,4,3,2,1,0:T(8,128)(2,1)S(1)} %shard_map.131), channel_id=1, source_target_pairs={{0,16},{16,0},{1,17},{17,1},{2,18},{18,2},{3,19},{19,3},{4,20},{20... | collective-permute-start | bytes 2359304 | tf_op jit(solution)/shard_map/ppermute | solution.py:23
  30.0 1.9 %collective-permute-done.4 = bf16[4,2,3,4,2,16,128]{6,5,4,3,2,1,0:T(8,128)(2,1)S(1)} collective-permute-done((bf16[4,2,3,4,2,16,128]{6,5,4,3,2,1,0:T(8,128)(2,1)S(1)}, bf16[4,2,3,4,2,16,128]{6,5,4,3,2,1,0:T(8,128)(2,1)S(1)}, u32[]{:S(2)}, u32[]{:S(2)}) %collective-permute-start.4) | collective-permute-done | bytes 786464 | tf_op jit(solution)/shard_map/ppermute | solution.py:23
  31.9 1.6 %copy-done = bf16[1152,896]{1,0:T(8,128)(2,1)S(1)} copy-done((bf16[1152,896]{1,0:T(8,128)(2,1)S(1)}, bf16[1152,896]{1,0:T(8,128)(2,1)}, u32[]{:S(2)}) %copy-start) | copy-done | bytes 2064408
  33.5 0.9 copy-done.2
  34.3 3.3 %shard_map.132 = (bf16[192,128]{1,0:T(8,128)(2,1)}, bf16[3,4,2,16,128]{4,3,2,1,0:T(8,128)(2,1)S(1)}, f32[768,128]{1,0:T(8,128)S(1)}, f32[192,128]{1,0:T(8,128)S(...) custom-call(s32[296]{0:T(512)S(1)} %copy-done.7, ...), custom_call_target="tpu_custom_call" | custom-call | flops 452984832 | bytes 2097152 | tf_op jit(solution)/shard_map/pallas_call | solution.py:541
  37.6 4.5 %collective-permute-start.5 = (bf16[3,4,2,16,128]{4,3,2,1,0:T(8,128)(2,1)S(1)}, bf16[3,4,2,16,128]{4,3,2,1,0:T(8,128)(2,1)S(1)}, u32[]{:S(2)}, u32[]{:S(2)}) collective-permute-start(bf16[3,4,2,16,128]{4,3,2,1,0:T(8,128)(2,1)S(1)} %get-tuple-element.46.own_ref), channel_id=1, source_target_pairs={{0,32},{32,0},{1,33},{33,1},{2,34},{34,2},{3,35},{35,3},{4,36},{36... | collective-permute-start | bytes 294920 | tf_op jit(solution)/shard_map/ppermute | solution.py:28
  42.2 4.1 %shard_map.133 = (f32[2,1408,128]{2,1,0:T(8,128)S(1)}, f32[960,256]{1,0:T(8,128)S(1)}) custom-call(s32[296]{0:T(512)S(1)} %copy-done.7, bf16[192,192]{1,0:T(8,128)(2,1)S(1)} %copy-done.2, bf16[1152,896]{1,0:T(8,128)(2,1)S(1)} %copy-done, bf16[1152,768]{1,0:T(8,128)(2,1)S(1)} %copy-done.1, f32[768,128]{1,0:T(8,128)S(1)} %get-tuple-element.37.pre_ref, ...), custom_call_target="tpu_custom_call" | custom-call | flops 905969664 | bytes 2097152 | tf_op jit(solution)/shard_map/pallas_call | solution.py:541
  46.3 0.0 collective-permute-done.5.across_ref
  46.3 0.1 shard_map.134
  46.4 0.7 collective-permute-start.6
  47.1 0.0 collective-permute-start.7
  47.1 2.4 %collective-permute-start.8 = (bf16[2,3,4,2,16,128]{5,4,3,2,1,0:T(8,128)(2,1)S(1)}, bf16[2,3,4,2,16,128]{5,4,3,2,1,0:T(8,128)(2,1)}, u32[]{:S(2)}, u32[]{:S(2)}) collective-permute-start(bf16[2,3,4,2,16,128]{5,4,3,2,1,0:T(8,128)(2,1)S(1)} %get-tuple-element.48.own_ref), channel_id=1, source_target_pairs={{0,128},{64,192},{128,0},{192,64},{1,129},{65,193},{129,1},{193,65... | collective-permute-start | bytes 589832 | tf_op jit(solution)/shard_map/ppermute | solution.py:28
  49.6 1.4 %collective-permute-start.9 = (bf16[2,3,4,2,16,128]{5,4,3,2,1,0:T(8,128)(2,1)S(1)}, bf16[2,3,4,2,16,128]{5,4,3,2,1,0:T(8,128)(2,1)}, u32[]{:S(2)}, u32[]{:S(2)}) collective-permute-start(bf16[2,3,4,2,16,128]{5,4,3,2,1,0:T(8,128)(2,1)S(1)} %get-tuple-element.48.own_ref), channel_id=1, source_target_pairs={{0,192},{64,128},{128,64},{192,0},{1,193},{65,129},{129,65},{193,1... | collective-permute-start | bytes 589832 | tf_op jit(solution)/shard_map/ppermute | solution.py:28
  51.0 0.0 collective-permute-done.6
  51.0 0.8 fusion
  51.8 5.1 %all-to-all-start = ((bf16[16,88,128]{2,1,0:T(8,128)(2,1)}), bf16[16,88,128]{2,1,0:T(8,128)(2,1)S(1)}, u32[]{:S(2)}, u32[]{:S(2)}) async-start(bf16[16,88,128]{2,1,0:T(8,128)(2,1)} %bitcast.29), calls=%async_computation | async-start | bytes 720896 | tf_op jit(solution)/shard_map/all_to_all | solution.py:653
  56.9 0.0 copy-start.3
  56.9 0.0 copy-start.8
  56.9 0.0 collective-permute-done.7.one_ref
  56.9 2.0 %collective-permute-done.8.two_ref = bf16[2,3,4,2,16,128]{5,4,3,2,1,0:T(8,128)(2,1)} collective-permute-done((bf16[2,3,4,2,16,128]{5,4,3,2,1,0:T(8,128)(2,1)S(1)}, bf16[2,3,4,2,16,128]{5,4,3,2,1,0:T(8,128)(2,1)}, u32[]{:S(2)}, u32[]{:S(2)}) %collective-permute-start.8) | collective-permute-done | bytes 196640 | tf_op jit(solution)/shard_map/ppermute | solution.py:28
  58.9 2.0 %collective-permute-done.9.three_ref = bf16[2,3,4,2,16,128]{5,4,3,2,1,0:T(8,128)(2,1)} collective-permute-done((bf16[2,3,4,2,16,128]{5,4,3,2,1,0:T(8,128)(2,1)S(1)}, bf16[2,3,4,2,16,128]{5,4,3,2,1,0:T(8,128)(2,1)}, u32[]{:S(2)}, u32[]{:S(2)}) %collective-permute-start.9) | collective-permute-done | bytes 196640 | tf_op jit(solution)/shard_map/ppermute | solution.py:28
  60.9 1.2 %shard_map.135.table_ref = bf16[4,2,3,4,2,16,128]{6,5,4,3,2,1,0:T(8,128)(2,1)S(1)} custom-call(bf16[2,3,4,2,16,128]{5,4,3,2,1,0:T(8,128)(2,1)S(1)} %get-tuple-element.48.own_ref, bf16[2,3,4,2,16,128]{5,4,3,2,1,0:T(8,128)(2,1)} %collective-permute-done.7.one_ref, bf16[2,3,4,2,16,128]{5,4,3,2,1,0:T(8,128)(2,1)} %collective-permute-done.8.two_ref, ...), custom_call_target="tpu_custom_call" | custom-call | flops 22649241600 | bytes 2097152 | tf_op jit(solution)/shard_map/pallas_call | solution.py:541
  62.1 0.9 copy-done.4
  63.0 2.0 %all-to-all-done.pieces_ref = bf16[16,88,128]{2,1,0:T(8,128)(2,1)S(1)} async-done(((bf16[16,88,128]{2,1,0:T(8,128)(2,1)}), bf16[16,88,128]{2,1,0:T(8,128)(2,1)S(1)}, u32[]{:S(2)}, u32[]{:S(2)}) %all-to-all-start) | async-done | bytes 360480 | tf_op jit(solution)/shard_map/all_to_all | solution.py:653
  65.0 1.1 %copy-done.5 = bf16[4,2,3,4,2,16,128]{6,5,4,3,2,1,0:T(8,128)(2,1)S(1)} copy-done((bf16[4,2,3,4,2,16,128]{6,5,4,3,2,1,0:T(8,128)(2,1)S(1)}, bf16[4,2,3,4,2,16,128]{6,5,4,3,2,1,0:T(8,128)(2,1)}, u32[]{:S(2)}) %copy-start.5) | copy-done | bytes 786456
  66.1 1.0 shard_map.136
  67.1 2.4 %collective-permute-start.10 = (bf16[4,2,3,4,2,16,128]{6,5,4,3,2,1,0:T(8,128)(2,1)}, bf16[4,2,3,4,2,16,128]{6,5,4,3,2,1,0:T(8,128)(2,1)}, u32[]{:S(2)}, u32[]{:S(2)}) collective-permute-start(bf16[4,2,3,4,2,16,128]{6,5,4,3,2,1,0:T(8,128)(2,1)} %get-tuple-element.49), channel_id=1, source_target_pairs={{0,16},{16,0},{1,17},{17,1},{2,18},{18,2},{3,19},{19,3},{4,20},{20... | collective-permute-start | bytes 2359304 | tf_op jit(solution)/shard_map/ppermute | solution.py:23
  69.5 7.6 %all-to-all-start.1 = ((bf16[8,88,128]{2,1,0:T(8,128)(2,1)}), bf16[8,88,128]{2,1,0:T(8,128)(2,1)S(1)}, u32[]{:S(2)}, u32[]{:S(2)}) async-start(bf16[8,88,128]{2,1,0:T(8,128)(2,1)} %get-tuple-element.52), calls=%async_computation.1 | async-start | bytes 360448 | tf_op jit(solution)/shard_map/all_to_all | solution.py:661
  77.1 3.8 %shard_map.137 = (bf16[3,16,16,128]{3,2,1,0:T(8,128)(2,1)}, f32[8,128]{1,0:T(8,128)S(1)}) custom-call(s32[296]{0:T(512)S(1)} %copy-done.8, bf16[192,192]{1,0:T(8,128)(2,1)S(1)} %copy-done.3, bf16[24,4,2,16,128]{4,3,2,1,0:T(8,128)(2,1)} %bitcast.13.mine_ref, bf16[24,4,2,16,128]{4,3,2,1,0:T(8,128)(2,1)} %bitcast.14.other_ref, bf16[1152,768]{1,0:T(8,128)(2,1)S(1)} %copy-done.1, ...), custom_call_target="tpu_custom_call" | custom-call | flops 905969664 | bytes 2097152 | tf_op jit(solution)/shard_map/pallas_call | solution.py:541
  81.0 6.0 %all-to-all-done.1.pieces_ref = bf16[8,88,128]{2,1,0:T(8,128)(2,1)S(1)} async-done(((bf16[8,88,128]{2,1,0:T(8,128)(2,1)}), bf16[8,88,128]{2,1,0:T(8,128)(2,1)S(1)}, u32[]{:S(2)}, u32[]{:S(2)}) %all-to-all-start.1) | async-done | bytes 180256 | tf_op jit(solution)/shard_map/all_to_all | solution.py:661
  87.0 13.9 %all_to_all.15 = bf16[16,88,128]{2,1,0:T(8,128)(2,1)S(1)} all-to-all(bf16[16,88,128]{2,1,0:T(8,128)(2,1)S(1)} %shard_map.138), channel_id=1, replica_groups=mesh['y'=4,'z'=2,'c'=2,'w'=4,'x'=4] {'x','y'}, dimensions={0} | all-to-all | bytes 720896 | tf_op jit(solution)/shard_map/all_to_all | solution.py:683
  101.0 2.4 %collective-permute-start.11 = (bf16[1408,128]{1,0:T(8,128)(2,1)S(1)}, bf16[1408,128]{1,0:T(8,128)(2,1)S(1)}, u32[]{:S(2)}, u32[]{:S(2)}) collective-permute-start(bf16[1408,128]{1,0:T(8,128)(2,1)S(1)} %bitcast.25), channel_id=1, source_target_pairs={{0,16},{16,0},{1,17},{17,1},{2,18},{18,2},{3,19},{19,3},{4,20},{20... | collective-permute-start | bytes 1081352 | tf_op jit(solution)/shard_map/ppermute | solution.py:23
  103.4 1.3 %collective-permute-done.11.other_ref = bf16[1408,128]{1,0:T(8,128)(2,1)S(1)} collective-permute-done((bf16[1408,128]{1,0:T(8,128)(2,1)S(1)}, bf16[1408,128]{1,0:T(8,128)(2,1)S(1)}, u32[]{:S(2)}, u32[]{:S(2)}) %collective-permute-start.11) | collective-permute-done | bytes 360480 | tf_op jit(solution)/shard_map/ppermute | solution.py:23
  104.7 1.3 %shard_map.139 = (f32[9,128,128]{2,1,0:T(8,128)}, f32[9,128,128]{2,1,0:T(8,128)}, f32[4,128,128]{2,1,0:T(8,128)}) custom-call(bf16[1408,128]{1,0:T(8,128)(2,1)S(1)} %bitcast.26, bf16[1408,128]{1,0:T(8,128)(2,1)S(1)} %collective-permute-done.11.other_ref), custom_call_target="tpu_custom_call" | custom-call | flops 226492416 | bytes 2097152 | tf_op jit(solution)/shard_map/pallas_call | solution.py:541
  (14 shorter events, 0.1 us)
Async XLA Ops:
  0.6 0.9 copy-start.9
  1.6 9.9 %collective-permute-start = (bf16[3,4,2,16,128]{4,3,2,1,0:T(8,128)(2,1)S(1)}, bf16[3,4,2,16,128]{4,3,2,1,0:T(8,128)(2,1)S(1)}, u32[]{:S(2)}, u32[]{:S(2)}) collective-permute-start(bf16[3,4,2,16,128]{4,3,2,1,0:T(8,128)(2,1)S(1)} %shard_map.129.own_ref), channel_id=1, source_target_pairs={{0,32},{32,0},{1,33},{33,1},{2,34},{34,2},{3,35},{35,3},{4,36},{36... | collective-permute-start | bytes 294920 | tf_op jit(solution)/shard_map/ppermute | solution.py:28
  11.6 10.8 %collective-permute-start.1 = (bf16[2,3,4,2,16,128]{5,4,3,2,1,0:T(8,128)(2,1)S(1)}, bf16[2,3,4,2,16,128]{5,4,3,2,1,0:T(8,128)(2,1)S(1)}, u32[]{:S(2)}, u32[]{:S(2)}) collective-permute-start(bf16[2,3,4,2,16,128]{5,4,3,2,1,0:T(8,128)(2,1)S(1)} %shard_map.130.own_ref), channel_id=1, source_target_pairs={{0,64},{64,0},{128,192},{192,128},{1,65},{65,1},{129,193},{193,129... | collective-permute-start | bytes 589832 | tf_op jit(solution)/shard_map/ppermute | solution.py:28
  13.4 10.4 %collective-permute-start.2 = (bf16[2,3,4,2,16,128]{5,4,3,2,1,0:T(8,128)(2,1)S(1)}, bf16[2,3,4,2,16,128]{5,4,3,2,1,0:T(8,128)(2,1)S(1)}, u32[]{:S(2)}, u32[]{:S(2)}) collective-permute-start(bf16[2,3,4,2,16,128]{5,4,3,2,1,0:T(8,128)(2,1)S(1)} %shard_map.130.own_ref), channel_id=1, source_target_pairs={{0,128},{64,192},{128,0},{192,64},{1,129},{65,193},{129,1},{193,65... | collective-permute-start | bytes 589832 | tf_op jit(solution)/shard_map/ppermute | solution.py:28
  16.0 10.9 %collective-permute-start.3 = (bf16[2,3,4,2,16,128]{5,4,3,2,1,0:T(8,128)(2,1)S(1)}, bf16[2,3,4,2,16,128]{5,4,3,2,1,0:T(8,128)(2,1)S(1)}, u32[]{:S(2)}, u32[]{:S(2)}) collective-permute-start(bf16[2,3,4,2,16,128]{5,4,3,2,1,0:T(8,128)(2,1)S(1)} %shard_map.130.own_ref), channel_id=1, source_target_pairs={{0,192},{64,128},{128,64},{192,0},{1,193},{65,129},{129,65},{193,1... | collective-permute-start | bytes 589832 | tf_op jit(solution)/shard_map/ppermute | solution.py:28
  22.3 9.5 %copy-start.6 = (f32[768,256]{1,0:T(8,128)S(1)}, f32[768,256]{1,0:T(8,128)}, u32[]{:S(2)}) copy-start(f32[768,256]{1,0:T(8,128)} %get-tuple-element.34.staged_ref) | copy-start | bytes 2359300
  26.9 0.7 copy-start.7
  28.2 3.6 %collective-permute-start.4 = (bf16[4,2,3,4,2,16,128]{6,5,4,3,2,1,0:T(8,128)(2,1)S(1)}, bf16[4,2,3,4,2,16,128]{6,5,4,3,2,1,0:T(8,128)(2,1)S(1)}, u32[]{:S(2)}, u32[]{:S(2)}) collective-permute-start(bf16[4,2,3,4,2,16,128]{6,5,4,3,2,1,0:T(8,128)(2,1)S(1)} %shard_map.131), channel_id=1, source_target_pairs={{0,16},{16,0},{1,17},{17,1},{2,18},{18,2},{3,19},{19,3},{4,20},{20... | collective-permute-start | bytes 2359304 | tf_op jit(solution)/shard_map/ppermute | solution.py:23
  31.9 1.6 %copy-start = (bf16[1152,896]{1,0:T(8,128)(2,1)S(1)}, bf16[1152,896]{1,0:T(8,128)(2,1)}, u32[]{:S(2)}) copy-start(bf16[1152,896]{1,0:T(8,128)(2,1)} %get-tuple-element.33.early_ref) | copy-start | bytes 6193156
  33.5 0.9 copy-start.2
  34.3 7.8 %copy-start.1 = (bf16[1152,768]{1,0:T(8,128)(2,1)S(1)}, bf16[1152,768]{1,0:T(8,128)(2,1)}, u32[]{:S(2)}) copy-start(bf16[1152,768]{1,0:T(8,128)(2,1)} %get-tuple-element.36.late_ref) | copy-start | bytes 5308420
  37.6 8.7 %collective-permute-start.5 = (bf16[3,4,2,16,128]{4,3,2,1,0:T(8,128)(2,1)S(1)}, bf16[3,4,2,16,128]{4,3,2,1,0:T(8,128)(2,1)S(1)}, u32[]{:S(2)}, u32[]{:S(2)}) collective-permute-start(bf16[3,4,2,16,128]{4,3,2,1,0:T(8,128)(2,1)S(1)} %get-tuple-element.46.own_ref), channel_id=1, source_target_pairs={{0,32},{32,0},{1,33},{33,1},{2,34},{34,2},{3,35},{35,3},{4,36},{36... | collective-permute-start | bytes 294920 | tf_op jit(solution)/shard_map/ppermute | solution.py:28
  46.4 4.6 %collective-permute-start.6 = (f32[1408,128]{1,0:T(8,128)S(1)}, f32[1408,128]{1,0:T(8,128)S(1)}, u32[]{:S(2)}, u32[]{:S(2)}) collective-permute-start(f32[1408,128]{1,0:T(8,128)S(1)} %get-tuple-element.47), channel_id=1, source_target_pairs={{0,16},{16,0},{1,17},{17,1},{2,18},{18,2},{3,19},{19,3},{4,20},{20... | collective-permute-start | bytes 2162696 | tf_op jit(solution)/shard_map/ppermute | solution.py:23
  47.1 9.8 %collective-permute-start.7 = (bf16[2,3,4,2,16,128]{5,4,3,2,1,0:T(8,128)(2,1)S(1)}, bf16[2,3,4,2,16,128]{5,4,3,2,1,0:T(8,128)(2,1)}, u32[]{:S(2)}, u32[]{:S(2)}) collective-permute-start(bf16[2,3,4,2,16,128]{5,4,3,2,1,0:T(8,128)(2,1)S(1)} %get-tuple-element.48.own_ref), channel_id=1, source_target_pairs={{0,64},{64,0},{128,192},{192,128},{1,65},{65,1},{129,193},{193,129... | collective-permute-start | bytes 589832 | tf_op jit(solution)/shard_map/ppermute | solution.py:28
  47.1 11.8 %collective-permute-start.8 = (bf16[2,3,4,2,16,128]{5,4,3,2,1,0:T(8,128)(2,1)S(1)}, bf16[2,3,4,2,16,128]{5,4,3,2,1,0:T(8,128)(2,1)}, u32[]{:S(2)}, u32[]{:S(2)}) collective-permute-start(bf16[2,3,4,2,16,128]{5,4,3,2,1,0:T(8,128)(2,1)S(1)} %get-tuple-element.48.own_ref), channel_id=1, source_target_pairs={{0,128},{64,192},{128,0},{192,64},{1,129},{65,193},{129,1},{193,65... | collective-permute-start | bytes 589832 | tf_op jit(solution)/shard_map/ppermute | solution.py:28
  49.6 11.4 %collective-permute-start.9 = (bf16[2,3,4,2,16,128]{5,4,3,2,1,0:T(8,128)(2,1)S(1)}, bf16[2,3,4,2,16,128]{5,4,3,2,1,0:T(8,128)(2,1)}, u32[]{:S(2)}, u32[]{:S(2)}) collective-permute-start(bf16[2,3,4,2,16,128]{5,4,3,2,1,0:T(8,128)(2,1)S(1)} %get-tuple-element.48.own_ref), channel_id=1, source_target_pairs={{0,192},{64,128},{128,64},{192,0},{1,193},{65,129},{129,65},{193,1... | collective-permute-start | bytes 589832 | tf_op jit(solution)/shard_map/ppermute | solution.py:28
  51.8 13.2 %all-to-all-start = ((bf16[16,88,128]{2,1,0:T(8,128)(2,1)}), bf16[16,88,128]{2,1,0:T(8,128)(2,1)S(1)}, u32[]{:S(2)}, u32[]{:S(2)}) async-start(bf16[16,88,128]{2,1,0:T(8,128)(2,1)} %bitcast.29), calls=%async_computation | async-start | bytes 720896 | tf_op jit(solution)/shard_map/all_to_all | solution.py:653
  56.9 20.2 %copy-start.3 = (bf16[192,192]{1,0:T(8,128)(2,1)S(1)}, bf16[192,192]{1,0:T(8,128)(2,1)}, u32[]{:S(2)}) copy-start(bf16[192,192]{1,0:T(8,128)(2,1)} %get-tuple-element.32.turn_ref) | copy-start | bytes 221188
  56.9 20.2 %copy-start.8 = (s32[296]{0:T(512)S(1)}, s32[296]{0:T(512)}, u32[]{:S(2)}) copy-start(s32[296]{0:T(512)} %get-tuple-element.31.index_ref) | copy-start | bytes 3556
  62.1 0.9 copy-start.4
  65.0 1.1 %copy-start.5 = (bf16[4,2,3,4,2,16,128]{6,5,4,3,2,1,0:T(8,128)(2,1)S(1)}, bf16[4,2,3,4,2,16,128]{6,5,4,3,2,1,0:T(8,128)(2,1)}, u32[]{:S(2)}) copy-start(bf16[4,2,3,4,2,16,128]{6,5,4,3,2,1,0:T(8,128)(2,1)} %copy-done.4) | copy-start | bytes 2359300
  67.1 10.0 %collective-permute-start.10 = (bf16[4,2,3,4,2,16,128]{6,5,4,3,2,1,0:T(8,128)(2,1)}, bf16[4,2,3,4,2,16,128]{6,5,4,3,2,1,0:T(8,128)(2,1)}, u32[]{:S(2)}, u32[]{:S(2)}) collective-permute-start(bf16[4,2,3,4,2,16,128]{6,5,4,3,2,1,0:T(8,128)(2,1)} %get-tuple-element.49), channel_id=1, source_target_pairs={{0,16},{16,0},{1,17},{17,1},{2,18},{18,2},{3,19},{19,3},{4,20},{20... | collective-permute-start | bytes 2359304 | tf_op jit(solution)/shard_map/ppermute | solution.py:23
  69.5 17.5 %all-to-all-start.1 = ((bf16[8,88,128]{2,1,0:T(8,128)(2,1)}), bf16[8,88,128]{2,1,0:T(8,128)(2,1)S(1)}, u32[]{:S(2)}, u32[]{:S(2)}) async-start(bf16[8,88,128]{2,1,0:T(8,128)(2,1)} %get-tuple-element.52), calls=%async_computation.1 | async-start | bytes 360448 | tf_op jit(solution)/shard_map/all_to_all | solution.py:661
  101.0 3.7 %collective-permute-start.11 = (bf16[1408,128]{1,0:T(8,128)(2,1)S(1)}, bf16[1408,128]{1,0:T(8,128)(2,1)S(1)}, u32[]{:S(2)}, u32[]{:S(2)}) collective-permute-start(bf16[1408,128]{1,0:T(8,128)(2,1)S(1)} %bitcast.25), channel_id=1, source_target_pairs={{0,16},{16,0},{1,17},{17,1},{2,18},{18,2},{3,19},{19,3},{4,20},{20... | collective-permute-start | bytes 1081352 | tf_op jit(solution)/shard_map/ppermute | solution.py:23

commit v4 on v3

--- a/solution.py
+++ b/solution.py
@@ -456,20 +456,13 @@
     out_ref[...] = as_cells(cells_ref[...]).astype(BF16)
 
 
-def first_pair_kernel(own_ref, across_ref, pair_ref):
+def first_pair_kernel(own_ref, across_ref, index_ref, pair_ref):
     pair_ref[0] = own_ref[...]
     pair_ref[1] = across_ref[...]
 
 
-def first_table_kernel(own_ref, one_ref, two_ref, three_ref, index_ref, table_ref):
-    for at, part_ref in enumerate((own_ref, one_ref, two_ref, three_ref)):
-        table_ref[at] = part_ref[...]
-
-
-def pair_kernel(own_ref, across_ref, grads_ref, pair_ref, give_ref):
-    pair_ref[0] = own_ref[...]
-    pair_ref[1] = across_ref[...]
-    give_ref[...] = grads_ref[1]
+def gate_kernel(*refs):
+    refs[-1][...] = jnp.zeros_like(refs[-1])
 
 
 def table_kernel(own_ref, one_ref, two_ref, three_ref, table_ref):
@@ -483,13 +476,21 @@
         copies_ref[at] = total
 
 
-def first_sum_kernel(pieces_ref, table_ref, copies_ref, out_ref):
+def first_sum_kernel(pieces_ref, flag_ref, own_ref, across_ref, copies_ref, pair_ref):
     spread_sum(pieces_ref, copies_ref)
-    out_ref[...] = table_ref[...]
-
-
-def second_sum_kernel(pieces_ref, flag_ref, copies_ref):
+    pair_ref[0] = own_ref[...]
+    pair_ref[1] = across_ref[...]
+
+
+def second_sum_kernel(
+    pieces_ref, flag_ref, own_ref, one_ref, two_ref, three_ref, copies_ref, table_ref
+):
     spread_sum(pieces_ref, copies_ref)
+    table_kernel(own_ref, one_ref, two_ref, three_ref, table_ref)
+
+
+def hold_kernel(block_ref, flag_ref, out_ref):
+    out_ref[...] = block_ref[...]
 
 
 def finish_kernel(scale, mine_ref, other_ref, first_ref, second_ref, down_ref):
@@ -583,14 +584,9 @@
         cost=4,
         room=60,
     )
-    pair = call(first_pair_kernel, shape((2,) + ring.shape, BF16), [own_ring, across])
+    pair = call(first_pair_kernel, shape((2,) + ring.shape, BF16), [own_ring, across, index], specs=[vmem, vmem, smem])
     along = [swap_apart(pair, "y", apart) for apart in (1, 2, 3)]
-    mine = call(
-        first_table_kernel,
-        shape((4,) + pair.shape, BF16),
-        [pair] + along + [index],
-        specs=[vmem] * 4 + [smem],
-    )
+    mine = call(table_kernel, shape((4,) + pair.shape, BF16), [pair] + along)
     other = swap_core(mine)
 
     def table(block):
@@ -624,7 +620,6 @@
         specs=[smem] + [vmem] * 5,
         cost=2,
     )
-    across = swap_apart(delta_ring, "z", 1)
     grads, rest = call(
         gradient_kernel,
         (shape((2, 11 * CH, CH), F32), shape((cells + strips, 2 * CH), F32)),
@@ -642,23 +637,24 @@
         specs=[smem] + [vmem] * 11,
         cost=4,
     )
-    pair, give = call(
-        pair_kernel,
-        (shape((2,) + ring.shape, BF16), shape(grads.shape[1:], F32)),
-        [delta_ring, across, grads],
-    )
-    kept = (grads[0] + swap_core(give)).astype(BF16)
+    kept = (grads[0] + swap_core(grads[1])).astype(BF16)
+    part = kept.shape[0] // plane
+    across = swap_apart(delta_ring, "z", 1)
+    pieces = lax.all_to_all(kept.reshape(plane, part, CH), PLANE, 0, 0)
+    copies, pair = call(
+        first_sum_kernel,
+        (shape((deep, part, CH), BF16), shape((2,) + ring.shape, BF16)),
+        [pieces, call(gate_kernel, flag, [across], cost=100), delta_ring, across],
+    )
     along = [swap_apart(pair, "y", apart) for apart in (1, 2, 3)]
-    part = kept.shape[0] // plane
-    pieces = lax.all_to_all(kept.reshape(plane, part, CH), PLANE, 0, 0)
-    mine = call(table_kernel, shape((4,) + pair.shape, BF16), [pair] + along, cost=100)
+    pieces = lax.all_to_all(copies, DEPTH, 0, 0)
     copies, mine = call(
-        first_sum_kernel,
-        (shape((deep, part, CH), BF16), shape(mine.shape, BF16)),
-        [pieces, mine],
+        second_sum_kernel,
+        (shape((plane, part, CH), BF16), shape((4,) + pair.shape, BF16)),
+        [pieces, call(gate_kernel, flag, along, cost=100), pair] + along,
     )
     other = swap_core(mine)
-    pieces = lax.all_to_all(copies, DEPTH, 0, 0)
+    summed = lax.all_to_all(copies, PLANE, 0, 0).reshape(-1, CH)
     input_grad, done = call(
         backward_kernel,
         (shape(x.shape, BF16), flag),
@@ -677,10 +673,9 @@
             cell_rows,
         ],
         specs=[smem] + [vmem] * 5,
-        cost=4,
-    )
-    copies = call(second_sum_kernel, shape((plane, part, CH), BF16), [pieces, done])
-    summed = lax.all_to_all(copies, PLANE, 0, 0).reshape(-1, CH)
+        cost=100,
+    )
+    summed = call(hold_kernel, shape(summed.shape, BF16), [summed, done])
     scale = 1.0 / math.sqrt(lax.axis_size(("w", "x")) * total_tiles * EDGE * EDGE)
     first_grad, second_grad, down_grad = call(
         functools.partial(finish_kernel, scale),

time: 107 us -> 101 us (0.944)
  waiting for transfers between devices: 21.9 us -> 37.1 us
  blocking collectives: 13.9 us -> 0 us
  starting transfers between devices: 40.6 us -> 36.1 us
  local copies, waits for them, and re-layouts: 6.12 us -> 4.14 us
    all_to_all x1 -> x0, blocking collectives: 13.9 us -> none  [shards(): summed = lax.all_to_all(copies, PLANE, 0, 0).reshape(-1, CH)]
    ppermute x8, waiting for transfers between devices: 10.7 us -> 17.1 us  [swap_apart(): return lax.ppermute(block, axis, [(i, i ^ apart) for i in range(number)])]
    all_to_all x1, waiting for transfers between devices: 1.97 us -> 7.4 us  [shards(): pieces = lax.all_to_all(kept.reshape(plane, part, CH), PLANE, 0, 0)]
    ppermute x8, starting transfers between devices: 20.7 us -> 16.1 us  [swap_apart(): return lax.ppermute(block, axis, [(i, i ^ apart) for i in range(number)])]
    all_to_all x0 -> x1, waiting for transfers between devices: none -> 3.83 us  [shards(): summed = lax.all_to_all(copies, PLANE, 0, 0).reshape(-1, CH)]
    all_to_all x0 -> x1, starting transfers between devices: none -> 3.55 us  [shards(): summed = lax.all_to_all(copies, PLANE, 0, 0).reshape(-1, CH)]
    all_to_all x1, starting transfers between devices: 7.62 us -> 4.08 us  [shards(): pieces = lax.all_to_all(copies, DEPTH, 0, 0)]
    unnamed x20 -> x18, local copies, waits for them, and re-layouts: 6.12 us -> 4.09 us
  transfers between devices with their start and end apart: 14 -> 15, of which waited for: 9 -> 12; matrix products, arithmetic and copies ran while one was open for 1% -> 1% of each run, Pallas kernels for 15% -> 10%
where the time goes in v4:
time: 101 us; the launch traced here: 100 us
  waiting for transfers between devices  37.1 us (37%)
  starting transfers between devices  36.1 us (36%)
  Pallas kernels  21.4 us (21%)
  local copies, waits for them, and re-layouts  4.14 us (4%)
    pallas_call x13, Pallas kernels, call(): pl.pallas_call(kernel, out_shape=outs, in_specs=specs or [vmem] * len(ope...  21.4 us
    ppermute x8, waiting for transfers between devices, swap_apart(): return lax.ppermute(block, axis, [(i, i ^ apart) for i in range(number)])  17.1 us
    ppermute x8, starting transfers between devices, swap_apart(): return lax.ppermute(block, axis, [(i, i ^ apart) for i in range(number)])  16.1 us
    ppermute x4, starting transfers between devices, swap_core(): return lax.ppermute(block, 'c', [(0, 1), (1, 0)])  8.27 us
    all_to_all x1, waiting for transfers between devices, shards(): pieces = lax.all_to_all(kept.reshape(plane, part, CH), PLANE, 0, 0)  7.4 us
    ppermute x4, waiting for transfers between devices, swap_core(): return lax.ppermute(block, 'c', [(0, 1), (1, 0)])  4.66 us
    all_to_all x1, waiting for transfers between devices, shards(): pieces = lax.all_to_all(copies, DEPTH, 0, 0)  4.14 us
    all_to_all x1, starting transfers between devices, shards(): pieces = lax.all_to_all(kept.reshape(plane, part, CH), PLANE, 0, 0)  4.12 us
  transfers between devices with their start and end apart: 15, of which 12 were waited for; matrix products, arithmetic and copies ran while one was open for 1% of the time, Pallas kernels for 10%

profile of v4, /device:TPU:1, one launch (start us, length us, event | category | flops | bytes accessed | tf_op | source)
XLA Modules:
  0.0 100.3 jit_solution(2669589056364515640)
XLA Ops:
  0.6 0.0 copy-start.8
  0.6 0.9 copy-done.8
  1.6 0.1 shard_map.129.own_ref
  1.6 7.8 %collective-permute-start = (bf16[3,4,2,16,128]{4,3,2,1,0:T(8,128)(2,1)S(1)}, bf16[3,4,2,16,128]{4,3,2,1,0:T(8,128)(2,1)S(1)}, u32[]{:S(2)}, u32[]{:S(2)}) collective-permute-start(bf16[3,4,2,16,128]{4,3,2,1,0:T(8,128)(2,1)S(1)} %shard_map.129.own_ref), channel_id=1, source_target_pairs={{0,32},{32,0},{1,33},{33,1},{2,34},{34,2},{3,35},{35,3},{4,36},{36... | collective-permute-start | bytes 294920 | tf_op jit(solution)/shard_map/ppermute | solution.py:28
  9.4 6.3 %shard_map.128 = (s32[296]{0:T(512)}, bf16[192,192]{1,0:T(8,128)(2,1)}, bf16[1152,896]{1,0:T(8,128)(2,1)}, bf16[1152,768]{1,0:T(8,128)(2,1)}, f32[768,256]{1,0:T(8,128)}) custom-call(s32[4,48]{1,0:T(4,128)} %bitcast.36, s32[4,48]{1,0:T(4,128)} %bitcast.37, s32[48]{0:T(128)} %slot_ref.1, bf16[3,16,16,128]{3,2,1,0:T(8,128)(2,1)} %bitcast.28, ...), custom_call_target="tpu_custom_call" | custom-call | flops 905969664 | bytes 2097152 | tf_op jit(solution)/shard_map/pallas_call | solution.py:542
  15.8 0.0 copy-start.3
  15.8 0.0 collective-permute-done.across_ref
  15.8 0.0 copy-start.4
  15.8 0.8 copy-done.4
  16.7 0.6 shard_map.130.own_ref
  17.2 1.4 %collective-permute-start.1 = (bf16[2,3,4,2,16,128]{5,4,3,2,1,0:T(8,128)(2,1)S(1)}, bf16[2,3,4,2,16,128]{5,4,3,2,1,0:T(8,128)(2,1)S(1)}, u32[]{:S(2)}, u32[]{:S(2)}) collective-permute-start(bf16[2,3,4,2,16,128]{5,4,3,2,1,0:T(8,128)(2,1)S(1)} %shard_map.130.own_ref), channel_id=1, source_target_pairs={{0,64},{64,0},{128,192},{192,128},{1,65},{65,1},{129,193},{193,129... | collective-permute-start | bytes 589832 | tf_op jit(solution)/shard_map/ppermute | solution.py:28
  18.6 2.6 %collective-permute-start.2 = (bf16[2,3,4,2,16,128]{5,4,3,2,1,0:T(8,128)(2,1)S(1)}, bf16[2,3,4,2,16,128]{5,4,3,2,1,0:T(8,128)(2,1)S(1)}, u32[]{:S(2)}, u32[]{:S(2)}) collective-permute-start(bf16[2,3,4,2,16,128]{5,4,3,2,1,0:T(8,128)(2,1)S(1)} %shard_map.130.own_ref), channel_id=1, source_target_pairs={{0,128},{64,192},{128,0},{192,64},{1,129},{65,193},{129,1},{193,65... | collective-permute-start | bytes 589832 | tf_op jit(solution)/shard_map/ppermute | solution.py:28
  21.2 0.0 collective-permute-start.3
  21.2 1.5 %collective-permute-done.1.one_ref = bf16[2,3,4,2,16,128]{5,4,3,2,1,0:T(8,128)(2,1)S(1)} collective-permute-done((bf16[2,3,4,2,16,128]{5,4,3,2,1,0:T(8,128)(2,1)S(1)}, bf16[2,3,4,2,16,128]{5,4,3,2,1,0:T(8,128)(2,1)S(1)}, u32[]{:S(2)}, u32[]{:S(2)}) %collective-permute-start.1) | collective-permute-done | bytes 196640 | tf_op jit(solution)/shard_map/ppermute | solution.py:28
  22.8 6.7 %collective-permute-done.2.two_ref = bf16[2,3,4,2,16,128]{5,4,3,2,1,0:T(8,128)(2,1)S(1)} collective-permute-done((bf16[2,3,4,2,16,128]{5,4,3,2,1,0:T(8,128)(2,1)S(1)}, bf16[2,3,4,2,16,128]{5,4,3,2,1,0:T(8,128)(2,1)S(1)}, u32[]{:S(2)}, u32[]{:S(2)}) %collective-permute-start.2) | collective-permute-done | bytes 196640 | tf_op jit(solution)/shard_map/ppermute | solution.py:28
  29.5 3.0 %collective-permute-done.3.three_ref = bf16[2,3,4,2,16,128]{5,4,3,2,1,0:T(8,128)(2,1)S(1)} collective-permute-done((bf16[2,3,4,2,16,128]{5,4,3,2,1,0:T(8,128)(2,1)S(1)}, bf16[2,3,4,2,16,128]{5,4,3,2,1,0:T(8,128)(2,1)S(1)}, u32[]{:S(2)}, u32[]{:S(2)}) %collective-permute-start.3) | collective-permute-done | bytes 196640 | tf_op jit(solution)/shard_map/ppermute | solution.py:28
  32.5 0.1 shard_map.131
  32.6 1.6 %collective-permute-start.4 = (bf16[4,2,3,4,2,16,128]{6,5,4,3,2,1,0:T(8,128)(2,1)S(1)}, bf16[4,2,3,4,2,16,128]{6,5,4,3,2,1,0:T(8,128)(2,1)S(1)}, u32[]{:S(2)}, u32[]{:S(2)}) collective-permute-start(bf16[4,2,3,4,2,16,128]{6,5,4,3,2,1,0:T(8,128)(2,1)S(1)} %shard_map.131), channel_id=1, source_target_pairs={{0,16},{16,0},{1,17},{17,1},{2,18},{18,2},{3,19},{19,3},{4,20},{20... | collective-permute-start | bytes 2359304 | tf_op jit(solution)/shard_map/ppermute | solution.py:23
  34.1 1.9 %collective-permute-done.4 = bf16[4,2,3,4,2,16,128]{6,5,4,3,2,1,0:T(8,128)(2,1)S(1)} collective-permute-done((bf16[4,2,3,4,2,16,128]{6,5,4,3,2,1,0:T(8,128)(2,1)S(1)}, bf16[4,2,3,4,2,16,128]{6,5,4,3,2,1,0:T(8,128)(2,1)S(1)}, u32[]{:S(2)}, u32[]{:S(2)}) %collective-permute-start.4) | collective-permute-done | bytes 786464 | tf_op jit(solution)/shard_map/ppermute | solution.py:23
  36.0 1.1 %copy-done.2 = f32[768,256]{1,0:T(8,128)S(1)} copy-done((f32[768,256]{1,0:T(8,128)S(1)}, f32[768,256]{1,0:T(8,128)}, u32[]{:S(2)}) %copy-start.2) | copy-done | bytes 786456
  37.2 3.3 %shard_map.132 = (bf16[192,128]{1,0:T(8,128)(2,1)}, bf16[3,4,2,16,128]{4,3,2,1,0:T(8,128)(2,1)S(1)}, f32[768,128]{1,0:T(8,128)S(1)}, f32[192,128]{1,0:T(8,128)S(...) custom-call(s32[296]{0:T(512)S(1)} %copy-done.5, ...), custom_call_target="tpu_custom_call" | custom-call | flops 452984832 | bytes 2097152 | tf_op jit(solution)/shard_map/pallas_call | solution.py:542
  40.5 4.1 %shard_map.133 = (f32[2,1408,128]{2,1,0:T(8,128)S(1)}, f32[960,256]{1,0:T(8,128)S(1)}) custom-call(s32[296]{0:T(512)S(1)} %copy-done.5, bf16[192,192]{1,0:T(8,128)(2,1)S(1)} %copy-done.3, bf16[1152,896]{1,0:T(8,128)(2,1)S(1)} %copy-done, bf16[1152,768]{1,0:T(8,128)(2,1)S(1)} %copy-done.1, f32[768,128]{1,0:T(8,128)S(1)} %get-tuple-element.37.pre_ref, ...), custom_call_target="tpu_custom_call" | custom-call | flops 905969664 | bytes 2097152 | tf_op jit(solution)/shard_map/pallas_call | solution.py:542
  44.7 0.5 collective-permute-start.5
  45.1 0.4 collective-permute-start.6
  45.5 1.4 %collective-permute-done.5 = f32[1408,128]{1,0:T(8,128)S(1)} collective-permute-done((f32[1408,128]{1,0:T(8,128)S(1)}, f32[1408,128]{1,0:T(8,128)S(1)}, u32[]{:S(2)}, u32[]{:S(2)}) %collective-permute-start.5) | collective-permute-done | bytes 720928 | tf_op jit(solution)/shard_map/ppermute | solution.py:23
  46.9 0.8 fusion
  47.8 4.1 %all-to-all-start = ((bf16[16,88,128]{2,1,0:T(8,128)(2,1)}), bf16[16,88,128]{2,1,0:T(8,128)(2,1)S(1)}, u32[]{:S(2)}, u32[]{:S(2)}) async-start(bf16[16,88,128]{2,1,0:T(8,128)(2,1)} %bitcast.13), calls=%async_computation | async-start | bytes 720896 | tf_op jit(solution)/shard_map/all_to_all | solution.py:643
  51.9 1.4 %collective-permute-done.6.refs_0_.across_ref = bf16[3,4,2,16,128]{4,3,2,1,0:T(8,128)(2,1)S(1)} collective-permute-done((bf16[3,4,2,16,128]{4,3,2,1,0:T(8,128)(2,1)S(1)}, bf16[3,4,2,16,128]{4,3,2,1,0:T(8,128)(2,1)S(1)}, u32[]{:S(2)}, u32[]{:S(2)}) %collective-permute-start.6) | collective-permute-done | bytes 98336 | tf_op jit(solution)/shard_map/ppermute | solution.py:28
  53.3 7.4 %all-to-all-done.pieces_ref = bf16[16,88,128]{2,1,0:T(8,128)(2,1)S(1)} async-done(((bf16[16,88,128]{2,1,0:T(8,128)(2,1)}), bf16[16,88,128]{2,1,0:T(8,128)(2,1)S(1)}, u32[]{:S(2)}, u32[]{:S(2)}) %all-to-all-start) | async-done | bytes 360480 | tf_op jit(solution)/shard_map/all_to_all | solution.py:643
  60.7 0.7 shard_map.135
  61.4 0.3 collective-permute-start.7
  61.7 1.5 %collective-permute-start.8 = (bf16[2,3,4,2,16,128]{5,4,3,2,1,0:T(8,128)(2,1)S(1)}, bf16[2,3,4,2,16,128]{5,4,3,2,1,0:T(8,128)(2,1)S(1)}, u32[]{:S(2)}, u32[]{:S(2)}) collective-permute-start(bf16[2,3,4,2,16,128]{5,4,3,2,1,0:T(8,128)(2,1)S(1)} %get-tuple-element.48.own_ref), channel_id=1, source_target_pairs={{0,128},{64,192},{128,0},{192,64},{1,129},{65,193},{129,1},{193,65... | collective-permute-start | bytes 589832 | tf_op jit(solution)/shard_map/ppermute | solution.py:28
  63.2 2.1 %collective-permute-start.9 = (bf16[2,3,4,2,16,128]{5,4,3,2,1,0:T(8,128)(2,1)S(1)}, bf16[2,3,4,2,16,128]{5,4,3,2,1,0:T(8,128)(2,1)S(1)}, u32[]{:S(2)}, u32[]{:S(2)}) collective-permute-start(bf16[2,3,4,2,16,128]{5,4,3,2,1,0:T(8,128)(2,1)S(1)} %get-tuple-element.48.own_ref), channel_id=1, source_target_pairs={{0,192},{64,128},{128,64},{192,0},{1,193},{65,129},{129,65},{193,1... | collective-permute-start | bytes 589832 | tf_op jit(solution)/shard_map/ppermute | solution.py:28
  65.3 4.1 %all-to-all-start.1 = ((bf16[8,88,128]{2,1,0:T(8,128)(2,1)}), bf16[8,88,128]{2,1,0:T(8,128)(2,1)S(1)}, u32[]{:S(2)}, u32[]{:S(2)}) async-start(bf16[8,88,128]{2,1,0:T(8,128)(2,1)} %get-tuple-element.47), calls=%async_computation.1 | async-start | bytes 360448 | tf_op jit(solution)/shard_map/all_to_all | solution.py:650
  69.4 0.0 collective-permute-done.7.refs_0_.one_ref
  69.4 1.0 collective-permute-done.8.refs_1_.two_ref
  70.4 3.4 %collective-permute-done.9.refs_2_.three_ref = bf16[2,3,4,2,16,128]{5,4,3,2,1,0:T(8,128)(2,1)S(1)} collective-permute-done((bf16[2,3,4,2,16,128]{5,4,3,2,1,0:T(8,128)(2,1)S(1)}, bf16[2,3,4,2,16,128]{5,4,3,2,1,0:T(8,128)(2,1)S(1)}, u32[]{:S(2)}, u32[]{:S(2)}) %collective-permute-start.9) | collective-permute-done | bytes 196640 | tf_op jit(solution)/shard_map/ppermute | solution.py:28
  73.8 4.1 %all-to-all-done.1.pieces_ref = bf16[8,88,128]{2,1,0:T(8,128)(2,1)S(1)} async-done(((bf16[8,88,128]{2,1,0:T(8,128)(2,1)}), bf16[8,88,128]{2,1,0:T(8,128)(2,1)S(1)}, u32[]{:S(2)}, u32[]{:S(2)}) %all-to-all-start.1) | async-done | bytes 180256 | tf_op jit(solution)/shard_map/all_to_all | solution.py:650
  77.9 1.1 %shard_map.137 = (bf16[16,88,128]{2,1,0:T(8,128)(2,1)}, bf16[4,2,3,4,2,16,128]{6,5,4,3,2,1,0:T(8,128)(2,1)}) custom-call(bf16[8,88,128]{2,1,0:T(8,128)(2,1)S(1)} %all-to-all-done.1.pieces_ref, f32[8,128]{1,0:T(8,128)S(1)} %shard_map.136.flag_ref, bf16[2,3,4,2,16,128]{5,4,3,2,1,0:T(8,128)(2,1)S(1)} %get-tuple-element.48.own_ref, ...), custom_call_target="tpu_custom_call" | custom-call | flops 226492416 | bytes 2097152 | tf_op jit(solution)/shard_map/pallas_call | solution.py:542
  79.0 4.6 %collective-permute-start.10 = (bf16[4,2,3,4,2,16,128]{6,5,4,3,2,1,0:T(8,128)(2,1)}, bf16[4,2,3,4,2,16,128]{6,5,4,3,2,1,0:T(8,128)(2,1)}, u32[]{:S(2)}, u32[]{:S(2)}) collective-permute-start(bf16[4,2,3,4,2,16,128]{6,5,4,3,2,1,0:T(8,128)(2,1)} %get-tuple-element.49), channel_id=1, source_target_pairs={{0,16},{16,0},{1,17},{17,1},{2,18},{18,2},{3,19},{19,3},{4,20},{20... | collective-permute-start | bytes 2359304 | tf_op jit(solution)/shard_map/ppermute | solution.py:23
  83.6 3.5 %all-to-all-start.2 = ((bf16[16,88,128]{2,1,0:T(8,128)(2,1)}), bf16[16,88,128]{2,1,0:T(8,128)(2,1)S(1)}, u32[]{:S(2)}, u32[]{:S(2)}) async-start(bf16[16,88,128]{2,1,0:T(8,128)(2,1)} %get-tuple-element.52), calls=%async_computation.2 | async-start | bytes 720896 | tf_op jit(solution)/shard_map/all_to_all | solution.py:657
  87.1 0.0 collective-permute-done.10
  87.1 1.2 %copy-done.7 = f32[960,256]{1,0:T(8,128)S(1)} copy-done((f32[960,256]{1,0:T(8,128)S(1)}, f32[960,256]{1,0:T(8,128)}, u32[]{:S(2)}) %copy-start.7) | copy-done | bytes 983064
  88.3 3.8 %shard_map.138 = (bf16[3,16,16,128]{3,2,1,0:T(8,128)(2,1)}, f32[8,128]{1,0:T(8,128)S(1)}) custom-call(s32[296]{0:T(512)S(1)} %copy-done.5, bf16[192,192]{1,0:T(8,128)(2,1)S(1)} %copy-done.3, bf16[24,4,2,16,128]{4,3,2,1,0:T(8,128)(2,1)} %bitcast.14.mine_ref, bf16[24,4,2,16,128]{4,3,2,1,0:T(8,128)(2,1)} %bitcast.15.other_ref, bf16[1152,768]{1,0:T(8,128)(2,1)S(1)} %copy-done.1, ...), custom_call_target="tpu_custom_call" | custom-call | flops 22649241600 | bytes 2097152 | tf_op jit(solution)/shard_map/pallas_call | solution.py:542
  92.2 3.8 %all-to-all-done.2 = bf16[16,88,128]{2,1,0:T(8,128)(2,1)S(1)} async-done(((bf16[16,88,128]{2,1,0:T(8,128)(2,1)}), bf16[16,88,128]{2,1,0:T(8,128)(2,1)S(1)}, u32[]{:S(2)}, u32[]{:S(2)}) %all-to-all-start.2) | async-done | bytes 360480 | tf_op jit(solution)/shard_map/all_to_all | solution.py:657
  96.0 1.7 %collective-permute-start.11 = (bf16[1408,128]{1,0:T(8,128)(2,1)S(1)}, bf16[1408,128]{1,0:T(8,128)(2,1)S(1)}, u32[]{:S(2)}, u32[]{:S(2)}) collective-permute-start(bf16[1408,128]{1,0:T(8,128)(2,1)S(1)} %shard_map.139.mine_ref), channel_id=1, source_target_pairs={{0,16},{16,0},{1,17},{17,1},{2,18},{18,2},{3,19},{19,3},{4,20},{20... | collective-permute-start | bytes 1081352 | tf_op jit(solution)/shard_map/ppermute | solution.py:23
  97.7 1.3 %collective-permute-done.11.other_ref = bf16[1408,128]{1,0:T(8,128)(2,1)S(1)} collective-permute-done((bf16[1408,128]{1,0:T(8,128)(2,1)S(1)}, bf16[1408,128]{1,0:T(8,128)(2,1)S(1)}, u32[]{:S(2)}, u32[]{:S(2)}) %collective-permute-start.11) | collective-permute-done | bytes 360480 | tf_op jit(solution)/shard_map/ppermute | solution.py:23
  99.0 1.3 %shard_map.140 = (f32[9,128,128]{2,1,0:T(8,128)}, f32[9,128,128]{2,1,0:T(8,128)}, f32[4,128,128]{2,1,0:T(8,128)}) custom-call(bf16[1408,128]{1,0:T(8,128)(2,1)S(1)} %shard_map.139.mine_ref, bf16[1408,128]{1,0:T(8,128)(2,1)S(1)} %collective-permute-done.11.other_ref), custom_call_target="tpu_custom_call" | custom-call | flops 226492416 | bytes 2097152 | tf_op jit(solution)/shard_map/pallas_call | solution.py:542
  (15 shorter events, 0.1 us)
Async XLA Ops:
  0.6 0.9 copy-start.8
  1.6 14.2 %collective-permute-start = (bf16[3,4,2,16,128]{4,3,2,1,0:T(8,128)(2,1)S(1)}, bf16[3,4,2,16,128]{4,3,2,1,0:T(8,128)(2,1)S(1)}, u32[]{:S(2)}, u32[]{:S(2)}) collective-permute-start(bf16[3,4,2,16,128]{4,3,2,1,0:T(8,128)(2,1)S(1)} %shard_map.129.own_ref), channel_id=1, source_target_pairs={{0,32},{32,0},{1,33},{33,1},{2,34},{34,2},{3,35},{35,3},{4,36},{36... | collective-permute-start | bytes 294920 | tf_op jit(solution)/shard_map/ppermute | solution.py:28
  15.8 20.2 %copy-start = (bf16[1152,896]{1,0:T(8,128)(2,1)S(1)}, bf16[1152,896]{1,0:T(8,128)(2,1)}, u32[]{:S(2)}) copy-start(bf16[1152,896]{1,0:T(8,128)(2,1)} %get-tuple-element.33.early_ref) | copy-start | bytes 6193156
  15.8 20.2 %copy-start.3 = (bf16[192,192]{1,0:T(8,128)(2,1)S(1)}, bf16[192,192]{1,0:T(8,128)(2,1)}, u32[]{:S(2)}) copy-start(bf16[192,192]{1,0:T(8,128)(2,1)} %get-tuple-element.32.turn_ref) | copy-start | bytes 221188
  15.8 0.8 copy-start.4
  16.7 19.4 %copy-start.5 = (s32[296]{0:T(512)S(1)}, s32[296]{0:T(512)}, u32[]{:S(2)}) copy-start(s32[296]{0:T(512)} %get-tuple-element.31.index_ref) | copy-start | bytes 3556
  17.2 5.5 %collective-permute-start.1 = (bf16[2,3,4,2,16,128]{5,4,3,2,1,0:T(8,128)(2,1)S(1)}, bf16[2,3,4,2,16,128]{5,4,3,2,1,0:T(8,128)(2,1)S(1)}, u32[]{:S(2)}, u32[]{:S(2)}) collective-permute-start(bf16[2,3,4,2,16,128]{5,4,3,2,1,0:T(8,128)(2,1)S(1)} %shard_map.130.own_ref), channel_id=1, source_target_pairs={{0,64},{64,0},{128,192},{192,128},{1,65},{65,1},{129,193},{193,129... | collective-permute-start | bytes 589832 | tf_op jit(solution)/shard_map/ppermute | solution.py:28
  18.6 10.9 %collective-permute-start.2 = (bf16[2,3,4,2,16,128]{5,4,3,2,1,0:T(8,128)(2,1)S(1)}, bf16[2,3,4,2,16,128]{5,4,3,2,1,0:T(8,128)(2,1)S(1)}, u32[]{:S(2)}, u32[]{:S(2)}) collective-permute-start(bf16[2,3,4,2,16,128]{5,4,3,2,1,0:T(8,128)(2,1)S(1)} %shard_map.130.own_ref), channel_id=1, source_target_pairs={{0,128},{64,192},{128,0},{192,64},{1,129},{65,193},{129,1},{193,65... | collective-permute-start | bytes 589832 | tf_op jit(solution)/shard_map/ppermute | solution.py:28
  21.2 11.3 %collective-permute-start.3 = (bf16[2,3,4,2,16,128]{5,4,3,2,1,0:T(8,128)(2,1)S(1)}, bf16[2,3,4,2,16,128]{5,4,3,2,1,0:T(8,128)(2,1)S(1)}, u32[]{:S(2)}, u32[]{:S(2)}) collective-permute-start(bf16[2,3,4,2,16,128]{5,4,3,2,1,0:T(8,128)(2,1)S(1)} %shard_map.130.own_ref), channel_id=1, source_target_pairs={{0,192},{64,128},{128,64},{192,0},{1,193},{65,129},{129,65},{193,1... | collective-permute-start | bytes 589832 | tf_op jit(solution)/shard_map/ppermute | solution.py:28
  32.6 3.5 %collective-permute-start.4 = (bf16[4,2,3,4,2,16,128]{6,5,4,3,2,1,0:T(8,128)(2,1)S(1)}, bf16[4,2,3,4,2,16,128]{6,5,4,3,2,1,0:T(8,128)(2,1)S(1)}, u32[]{:S(2)}, u32[]{:S(2)}) collective-permute-start(bf16[4,2,3,4,2,16,128]{6,5,4,3,2,1,0:T(8,128)(2,1)S(1)} %shard_map.131), channel_id=1, source_target_pairs={{0,16},{16,0},{1,17},{17,1},{2,18},{18,2},{3,19},{19,3},{4,20},{20... | collective-permute-start | bytes 2359304 | tf_op jit(solution)/shard_map/ppermute | solution.py:23
  36.0 1.1 %copy-start.2 = (f32[768,256]{1,0:T(8,128)S(1)}, f32[768,256]{1,0:T(8,128)}, u32[]{:S(2)}) copy-start(f32[768,256]{1,0:T(8,128)} %get-tuple-element.34.staged_ref) | copy-start | bytes 2359300
  37.2 3.3 %copy-start.1 = (bf16[1152,768]{1,0:T(8,128)(2,1)S(1)}, bf16[1152,768]{1,0:T(8,128)(2,1)}, u32[]{:S(2)}) copy-start(bf16[1152,768]{1,0:T(8,128)(2,1)} %get-tuple-element.36.late_ref) | copy-start | bytes 5308420
  44.6 3.2 %copy-start.6 = (f32[960,256]{1,0:T(8,128)}, f32[960,256]{1,0:T(8,128)S(1)}, u32[]{:S(2)}) copy-start(f32[960,256]{1,0:T(8,128)S(1)} %get-tuple-element.50.rest_ref) | copy-start | bytes 2949124
  44.7 2.3 %collective-permute-start.5 = (f32[1408,128]{1,0:T(8,128)S(1)}, f32[1408,128]{1,0:T(8,128)S(1)}, u32[]{:S(2)}, u32[]{:S(2)}) collective-permute-start(f32[1408,128]{1,0:T(8,128)S(1)} %slice_bitcast_fusion), channel_id=1, source_target_pairs={{0,16},{16,0},{1,17},{17,1},{2,18},{18,2},{3,19},{19,3},{4,20},{20... | collective-permute-start | bytes 2162696 | tf_op jit(solution)/shard_map/ppermute | solution.py:23
  45.1 8.2 %collective-permute-start.6 = (bf16[3,4,2,16,128]{4,3,2,1,0:T(8,128)(2,1)S(1)}, bf16[3,4,2,16,128]{4,3,2,1,0:T(8,128)(2,1)S(1)}, u32[]{:S(2)}, u32[]{:S(2)}) collective-permute-start(bf16[3,4,2,16,128]{4,3,2,1,0:T(8,128)(2,1)S(1)} %get-tuple-element.46.own_ref), channel_id=1, source_target_pairs={{0,32},{32,0},{1,33},{33,1},{2,34},{34,2},{3,35},{35,3},{4,36},{36... | collective-permute-start | bytes 294920 | tf_op jit(solution)/shard_map/ppermute | solution.py:28
  47.8 12.9 %all-to-all-start = ((bf16[16,88,128]{2,1,0:T(8,128)(2,1)}), bf16[16,88,128]{2,1,0:T(8,128)(2,1)S(1)}, u32[]{:S(2)}, u32[]{:S(2)}) async-start(bf16[16,88,128]{2,1,0:T(8,128)(2,1)} %bitcast.13), calls=%async_computation | async-start | bytes 720896 | tf_op jit(solution)/shard_map/all_to_all | solution.py:643
  61.4 7.9 %collective-permute-start.7 = (bf16[2,3,4,2,16,128]{5,4,3,2,1,0:T(8,128)(2,1)S(1)}, bf16[2,3,4,2,16,128]{5,4,3,2,1,0:T(8,128)(2,1)S(1)}, u32[]{:S(2)}, u32[]{:S(2)}) collective-permute-start(bf16[2,3,4,2,16,128]{5,4,3,2,1,0:T(8,128)(2,1)S(1)} %get-tuple-element.48.own_ref), channel_id=1, source_target_pairs={{0,64},{64,0},{128,192},{192,128},{1,65},{65,1},{129,193},{193,129... | collective-permute-start | bytes 589832 | tf_op jit(solution)/shard_map/ppermute | solution.py:28
  61.7 8.6 %collective-permute-start.8 = (bf16[2,3,4,2,16,128]{5,4,3,2,1,0:T(8,128)(2,1)S(1)}, bf16[2,3,4,2,16,128]{5,4,3,2,1,0:T(8,128)(2,1)S(1)}, u32[]{:S(2)}, u32[]{:S(2)}) collective-permute-start(bf16[2,3,4,2,16,128]{5,4,3,2,1,0:T(8,128)(2,1)S(1)} %get-tuple-element.48.own_ref), channel_id=1, source_target_pairs={{0,128},{64,192},{128,0},{192,64},{1,129},{65,193},{129,1},{193,65... | collective-permute-start | bytes 589832 | tf_op jit(solution)/shard_map/ppermute | solution.py:28
  63.2 10.6 %collective-permute-start.9 = (bf16[2,3,4,2,16,128]{5,4,3,2,1,0:T(8,128)(2,1)S(1)}, bf16[2,3,4,2,16,128]{5,4,3,2,1,0:T(8,128)(2,1)S(1)}, u32[]{:S(2)}, u32[]{:S(2)}) collective-permute-start(bf16[2,3,4,2,16,128]{5,4,3,2,1,0:T(8,128)(2,1)S(1)} %get-tuple-element.48.own_ref), channel_id=1, source_target_pairs={{0,192},{64,128},{128,64},{192,0},{1,193},{65,129},{129,65},{193,1... | collective-permute-start | bytes 589832 | tf_op jit(solution)/shard_map/ppermute | solution.py:28
  65.3 12.6 %all-to-all-start.1 = ((bf16[8,88,128]{2,1,0:T(8,128)(2,1)}), bf16[8,88,128]{2,1,0:T(8,128)(2,1)S(1)}, u32[]{:S(2)}, u32[]{:S(2)}) async-start(bf16[8,88,128]{2,1,0:T(8,128)(2,1)} %get-tuple-element.47), calls=%async_computation.1 | async-start | bytes 360448 | tf_op jit(solution)/shard_map/all_to_all | solution.py:650
  79.0 8.1 %collective-permute-start.10 = (bf16[4,2,3,4,2,16,128]{6,5,4,3,2,1,0:T(8,128)(2,1)}, bf16[4,2,3,4,2,16,128]{6,5,4,3,2,1,0:T(8,128)(2,1)}, u32[]{:S(2)}, u32[]{:S(2)}) collective-permute-start(bf16[4,2,3,4,2,16,128]{6,5,4,3,2,1,0:T(8,128)(2,1)} %get-tuple-element.49), channel_id=1, source_target_pairs={{0,16},{16,0},{1,17},{17,1},{2,18},{18,2},{3,19},{19,3},{4,20},{20... | collective-permute-start | bytes 2359304 | tf_op jit(solution)/shard_map/ppermute | solution.py:23
  83.6 12.4 %all-to-all-start.2 = ((bf16[16,88,128]{2,1,0:T(8,128)(2,1)}), bf16[16,88,128]{2,1,0:T(8,128)(2,1)S(1)}, u32[]{:S(2)}, u32[]{:S(2)}) async-start(bf16[16,88,128]{2,1,0:T(8,128)(2,1)} %get-tuple-element.52), calls=%async_computation.2 | async-start | bytes 720896 | tf_op jit(solution)/shard_map/all_to_all | solution.py:657
  87.1 1.2 %copy-start.7 = (f32[960,256]{1,0:T(8,128)S(1)}, f32[960,256]{1,0:T(8,128)}, u32[]{:S(2)}) copy-start(f32[960,256]{1,0:T(8,128)} %copy-done.6) | copy-start | bytes 2949124
  96.0 3.0 %collective-permute-start.11 = (bf16[1408,128]{1,0:T(8,128)(2,1)S(1)}, bf16[1408,128]{1,0:T(8,128)(2,1)S(1)}, u32[]{:S(2)}, u32[]{:S(2)}) collective-permute-start(bf16[1408,128]{1,0:T(8,128)(2,1)S(1)} %shard_map.139.mine_ref), channel_id=1, source_target_pairs={{0,16},{16,0},{1,17},{17,1},{2,18},{18,2},{3,19},{19,3},{4,20},{20... | collective-permute-start | bytes 1081352 | tf_op jit(solution)/shard_map/ppermute | solution.py:23

commit v5 on v4

--- a/solution.py
+++ b/solution.py
@@ -54,10 +54,6 @@
     return jnp.dot(left, right, preferred_element_type=F32)
 
 
-def dot_rows(left, right):
-    return lax.dot_general(left, right, (((0,), (0,)), ((), ())), preferred_element_type=F32)
-
-
 def turned(turn, rows):
     high = rows.astype(BF16)
     low = (rows - high.astype(F32)).astype(BF16)
@@ -151,11 +147,58 @@
 W2_BACK, W1_BACK, ADJOINT = slice(0, 128), slice(128, 256), slice(256, 768)
 
 
+def index_kernel(near_ref, code_ref, slot_ref, index_ref, turn_hbm, turn_ref, sems):
+    total = slot_ref.shape[0]
+    tiles = 3
+    core = lax.axis_index("c")
+    at_y = lax.axis_index("y")
+    at_z = lax.axis_index("z")
+    first = ((at_y * 2 + at_z) * 2 + core) * tiles
+
+    def look(i, found):
+        here = slot_ref[i]
+        return tuple(jnp.where(here == first + k, i, found[k]) for k in range(tiles))
+
+    own = lax.fori_loop(0, total, look, (jnp.int32(0),) * tiles, unroll=8)
+
+    def place(at, tile):
+        slot = slot_ref[tile]
+        owner = (slot * 171) >> 9
+        local = slot - owner * tiles
+        chip = ((owner >> 2) ^ at_y) * 2 + (((owner >> 1) & 1) ^ at_z)
+        index_ref[at] = (owner + core) & 1
+        index_ref[at + 1] = chip * tiles + local
+
+    column = lax.broadcasted_iota(jnp.int32, (EDGE, 12 * EDGE), 1)
+    row = lax.broadcasted_iota(jnp.int32, (EDGE, 12 * EDGE), 0)
+    for n in range(12):
+        side, k = n // tiles, n % tiles
+        near = near_ref[side, own[k]]
+        code = code_ref[side, own[k]]
+        near_side = code >> 1
+        reverse = code & 1
+        place(near_at(n), near)
+        index_ref[near_at(n) + 2] = near_side
+        source = jnp.where(reverse == 1, EDGE - 1 - row, row) + n * EDGE
+        turn_ref[strip(n), :] = jnp.where(column == source, 1.0, 0.0).astype(F32).astype(BF16)
+        upright = near_side & 1
+        far = jnp.where((near_side == 1) | (near_side == 2), 1, 0)
+        for h in range(2):
+            lateral = jnp.where(upright == 1, (0, 2)[h], (3, 1)[h])
+            at = lateral_at(2 * n + h)
+            place(at, near_ref[lateral, near])
+            lateral_code = code_ref[lateral, near]
+            index_ref[at + 2] = lateral_code >> 1
+            index_ref[at + 3] = (far + lateral_code) & 1
+
+    finish(fetch([turn_ref], [turn_hbm], sems))
+
+
 def stage_kernel(
-    near_ref, code_ref, slot_ref, x_hbm, skip_hbm, down_hbm, w1_hbm, w2_hbm, wc_hbm,
-    index_ref, turn_hbm, early_hbm, late_hbm, cells_hbm,
+    index_ref, x_hbm, skip_hbm, down_hbm, w1_hbm, w2_hbm, wc_hbm,
+    flag_ref, early_hbm, late_hbm, cells_hbm,
     x_ref, skip_ref, down_ref, w1_ref, w2_ref, wc_ref,
-    turn_ref, early_ref, late_ref, cells_ref,
+    early_ref, late_ref, cells_ref,
     pad_ref, cot_ref, cols_ref, wc_back_ref, in_sems, out_sems,
 ):
     arrivals = fetch(
@@ -163,97 +206,59 @@
         (w1_ref, w2_ref, wc_ref, x_ref, down_ref, skip_ref),
         in_sems,
     )
+    for at in range(8):
+        flag_ref[at] = index_ref[at]
     pad_ref[...] = jnp.zeros_like(pad_ref)
     early_ref[704:, TAIL] = jnp.zeros_like(early_ref[704:, TAIL])
     early_ref[768:, X] = jnp.zeros_like(early_ref[768:, X])
-    total = slot_ref.shape[0]
-    tiles = 3
-    core = lax.axis_index("c")
-    at_y = lax.axis_index("y")
-    at_z = lax.axis_index("z")
-    first = ((at_y * 2 + at_z) * 2 + core) * tiles
-
-    def look(i, found):
-        here = slot_ref[i]
-        return tuple(jnp.where(here == first + k, i, found[k]) for k in range(tiles))
-
-    own = lax.fori_loop(0, total, look, (jnp.int32(0),) * tiles)
-
-    def place(at, tile):
-        slot = slot_ref[tile]
-        owner = slot // tiles
-        local = slot % tiles
-        chip = ((owner // 4) ^ at_y) * 2 + ((owner // 2) % 2 ^ at_z)
-        index_ref[at] = (owner + core) % 2
-        index_ref[at + 1] = chip * tiles + local
-
-    column = lax.broadcasted_iota(jnp.int32, (EDGE, 12 * EDGE), 1)
-    row = lax.broadcasted_iota(jnp.int32, (EDGE, 12 * EDGE), 0)
-    for n in range(12):
-        side, k = n // tiles, n % tiles
-        near = near_ref[side, own[k]]
-        code = code_ref[side, own[k]]
-        near_side = code // 2
-        reverse = code % 2
-        place(near_at(n), near)
-        index_ref[near_at(n) + 2] = near_side
-        source = jnp.where(reverse == 1, EDGE - 1 - row, row) + n * EDGE
-        turn_ref[strip(n), :] = jnp.where(column == source, 1.0, 0.0).astype(F32).astype(BF16)
-        upright = near_side % 2
-        far = jnp.where((near_side == 1) | (near_side == 2), 1, 0)
-        for h in range(2):
-            lateral = jnp.where(upright == 1, (0, 2)[h], (3, 1)[h])
-            at = lateral_at(2 * n + h)
-            place(at, near_ref[lateral, near])
-            lateral_code = code_ref[lateral, near]
-            index_ref[at + 2] = lateral_code // 2
-            index_ref[at + 3] = (far + lateral_code) % 2
-
     finish(arrivals)
-
-    def flip(block):
-        return jnp.transpose(block.astype(F32)).astype(BF16)
-
-    for a in range(3):
-        for b in range(3):
-            block = w1_ref[lanes(3 * a + b), :]
-            first_flip = flip(block)
-            second_flip = flip(w2_ref[lanes(3 * a + b), :])
-            back = lanes(8 - 3 * a - b)
-            late_ref[back, W1_BACK] = first_flip
-            late_ref[back, W2_BACK] = second_flip
-            for side in range(4):
-                for r in range(3):
-                    for k in range(3):
-                        if frame_source(side, r, k) != (a, b):
-                            continue
-                        early_ref[lanes(3 * r + k), lanes(side)] = block
-                        if r == 0:
-                            late_ref[lanes(6 + k), lanes(2 + side)] = first_flip
-                        if r <= 1:
-                            late_ref[lanes(3 * r + k), lanes(2 + side)] = second_flip
+    for side in range(4):
+        for r in range(3):
+            for k in range(3):
+                a, b = frame_source(side, r, k)
+                early_ref[lanes(3 * r + k), lanes(side)] = w1_ref[lanes(3 * a + b), :]
     early_ref[:, W2] = w2_ref[...]
     early_ref[:512, TAIL] = wc_ref[...]
     down = down_ref[...]
     early_ref[512:704, TAIL] = down
     x_rows = as_rows(x_ref[...])
     early_ref[:768, X] = x_rows
-    departures = fetch(
-        (early_ref, late_ref, turn_ref), (early_hbm, late_hbm, turn_hbm), out_sems
-    )
+    departures = fetch([early_ref], [early_hbm], out_sems)
+
+    def flip(block):
+        return jnp.transpose(block.astype(F32)).astype(BF16)
+
+    for a in range(3):
+        for b in range(3):
+            first_flip = flip(w1_ref[lanes(3 * a + b), :])
+            second_flip = flip(w2_ref[lanes(3 * a + b), :])
+            back = lanes(8 - 3 * a - b)
+            late_ref[back, W1_BACK] = first_flip
+            late_ref[back, W2_BACK] = second_flip
+            for side in range(4):
+                for r in range(2):
+                    for k in range(3):
+                        if frame_source(side, r, k) != (a, b):
+                            continue
+                        if r == 0:
+                            late_ref[lanes(6 + k), lanes(2 + side)] = first_flip
+                        late_ref[lanes(3 * r + k), lanes(2 + side)] = second_flip
+    last = pltpu.make_async_copy(late_ref, late_hbm, out_sems.at[1])
+    last.start()
+    departures.append(last)
     for at in range(4):
         wc_back_ref[:, lanes(at)] = flip(wc_ref[lanes(at), :])
     spread_down = dot(down, wc_back_ref[...])
     half = EDGE // 2
     for a in range(2):
         for b in range(2):
-            part = spread_down[:, lanes(2 * a + b)].reshape(tiles, half, half, CH)
+            part = spread_down[:, lanes(2 * a + b)].reshape(-1, half, half, CH)
             cot_ref[:, pl.ds(a, half, 2), pl.ds(b, half, 2), :] = part
     cells_ref[:, lanes(1)] = as_rows(cot_ref[...] + skip_ref[...].astype(F32))
     fill_pad(pad_ref, x_rows.astype(F32))
     windows(pad_ref, cols_ref)
     cells_ref[:, lanes(0)] = dot(cols_ref[...], w1_ref[...])
-    last = pltpu.make_async_copy(cells_ref, cells_hbm, out_sems.at[3])
+    last = pltpu.make_async_copy(cells_ref, cells_hbm, out_sems.at[2])
     last.start()
     finish(departures + [last])
 
@@ -350,17 +355,20 @@
 
     def put_grad(at, block):
         half = at // 11
-        grad_ref[jnp.where(core == half, 0, 1), lanes(at % 11), :] = block
+        grad_ref[jnp.where(core == half, 0, 1), lanes(at % 11), :] = jnp.transpose(block)
+
+    def across_rows(rows):
+        return jnp.transpose(rows.astype(F32)).astype(BF16)
 
     split_ref[...] = jnp.zeros_like(split_ref)
     turn = turn_ref[...]
-    down_grad = dot_rows(down_cols_ref[...], early_ref[512:704, TAIL])
+    down_grad = dot(across_rows(early_ref[512:704, TAIL]), down_cols_ref[...])
     for at in range(4):
-        put_grad(18 + at, down_grad[lanes(at)])
+        put_grad(18 + at, down_grad[:, lanes(at)])
     delta = delta_ref[...]
-    second_grad = dot_rows(cols2_ref[...], delta)
+    second_grad = dot(across_rows(delta), cols2_ref[...])
     for at in range(9):
-        put_grad(9 + at, second_grad[lanes(at)])
+        put_grad(9 + at, second_grad[:, lanes(at)])
     pad_ref[...] = jnp.zeros_like(pad_ref)
     fill_pad(pad_ref, delta.astype(F32))
     windows(pad_ref, cols3_ref)
@@ -380,19 +388,19 @@
     for n in range(12):
         chosen = pl.ds(pl.multiple_of(index_ref[near_at(n) + 2] * CH, CH), CH)
         split_ref[strip(n), chosen] = sent_delta[strip(n)]
-    sent_grad = dot_rows(strip_ref[...], split_ref[...])
+    sent_grad = dot(across_rows(split_ref[...]), strip_ref[...])
     fill_pad(pad_ref, early_ref[:768, X].astype(F32))
     put_seams(pad_ref, seam_ref[...])
     windows(pad_ref, cols_ref)
-    first_grad = dot_rows(cols_ref[...], inner_delta)
+    first_grad = dot(across_rows(inner_delta), cols_ref[...])
     for a in range(3):
         for b in range(3):
-            block = first_grad[lanes(3 * a + b)]
+            block = first_grad[:, lanes(3 * a + b)]
             for side in range(4):
                 for r in range(3):
                     for k in range(3):
                         if frame_source(side, r, k) == (a, b):
-                            block = block + sent_grad[lanes(3 * r + k), lanes(side)]
+                            block = block + sent_grad[lanes(side), lanes(3 * r + k)]
             put_grad(3 * a + b, block)
 
 
@@ -456,9 +464,11 @@
     out_ref[...] = as_cells(cells_ref[...]).astype(BF16)
 
 
-def first_pair_kernel(own_ref, across_ref, index_ref, pair_ref):
-    pair_ref[0] = own_ref[...]
-    pair_ref[1] = across_ref[...]
+def first_table_kernel(*refs):
+    table_ref = refs[-1]
+    for at in range(4):
+        table_ref[at, 0] = refs[at][...]
+        table_ref[at, 1] = refs[4 + at][...]
 
 
 def gate_kernel(*refs):
@@ -566,27 +576,43 @@
         conv2_weight.reshape(9 * CH, CH),
         coarse_kernel_weight.reshape(4 * CH, CH),
     ]
+    turn_shape = shape((strips, strips), BF16)
+    index, turn = call(
+        index_kernel,
+        (shape((296,), jnp.int32), turn_shape),
+        [face_neighbours.T, seam_codes.T, tile_slots],
+        [turn_shape],
+        (1,),
+        specs=[smem] * 3,
+        out_specs=(smem, hbm),
+        cost=4,
+        room=60,
+    )
     staged = (
-        shape((strips, strips), BF16),
         shape((9 * CH, 7 * CH), BF16),
         shape((9 * CH, 6 * CH), BF16),
         shape((cells, 2 * CH), F32),
     )
-    index, turn, early, late, staged_cells = call(
+    ready, early, late, staged_cells = call(
         stage_kernel,
-        (shape((296,), jnp.int32),) + staged,
-        [face_neighbours.T, seam_codes.T, tile_slots] + operands,
+        (shape((8,), jnp.int32),) + staged,
+        [index] + operands,
         tuple(operands) + staged
         + (pad, shape(x.shape, F32), all_cols, shape((CH, 4 * CH), BF16)),
         (len(operands), len(staged)),
-        specs=[smem] * 3 + [hbm] * 6,
-        out_specs=(smem,) + (hbm,) * 4,
-        cost=4,
+        specs=[smem] + [hbm] * 6,
+        out_specs=(smem,) + (hbm,) * 3,
+        cost=100,
         room=60,
     )
-    pair = call(first_pair_kernel, shape((2,) + ring.shape, BF16), [own_ring, across, index], specs=[vmem, vmem, smem])
-    along = [swap_apart(pair, "y", apart) for apart in (1, 2, 3)]
-    mine = call(table_kernel, shape((4,) + pair.shape, BF16), [pair] + along)
+    near_rings = [own_ring] + [swap_apart(own_ring, "y", apart) for apart in (1, 2, 3)]
+    far_rings = [across] + [swap_apart(across, "y", apart) for apart in (1, 2, 3)]
+    mine = call(
+        first_table_kernel,
+        shape((4, 2) + ring.shape, BF16),
+        near_rings + far_rings + [index, ready],
+        specs=[vmem] * 8 + [smem] * 2,
+    )
     other = swap_core(mine)
 
     def table(block):

time: 101 us -> 98.3 us (0.973)
  waiting for transfers between devices: 37.1 us -> 23.7 us
  starting transfers between devices: 36.1 us -> 45.7 us
    ppermute x8 -> x11, waiting for transfers between devices: 17.1 us -> 5.12 us  [swap_apart(): return lax.ppermute(block, axis, [(i, i ^ apart) for i in range(number)])]
    ppermute x8 -> x11, starting transfers between devices: 16.1 us -> 21.9 us  [swap_apart(): return lax.ppermute(block, axis, [(i, i ^ apart) for i in range(number)])]
    all_to_all x1, starting transfers between devices: 4.12 us -> 6.63 us  [shards(): pieces = lax.all_to_all(kept.reshape(plane, part, CH), PLANE, 0, 0)]
    ppermute x4, waiting for transfers between devices: 4.66 us -> 3.22 us  [swap_core(): return lax.ppermute(block, 'c', [(0, 1), (1, 0)])]
    ppermute x4, starting transfers between devices: 8.27 us -> 9.35 us  [swap_core(): return lax.ppermute(block, 'c', [(0, 1), (1, 0)])]
  transfers between devices with their start and end apart: 15 -> 18, of which waited for: 12 -> 7; matrix products, arithmetic and copies ran while one was open for 1% -> 1% of each run, Pallas kernels for 10% -> 12%
where the time goes in v5:
time: 98.3 us; the launch traced here: 97.7 us
  starting transfers between devices  45.7 us (46%)
  waiting for transfers between devices  23.7 us (24%)
  Pallas kernels  22.2 us (23%)
  local copies, waits for them, and re-layouts  4.48 us (5%)
    pallas_call x13, Pallas kernels, call(): pl.pallas_call(kernel, out_shape=outs, in_specs=specs or [vmem] * len(ope...  22.2 us
    ppermute x11, starting transfers between devices, swap_apart(): return lax.ppermute(block, axis, [(i, i ^ apart) for i in range(number)])  21.9 us
    ppermute x4, starting transfers between devices, swap_core(): return lax.ppermute(block, 'c', [(0, 1), (1, 0)])  9.35 us
    all_to_all x1, waiting for transfers between devices, shards(): pieces = lax.all_to_all(kept.reshape(plane, part, CH), PLANE, 0, 0)  8.03 us
    all_to_all x1, starting transfers between devices, shards(): pieces = lax.all_to_all(kept.reshape(plane, part, CH), PLANE, 0, 0)  6.63 us
    ppermute x11, waiting for transfers between devices, swap_apart(): return lax.ppermute(block, axis, [(i, i ^ apart) for i in range(number)])  5.12 us
    unnamed x18, local copies, waits for them, and re-layouts  4.43 us
    all_to_all x1, starting transfers between devices, shards(): pieces = lax.all_to_all(copies, DEPTH, 0, 0)  4.25 us
  transfers between devices with their start and end apart: 18, of which 7 were waited for; matrix products, arithmetic and copies ran while one was open for 1% of the time, Pallas kernels for 12%

profile of v5, /device:TPU:1, one launch (start us, length us, event | category | flops | bytes accessed | tf_op | source)
XLA Modules:
  0.0 97.7 jit_solution(9314038165594033599)
XLA Ops:
  0.6 0.0 copy-start.8
  0.6 0.9 copy-done.8
  1.6 0.1 shard_map.129.refs_0_
  1.6 7.8 %collective-permute-start.3 = (bf16[3,4,2,16,128]{4,3,2,1,0:T(8,128)(2,1)S(1)}, bf16[3,4,2,16,128]{4,3,2,1,0:T(8,128)(2,1)S(1)}, u32[]{:S(2)}, u32[]{:S(2)}) collective-permute-start(bf16[3,4,2,16,128]{4,3,2,1,0:T(8,128)(2,1)S(1)} %shard_map.129.refs_0_), channel_id=1, source_target_pairs={{0,32},{32,0},{1,33},{33,1},{2,34},{34,2},{3,35},{35,3},{4,36},{36... | collective-permute-start | bytes 294920 | tf_op jit(solution)/shard_map/ppermute | solution.py:28
  9.4 1.3 %collective-permute-start = (bf16[3,4,2,16,128]{4,3,2,1,0:T(8,128)(2,1)S(1)}, bf16[3,4,2,16,128]{4,3,2,1,0:T(8,128)(2,1)S(1)}, u32[]{:S(2)}, u32[]{:S(2)}) collective-permute-start(bf16[3,4,2,16,128]{4,3,2,1,0:T(8,128)(2,1)S(1)} %shard_map.129.refs_0_), channel_id=1, source_target_pairs={{0,64},{64,0},{128,192},{192,128},{1,65},{65,1},{129,193},{193,129... | collective-permute-start | bytes 294920 | tf_op jit(solution)/shard_map/ppermute | solution.py:28
  10.7 2.6 %collective-permute-start.1 = (bf16[3,4,2,16,128]{4,3,2,1,0:T(8,128)(2,1)S(1)}, bf16[3,4,2,16,128]{4,3,2,1,0:T(8,128)(2,1)S(1)}, u32[]{:S(2)}, u32[]{:S(2)}) collective-permute-start(bf16[3,4,2,16,128]{4,3,2,1,0:T(8,128)(2,1)S(1)} %shard_map.129.refs_0_), channel_id=1, source_target_pairs={{0,128},{64,192},{128,0},{192,64},{1,129},{65,193},{129,1},{193,65... | collective-permute-start | bytes 294920 | tf_op jit(solution)/shard_map/ppermute | solution.py:28
  13.4 0.0 collective-permute-start.2
  13.4 2.4 %shard_map.128 = (s32[296]{0:T(512)}, bf16[192,192]{1,0:T(8,128)(2,1)}) custom-call(s32[4,48]{1,0:T(4,128)} %bitcast.36, s32[4,48]{1,0:T(4,128)} %bitcast.37, s32[48]{0:T(128)} %slot_ref.1), custom_call_target="tpu_custom_call" | custom-call | flops 905969664 | bytes 2097152 | tf_op jit(solution)/shard_map/pallas_call | solution.py:552
  15.8 0.0 collective-permute-done.3.refs_4_
  15.8 0.1 collective-permute-start.4
  15.9 3.8 %collective-permute-start.5 = (bf16[3,4,2,16,128]{4,3,2,1,0:T(8,128)(2,1)S(1)}, bf16[3,4,2,16,128]{4,3,2,1,0:T(8,128)(2,1)S(1)}, u32[]{:S(2)}, u32[]{:S(2)}) collective-permute-start(bf16[3,4,2,16,128]{4,3,2,1,0:T(8,128)(2,1)S(1)} %collective-permute-done.3.refs_4_), channel_id=1, source_target_pairs={{0,128},{64,192},{128,0},{192,64},{1,129},{65,193},{129,1},{193,65... | collective-permute-start | bytes 294920 | tf_op jit(solution)/shard_map/ppermute | solution.py:28
  19.7 0.0 collective-permute-done.refs_1_
  19.8 0.0 collective-permute-start.6
  19.8 0.0 copy-start.3
  19.8 5.9 %shard_map.130 = (s32[8]{0:T(128)}, bf16[1152,896]{1,0:T(8,128)(2,1)}, bf16[1152,768]{1,0:T(8,128)(2,1)}, f32[768,256]{1,0:T(8,128)}) custom-call(s32[296]{0:T(512)} %get-tuple-element.32.index_ref.refs_8_, bf16[3,16,16,128]{3,2,1,0:T(8,128)(2,1)} %bitcast.28, bf16[3,16,16,128]{3,2,1,0:T(8,128)(2,1)} %bitcast.32, bf16[192,128]{1,0:T(8,128)(2,1)} %bitcast.34, ...), custom_call_target="tpu_custom_call" | custom-call | flops 22649241600 | bytes 2097152 | tf_op jit(solution)/shard_map/pallas_call | solution.py:552
  25.7 0.0 collective-permute-done.1.refs_2_
  25.7 0.0 collective-permute-done.5.refs_6_
  25.7 0.0 collective-permute-done.6.refs_7_
  25.7 0.0 copy-start.5
  25.8 0.7 copy-done.5
  26.5 0.6 shard_map.131
  27.1 2.6 %collective-permute-start.7 = (bf16[4,2,3,4,2,16,128]{6,5,4,3,2,1,0:T(8,128)(2,1)S(1)}, bf16[4,2,3,4,2,16,128]{6,5,4,3,2,1,0:T(8,128)(2,1)S(1)}, u32[]{:S(2)}, u32[]{:S(2)}) collective-permute-start(bf16[4,2,3,4,2,16,128]{6,5,4,3,2,1,0:T(8,128)(2,1)S(1)} %shard_map.131), channel_id=1, source_target_pairs={{0,16},{16,0},{1,17},{17,1},{2,18},{18,2},{3,19},{19,3},{4,20},{20... | collective-permute-start | bytes 2359304 | tf_op jit(solution)/shard_map/ppermute | solution.py:23
  29.7 1.9 %collective-permute-done.7 = bf16[4,2,3,4,2,16,128]{6,5,4,3,2,1,0:T(8,128)(2,1)S(1)} collective-permute-done((bf16[4,2,3,4,2,16,128]{6,5,4,3,2,1,0:T(8,128)(2,1)S(1)}, bf16[4,2,3,4,2,16,128]{6,5,4,3,2,1,0:T(8,128)(2,1)S(1)}, u32[]{:S(2)}, u32[]{:S(2)}) %collective-permute-start.7) | collective-permute-done | bytes 786464 | tf_op jit(solution)/shard_map/ppermute | solution.py:23
  31.6 1.6 %copy-done = bf16[1152,896]{1,0:T(8,128)(2,1)S(1)} copy-done((bf16[1152,896]{1,0:T(8,128)(2,1)S(1)}, bf16[1152,896]{1,0:T(8,128)(2,1)}, u32[]{:S(2)}) %copy-start) | copy-done | bytes 2064408
  33.2 3.3 %shard_map.132 = (bf16[192,128]{1,0:T(8,128)(2,1)}, bf16[3,4,2,16,128]{4,3,2,1,0:T(8,128)(2,1)S(1)}, f32[768,128]{1,0:T(8,128)S(1)}, f32[192,128]{1,0:T(8,128)S(...) custom-call(s32[296]{0:T(512)S(1)} %copy-done.4, ...), custom_call_target="tpu_custom_call" | custom-call | flops 452984832 | bytes 2097152 | tf_op jit(solution)/shard_map/pallas_call | solution.py:552
  36.5 3.0 %shard_map.133 = (f32[2,1408,128]{2,1,0:T(8,128)S(1)}, f32[960,256]{1,0:T(8,128)S(1)}) custom-call(s32[296]{0:T(512)S(1)} %copy-done.4, bf16[192,192]{1,0:T(8,128)(2,1)S(1)} %copy-done.3, bf16[1152,896]{1,0:T(8,128)(2,1)S(1)} %copy-done, bf16[1152,768]{1,0:T(8,128)(2,1)S(1)} %copy-done.1, f32[768,128]{1,0:T(8,128)S(1)} %get-tuple-element.39.pre_ref, ...), custom_call_target="tpu_custom_call" | custom-call | flops 905969664 | bytes 2097152 | tf_op jit(solution)/shard_map/pallas_call | solution.py:552
  39.5 0.5 collective-permute-start.8
  40.0 2.3 %collective-permute-start.9 = (bf16[3,4,2,16,128]{4,3,2,1,0:T(8,128)(2,1)S(1)}, bf16[3,4,2,16,128]{4,3,2,1,0:T(8,128)(2,1)S(1)}, u32[]{:S(2)}, u32[]{:S(2)}) collective-permute-start(bf16[3,4,2,16,128]{4,3,2,1,0:T(8,128)(2,1)S(1)} %get-tuple-element.48.own_ref), channel_id=1, source_target_pairs={{0,32},{32,0},{1,33},{33,1},{2,34},{34,2},{3,35},{35,3},{4,36},{36... | collective-permute-start | bytes 294920 | tf_op jit(solution)/shard_map/ppermute | solution.py:28
  42.3 0.8 fusion
  43.1 6.6 %all-to-all-start = ((bf16[16,88,128]{2,1,0:T(8,128)(2,1)}), bf16[16,88,128]{2,1,0:T(8,128)(2,1)S(1)}, u32[]{:S(2)}, u32[]{:S(2)}) async-start(bf16[16,88,128]{2,1,0:T(8,128)(2,1)} %bitcast.13), calls=%async_computation | async-start | bytes 720896 | tf_op jit(solution)/shard_map/all_to_all | solution.py:669
  49.8 8.0 %all-to-all-done.pieces_ref = bf16[16,88,128]{2,1,0:T(8,128)(2,1)S(1)} async-done(((bf16[16,88,128]{2,1,0:T(8,128)(2,1)}), bf16[16,88,128]{2,1,0:T(8,128)(2,1)S(1)}, u32[]{:S(2)}, u32[]{:S(2)}) %all-to-all-start) | async-done | bytes 360480 | tf_op jit(solution)/shard_map/all_to_all | solution.py:669
  57.8 0.7 shard_map.135
  58.6 0.3 collective-permute-start.10
  58.9 2.3 %collective-permute-start.11 = (bf16[2,3,4,2,16,128]{5,4,3,2,1,0:T(8,128)(2,1)S(1)}, bf16[2,3,4,2,16,128]{5,4,3,2,1,0:T(8,128)(2,1)S(1)}, u32[]{:S(2)}, u32[]{:S(2)}) collective-permute-start(bf16[2,3,4,2,16,128]{5,4,3,2,1,0:T(8,128)(2,1)S(1)} %get-tuple-element.50.own_ref), channel_id=1, source_target_pairs={{0,128},{64,192},{128,0},{192,64},{1,129},{65,193},{129,1},{193,65... | collective-permute-start | bytes 589832 | tf_op jit(solution)/shard_map/ppermute | solution.py:28
  61.2 1.3 %collective-permute-start.12 = (bf16[2,3,4,2,16,128]{5,4,3,2,1,0:T(8,128)(2,1)S(1)}, bf16[2,3,4,2,16,128]{5,4,3,2,1,0:T(8,128)(2,1)S(1)}, u32[]{:S(2)}, u32[]{:S(2)}) collective-permute-start(bf16[2,3,4,2,16,128]{5,4,3,2,1,0:T(8,128)(2,1)S(1)} %get-tuple-element.50.own_ref), channel_id=1, source_target_pairs={{0,192},{64,128},{128,64},{192,0},{1,193},{65,129},{129,65},{193,1... | collective-permute-start | bytes 589832 | tf_op jit(solution)/shard_map/ppermute | solution.py:28
  62.4 4.3 %all-to-all-start.1 = ((bf16[8,88,128]{2,1,0:T(8,128)(2,1)}), bf16[8,88,128]{2,1,0:T(8,128)(2,1)S(1)}, u32[]{:S(2)}, u32[]{:S(2)}) async-start(bf16[8,88,128]{2,1,0:T(8,128)(2,1)} %get-tuple-element.49), calls=%async_computation.1 | async-start | bytes 360448 | tf_op jit(solution)/shard_map/all_to_all | solution.py:676
  66.7 1.7 %collective-permute-done.11.refs_1_.two_ref = bf16[2,3,4,2,16,128]{5,4,3,2,1,0:T(8,128)(2,1)S(1)} collective-permute-done((bf16[2,3,4,2,16,128]{5,4,3,2,1,0:T(8,128)(2,1)S(1)}, bf16[2,3,4,2,16,128]{5,4,3,2,1,0:T(8,128)(2,1)S(1)}, u32[]{:S(2)}, u32[]{:S(2)}) %collective-permute-start.11) | collective-permute-done | bytes 196640 | tf_op jit(solution)/shard_map/ppermute | solution.py:28
  68.3 3.4 %collective-permute-done.12.refs_2_.three_ref = bf16[2,3,4,2,16,128]{5,4,3,2,1,0:T(8,128)(2,1)S(1)} collective-permute-done((bf16[2,3,4,2,16,128]{5,4,3,2,1,0:T(8,128)(2,1)S(1)}, bf16[2,3,4,2,16,128]{5,4,3,2,1,0:T(8,128)(2,1)S(1)}, u32[]{:S(2)}, u32[]{:S(2)}) %collective-permute-start.12) | collective-permute-done | bytes 196640 | tf_op jit(solution)/shard_map/ppermute | solution.py:28
  71.8 3.5 %all-to-all-done.1.pieces_ref = bf16[8,88,128]{2,1,0:T(8,128)(2,1)S(1)} async-done(((bf16[8,88,128]{2,1,0:T(8,128)(2,1)}), bf16[8,88,128]{2,1,0:T(8,128)(2,1)S(1)}, u32[]{:S(2)}, u32[]{:S(2)}) %all-to-all-start.1) | async-done | bytes 180256 | tf_op jit(solution)/shard_map/all_to_all | solution.py:676
  75.2 1.1 %shard_map.137 = (bf16[16,88,128]{2,1,0:T(8,128)(2,1)}, bf16[4,2,3,4,2,16,128]{6,5,4,3,2,1,0:T(8,128)(2,1)}) custom-call(bf16[8,88,128]{2,1,0:T(8,128)(2,1)S(1)} %all-to-all-done.1.pieces_ref, f32[8,128]{1,0:T(8,128)S(1)} %shard_map.136.flag_ref, bf16[2,3,4,2,16,128]{5,4,3,2,1,0:T(8,128)(2,1)S(1)} %get-tuple-element.50.own_ref, ...), custom_call_target="tpu_custom_call" | custom-call | flops 226492416 | bytes 2097152 | tf_op jit(solution)/shard_map/pallas_call | solution.py:552
  76.3 4.6 %collective-permute-start.13 = (bf16[4,2,3,4,2,16,128]{6,5,4,3,2,1,0:T(8,128)(2,1)}, bf16[4,2,3,4,2,16,128]{6,5,4,3,2,1,0:T(8,128)(2,1)}, u32[]{:S(2)}, u32[]{:S(2)}) collective-permute-start(bf16[4,2,3,4,2,16,128]{6,5,4,3,2,1,0:T(8,128)(2,1)} %get-tuple-element.51), channel_id=1, source_target_pairs={{0,16},{16,0},{1,17},{17,1},{2,18},{18,2},{3,19},{19,3},{4,20},{20... | collective-permute-start | bytes 2359304 | tf_op jit(solution)/shard_map/ppermute | solution.py:23
  80.9 3.5 %all-to-all-start.2 = ((bf16[16,88,128]{2,1,0:T(8,128)(2,1)}), bf16[16,88,128]{2,1,0:T(8,128)(2,1)S(1)}, u32[]{:S(2)}, u32[]{:S(2)}) async-start(bf16[16,88,128]{2,1,0:T(8,128)(2,1)} %get-tuple-element.54), calls=%async_computation.2 | async-start | bytes 720896 | tf_op jit(solution)/shard_map/all_to_all | solution.py:683
  84.5 1.2 %copy-done.7 = f32[960,256]{1,0:T(8,128)S(1)} copy-done((f32[960,256]{1,0:T(8,128)S(1)}, f32[960,256]{1,0:T(8,128)}, u32[]{:S(2)}) %copy-start.7) | copy-done | bytes 983064
  85.7 3.8 %shard_map.138 = (bf16[3,16,16,128]{3,2,1,0:T(8,128)(2,1)}, f32[8,128]{1,0:T(8,128)S(1)}) custom-call(s32[296]{0:T(512)S(1)} %copy-done.4, bf16[192,192]{1,0:T(8,128)(2,1)S(1)} %copy-done.3, bf16[24,4,2,16,128]{4,3,2,1,0:T(8,128)(2,1)} %bitcast.14.mine_ref, bf16[24,4,2,16,128]{4,3,2,1,0:T(8,128)(2,1)} %bitcast.15.other_ref, bf16[1152,768]{1,0:T(8,128)(2,1)S(1)} %copy-done.1, ...), custom_call_target="tpu_custom_call" | custom-call | flops 22649241600 | bytes 2097152 | tf_op jit(solution)/shard_map/pallas_call | solution.py:552
  89.5 3.8 %all-to-all-done.2 = bf16[16,88,128]{2,1,0:T(8,128)(2,1)S(1)} async-done(((bf16[16,88,128]{2,1,0:T(8,128)(2,1)}), bf16[16,88,128]{2,1,0:T(8,128)(2,1)S(1)}, u32[]{:S(2)}, u32[]{:S(2)}) %all-to-all-start.2) | async-done | bytes 360480 | tf_op jit(solution)/shard_map/all_to_all | solution.py:683
  93.4 1.7 %collective-permute-start.14 = (bf16[1408,128]{1,0:T(8,128)(2,1)S(1)}, bf16[1408,128]{1,0:T(8,128)(2,1)S(1)}, u32[]{:S(2)}, u32[]{:S(2)}) collective-permute-start(bf16[1408,128]{1,0:T(8,128)(2,1)S(1)} %shard_map.139.mine_ref), channel_id=1, source_target_pairs={{0,16},{16,0},{1,17},{17,1},{2,18},{18,2},{3,19},{19,3},{4,20},{20... | collective-permute-start | bytes 1081352 | tf_op jit(solution)/shard_map/ppermute | solution.py:23
  95.0 1.3 %collective-permute-done.14.other_ref = bf16[1408,128]{1,0:T(8,128)(2,1)S(1)} collective-permute-done((bf16[1408,128]{1,0:T(8,128)(2,1)S(1)}, bf16[1408,128]{1,0:T(8,128)(2,1)S(1)}, u32[]{:S(2)}, u32[]{:S(2)}) %collective-permute-start.14) | collective-permute-done | bytes 360480 | tf_op jit(solution)/shard_map/ppermute | solution.py:23
  96.3 1.3 %shard_map.140 = (f32[9,128,128]{2,1,0:T(8,128)}, f32[9,128,128]{2,1,0:T(8,128)}, f32[4,128,128]{2,1,0:T(8,128)}) custom-call(bf16[1408,128]{1,0:T(8,128)(2,1)S(1)} %shard_map.139.mine_ref, bf16[1408,128]{1,0:T(8,128)(2,1)S(1)} %collective-permute-done.14.other_ref), custom_call_target="tpu_custom_call" | custom-call | flops 226492416 | bytes 2097152 | tf_op jit(solution)/shard_map/pallas_call | solution.py:552
  (21 shorter events, 0.1 us)
Async XLA Ops:
  0.6 0.9 copy-start.8
  1.6 14.2 %collective-permute-start.3 = (bf16[3,4,2,16,128]{4,3,2,1,0:T(8,128)(2,1)S(1)}, bf16[3,4,2,16,128]{4,3,2,1,0:T(8,128)(2,1)S(1)}, u32[]{:S(2)}, u32[]{:S(2)}) collective-permute-start(bf16[3,4,2,16,128]{4,3,2,1,0:T(8,128)(2,1)S(1)} %shard_map.129.refs_0_), channel_id=1, source_target_pairs={{0,32},{32,0},{1,33},{33,1},{2,34},{34,2},{3,35},{35,3},{4,36},{36... | collective-permute-start | bytes 294920 | tf_op jit(solution)/shard_map/ppermute | solution.py:28
  9.4 10.3 %collective-permute-start = (bf16[3,4,2,16,128]{4,3,2,1,0:T(8,128)(2,1)S(1)}, bf16[3,4,2,16,128]{4,3,2,1,0:T(8,128)(2,1)S(1)}, u32[]{:S(2)}, u32[]{:S(2)}) collective-permute-start(bf16[3,4,2,16,128]{4,3,2,1,0:T(8,128)(2,1)S(1)} %shard_map.129.refs_0_), channel_id=1, source_target_pairs={{0,64},{64,0},{128,192},{192,128},{1,65},{65,1},{129,193},{193,129... | collective-permute-start | bytes 294920 | tf_op jit(solution)/shard_map/ppermute | solution.py:28
  10.7 14.9 %collective-permute-start.1 = (bf16[3,4,2,16,128]{4,3,2,1,0:T(8,128)(2,1)S(1)}, bf16[3,4,2,16,128]{4,3,2,1,0:T(8,128)(2,1)S(1)}, u32[]{:S(2)}, u32[]{:S(2)}) collective-permute-start(bf16[3,4,2,16,128]{4,3,2,1,0:T(8,128)(2,1)S(1)} %shard_map.129.refs_0_), channel_id=1, source_target_pairs={{0,128},{64,192},{128,0},{192,64},{1,129},{65,193},{129,1},{193,65... | collective-permute-start | bytes 294920 | tf_op jit(solution)/shard_map/ppermute | solution.py:28
  13.4 12.3 %collective-permute-start.2 = (bf16[3,4,2,16,128]{4,3,2,1,0:T(8,128)(2,1)S(1)}, bf16[3,4,2,16,128]{4,3,2,1,0:T(8,128)(2,1)S(1)}, u32[]{:S(2)}, u32[]{:S(2)}) collective-permute-start(bf16[3,4,2,16,128]{4,3,2,1,0:T(8,128)(2,1)S(1)} %shard_map.129.refs_0_), channel_id=1, source_target_pairs={{0,192},{64,128},{128,64},{192,0},{1,193},{65,129},{129,65},{193,1... | collective-permute-start | bytes 294920 | tf_op jit(solution)/shard_map/ppermute | solution.py:28
  15.8 9.9 %collective-permute-start.4 = (bf16[3,4,2,16,128]{4,3,2,1,0:T(8,128)(2,1)S(1)}, bf16[3,4,2,16,128]{4,3,2,1,0:T(8,128)(2,1)S(1)}, u32[]{:S(2)}, u32[]{:S(2)}) collective-permute-start(bf16[3,4,2,16,128]{4,3,2,1,0:T(8,128)(2,1)S(1)} %collective-permute-done.3.refs_4_), channel_id=1, source_target_pairs={{0,64},{64,0},{128,192},{192,128},{1,65},{65,1},{129,193},{193,129... | collective-permute-start | bytes 294920 | tf_op jit(solution)/shard_map/ppermute | solution.py:28
  15.9 9.8 %collective-permute-start.5 = (bf16[3,4,2,16,128]{4,3,2,1,0:T(8,128)(2,1)S(1)}, bf16[3,4,2,16,128]{4,3,2,1,0:T(8,128)(2,1)S(1)}, u32[]{:S(2)}, u32[]{:S(2)}) collective-permute-start(bf16[3,4,2,16,128]{4,3,2,1,0:T(8,128)(2,1)S(1)} %collective-permute-done.3.refs_4_), channel_id=1, source_target_pairs={{0,128},{64,192},{128,0},{192,64},{1,129},{65,193},{129,1},{193,65... | collective-permute-start | bytes 294920 | tf_op jit(solution)/shard_map/ppermute | solution.py:28
  19.8 6.0 %collective-permute-start.6 = (bf16[3,4,2,16,128]{4,3,2,1,0:T(8,128)(2,1)S(1)}, bf16[3,4,2,16,128]{4,3,2,1,0:T(8,128)(2,1)S(1)}, u32[]{:S(2)}, u32[]{:S(2)}) collective-permute-start(bf16[3,4,2,16,128]{4,3,2,1,0:T(8,128)(2,1)S(1)} %collective-permute-done.3.refs_4_), channel_id=1, source_target_pairs={{0,192},{64,128},{128,64},{192,0},{1,193},{65,129},{129,65},{193,1... | collective-permute-start | bytes 294920 | tf_op jit(solution)/shard_map/ppermute | solution.py:28
  19.8 6.0 %copy-start.4 = (s32[296]{0:T(512)S(1)}, s32[296]{0:T(512)}, u32[]{:S(2)}) copy-start(s32[296]{0:T(512)} %get-tuple-element.32.index_ref.refs_8_) | copy-start | bytes 3556
  19.8 11.9 %copy-start.3 = (bf16[192,192]{1,0:T(8,128)(2,1)S(1)}, bf16[192,192]{1,0:T(8,128)(2,1)}, u32[]{:S(2)}) copy-start(bf16[192,192]{1,0:T(8,128)(2,1)} %get-tuple-element.33.turn_ref) | copy-start | bytes 221188
  25.7 6.0 %copy-start.2 = (f32[768,256]{1,0:T(8,128)S(1)}, f32[768,256]{1,0:T(8,128)}, u32[]{:S(2)}) copy-start(f32[768,256]{1,0:T(8,128)} %get-tuple-element.36.staged_ref) | copy-start | bytes 2359300
  25.7 0.7 copy-start.5
  27.1 4.6 %collective-permute-start.7 = (bf16[4,2,3,4,2,16,128]{6,5,4,3,2,1,0:T(8,128)(2,1)S(1)}, bf16[4,2,3,4,2,16,128]{6,5,4,3,2,1,0:T(8,128)(2,1)S(1)}, u32[]{:S(2)}, u32[]{:S(2)}) collective-permute-start(bf16[4,2,3,4,2,16,128]{6,5,4,3,2,1,0:T(8,128)(2,1)S(1)} %shard_map.131), channel_id=1, source_target_pairs={{0,16},{16,0},{1,17},{17,1},{2,18},{18,2},{3,19},{19,3},{4,20},{20... | collective-permute-start | bytes 2359304 | tf_op jit(solution)/shard_map/ppermute | solution.py:23
  31.6 1.6 %copy-start = (bf16[1152,896]{1,0:T(8,128)(2,1)S(1)}, bf16[1152,896]{1,0:T(8,128)(2,1)}, u32[]{:S(2)}) copy-start(bf16[1152,896]{1,0:T(8,128)(2,1)} %get-tuple-element.35.early_ref) | copy-start | bytes 6193156
  33.2 3.3 %copy-start.1 = (bf16[1152,768]{1,0:T(8,128)(2,1)S(1)}, bf16[1152,768]{1,0:T(8,128)(2,1)}, u32[]{:S(2)}) copy-start(bf16[1152,768]{1,0:T(8,128)(2,1)} %get-tuple-element.38.late_ref) | copy-start | bytes 5308420
  39.5 3.7 %copy-start.6 = (f32[960,256]{1,0:T(8,128)}, f32[960,256]{1,0:T(8,128)S(1)}, u32[]{:S(2)}) copy-start(f32[960,256]{1,0:T(8,128)S(1)} %get-tuple-element.52.rest_ref) | copy-start | bytes 2949124
  39.5 2.8 %collective-permute-start.8 = (f32[1408,128]{1,0:T(8,128)S(1)}, f32[1408,128]{1,0:T(8,128)S(1)}, u32[]{:S(2)}, u32[]{:S(2)}) collective-permute-start(f32[1408,128]{1,0:T(8,128)S(1)} %slice_bitcast_fusion), channel_id=1, source_target_pairs={{0,16},{16,0},{1,17},{17,1},{2,18},{18,2},{3,19},{19,3},{4,20},{20... | collective-permute-start | bytes 2162696 | tf_op jit(solution)/shard_map/ppermute | solution.py:23
  40.0 9.8 %collective-permute-start.9 = (bf16[3,4,2,16,128]{4,3,2,1,0:T(8,128)(2,1)S(1)}, bf16[3,4,2,16,128]{4,3,2,1,0:T(8,128)(2,1)S(1)}, u32[]{:S(2)}, u32[]{:S(2)}) collective-permute-start(bf16[3,4,2,16,128]{4,3,2,1,0:T(8,128)(2,1)S(1)} %get-tuple-element.48.own_ref), channel_id=1, source_target_pairs={{0,32},{32,0},{1,33},{33,1},{2,34},{34,2},{3,35},{35,3},{4,36},{36... | collective-permute-start | bytes 294920 | tf_op jit(solution)/shard_map/ppermute | solution.py:28
  43.1 14.7 %all-to-all-start = ((bf16[16,88,128]{2,1,0:T(8,128)(2,1)}), bf16[16,88,128]{2,1,0:T(8,128)(2,1)S(1)}, u32[]{:S(2)}, u32[]{:S(2)}) async-start(bf16[16,88,128]{2,1,0:T(8,128)(2,1)} %bitcast.13), calls=%async_computation | async-start | bytes 720896 | tf_op jit(solution)/shard_map/all_to_all | solution.py:669
  58.6 8.1 %collective-permute-start.10 = (bf16[2,3,4,2,16,128]{5,4,3,2,1,0:T(8,128)(2,1)S(1)}, bf16[2,3,4,2,16,128]{5,4,3,2,1,0:T(8,128)(2,1)S(1)}, u32[]{:S(2)}, u32[]{:S(2)}) collective-permute-start(bf16[2,3,4,2,16,128]{5,4,3,2,1,0:T(8,128)(2,1)S(1)} %get-tuple-element.50.own_ref), channel_id=1, source_target_pairs={{0,64},{64,0},{128,192},{192,128},{1,65},{65,1},{129,193},{193,129... | collective-permute-start | bytes 589832 | tf_op jit(solution)/shard_map/ppermute | solution.py:28
  58.9 9.4 %collective-permute-start.11 = (bf16[2,3,4,2,16,128]{5,4,3,2,1,0:T(8,128)(2,1)S(1)}, bf16[2,3,4,2,16,128]{5,4,3,2,1,0:T(8,128)(2,1)S(1)}, u32[]{:S(2)}, u32[]{:S(2)}) collective-permute-start(bf16[2,3,4,2,16,128]{5,4,3,2,1,0:T(8,128)(2,1)S(1)} %get-tuple-element.50.own_ref), channel_id=1, source_target_pairs={{0,128},{64,192},{128,0},{192,64},{1,129},{65,193},{129,1},{193,65... | collective-permute-start | bytes 589832 | tf_op jit(solution)/shard_map/ppermute | solution.py:28
  61.2 10.6 %collective-permute-start.12 = (bf16[2,3,4,2,16,128]{5,4,3,2,1,0:T(8,128)(2,1)S(1)}, bf16[2,3,4,2,16,128]{5,4,3,2,1,0:T(8,128)(2,1)S(1)}, u32[]{:S(2)}, u32[]{:S(2)}) collective-permute-start(bf16[2,3,4,2,16,128]{5,4,3,2,1,0:T(8,128)(2,1)S(1)} %get-tuple-element.50.own_ref), channel_id=1, source_target_pairs={{0,192},{64,128},{128,64},{192,0},{1,193},{65,129},{129,65},{193,1... | collective-permute-start | bytes 589832 | tf_op jit(solution)/shard_map/ppermute | solution.py:28
  62.4 12.8 %all-to-all-start.1 = ((bf16[8,88,128]{2,1,0:T(8,128)(2,1)}), bf16[8,88,128]{2,1,0:T(8,128)(2,1)S(1)}, u32[]{:S(2)}, u32[]{:S(2)}) async-start(bf16[8,88,128]{2,1,0:T(8,128)(2,1)} %get-tuple-element.49), calls=%async_computation.1 | async-start | bytes 360448 | tf_op jit(solution)/shard_map/all_to_all | solution.py:676
  76.3 8.1 %collective-permute-start.13 = (bf16[4,2,3,4,2,16,128]{6,5,4,3,2,1,0:T(8,128)(2,1)}, bf16[4,2,3,4,2,16,128]{6,5,4,3,2,1,0:T(8,128)(2,1)}, u32[]{:S(2)}, u32[]{:S(2)}) collective-permute-start(bf16[4,2,3,4,2,16,128]{6,5,4,3,2,1,0:T(8,128)(2,1)} %get-tuple-element.51), channel_id=1, source_target_pairs={{0,16},{16,0},{1,17},{17,1},{2,18},{18,2},{3,19},{19,3},{4,20},{20... | collective-permute-start | bytes 2359304 | tf_op jit(solution)/shard_map/ppermute | solution.py:23
  80.9 12.4 %all-to-all-start.2 = ((bf16[16,88,128]{2,1,0:T(8,128)(2,1)}), bf16[16,88,128]{2,1,0:T(8,128)(2,1)S(1)}, u32[]{:S(2)}, u32[]{:S(2)}) async-start(bf16[16,88,128]{2,1,0:T(8,128)(2,1)} %get-tuple-element.54), calls=%async_computation.2 | async-start | bytes 720896 | tf_op jit(solution)/shard_map/all_to_all | solution.py:683
  84.5 1.2 %copy-start.7 = (f32[960,256]{1,0:T(8,128)S(1)}, f32[960,256]{1,0:T(8,128)}, u32[]{:S(2)}) copy-start(f32[960,256]{1,0:T(8,128)} %copy-done.6) | copy-start | bytes 2949124
  93.4 3.0 %collective-permute-start.14 = (bf16[1408,128]{1,0:T(8,128)(2,1)S(1)}, bf16[1408,128]{1,0:T(8,128)(2,1)S(1)}, u32[]{:S(2)}, u32[]{:S(2)}) collective-permute-start(bf16[1408,128]{1,0:T(8,128)(2,1)S(1)} %shard_map.139.mine_ref), channel_id=1, source_target_pairs={{0,16},{16,0},{1,17},{17,1},{2,18},{18,2},{3,19},{19,3},{4,20},{20... | collective-permute-start | bytes 1081352 | tf_op jit(solution)/shard_map/ppermute | solution.py:23

commit v6 on v5

--- a/solution.py
+++ b/solution.py
@@ -143,8 +143,17 @@
             ring_ref[n % 3, n // 3, depth] = rows
 
 
-W1_SIDES, W2, TAIL, X = (slice(0, 512), slice(512, 640), slice(640, 768), slice(768, 896))
-W2_BACK, W1_BACK, ADJOINT = slice(0, 128), slice(128, 256), slice(256, 768)
+W1, W2, TAIL = slice(0, 128), slice(128, 256), slice(256, 384)
+W2_BACK, W1_BACK, X = slice(0, 128), slice(128, 256), slice(256, 384)
+
+
+def side_weights(source_ref, chosen, sides_ref, depth, back=False):
+    for side in range(4):
+        for r in range(depth):
+            for k in range(3):
+                a, b = frame_source(side, r, k)
+                at = 8 - 3 * a - b if back else 3 * a + b
+                sides_ref[lanes(3 * r + k), lanes(side)] = source_ref[lanes(at), chosen]
 
 
 def index_kernel(near_ref, code_ref, slot_ref, index_ref, turn_hbm, turn_ref, sems):
@@ -210,19 +219,15 @@
         flag_ref[at] = index_ref[at]
     pad_ref[...] = jnp.zeros_like(pad_ref)
     early_ref[704:, TAIL] = jnp.zeros_like(early_ref[704:, TAIL])
-    early_ref[768:, X] = jnp.zeros_like(early_ref[768:, X])
+    late_ref[768:, X] = jnp.zeros_like(late_ref[768:, X])
     finish(arrivals)
-    for side in range(4):
-        for r in range(3):
-            for k in range(3):
-                a, b = frame_source(side, r, k)
-                early_ref[lanes(3 * r + k), lanes(side)] = w1_ref[lanes(3 * a + b), :]
+    early_ref[:, W1] = w1_ref[...]
     early_ref[:, W2] = w2_ref[...]
     early_ref[:512, TAIL] = wc_ref[...]
     down = down_ref[...]
     early_ref[512:704, TAIL] = down
     x_rows = as_rows(x_ref[...])
-    early_ref[:768, X] = x_rows
+    late_ref[:768, X] = x_rows
     departures = fetch([early_ref], [early_hbm], out_sems)
 
     def flip(block):
@@ -230,19 +235,9 @@
 
     for a in range(3):
         for b in range(3):
-            first_flip = flip(w1_ref[lanes(3 * a + b), :])
-            second_flip = flip(w2_ref[lanes(3 * a + b), :])
             back = lanes(8 - 3 * a - b)
-            late_ref[back, W1_BACK] = first_flip
-            late_ref[back, W2_BACK] = second_flip
-            for side in range(4):
-                for r in range(2):
-                    for k in range(3):
-                        if frame_source(side, r, k) != (a, b):
-                            continue
-                        if r == 0:
-                            late_ref[lanes(6 + k), lanes(2 + side)] = first_flip
-                        late_ref[lanes(3 * r + k), lanes(2 + side)] = second_flip
+            late_ref[back, W1_BACK] = flip(w1_ref[lanes(3 * a + b), :])
+            late_ref[back, W2_BACK] = flip(w2_ref[lanes(3 * a + b), :])
     last = pltpu.make_async_copy(late_ref, late_hbm, out_sems.at[1])
     last.start()
     departures.append(last)
@@ -282,9 +277,10 @@
     index_ref, turn_ref, mine_ref, other_ref, early_ref, staged_ref,
     coarse_ref, delta_ring_ref, pre_ref, strip_pre_ref, seam_ref, cols2_ref, strip_ref,
     down_cols_ref, delta_ref, line_ref,
-    pad_ref, patch_ref, wide_ref, fine_ref, cells_ref, line_cols_ref,
+    pad_ref, patch_ref, wide_ref, fine_ref, cells_ref, line_cols_ref, sides_ref,
 ):
     tiles = 3
+    side_weights(early_ref, W1, sides_ref, 3)
     patch_ref[...] = jnp.zeros_like(patch_ref)
     pad_ref[...] = jnp.zeros_like(pad_ref)
     line_ref[...] = jnp.zeros_like(line_ref)
@@ -312,7 +308,7 @@
         for b in range(3):
             part = patch_ref[:, r, b : b + EDGE, :].astype(BF16)
             strip_ref[:, lanes(3 * r + b)] = as_rows(part)
-    wide_ref[...] = dot(strip_ref[...], early_ref[:, W1_SIDES])
+    wide_ref[...] = dot(strip_ref[...], sides_ref[...])
     for n in range(12):
         strip_pre_ref[strip(n), :] = pick(wide_ref, n * EDGE, EDGE, index_ref[near_at(n) + 2])
     line_ref[:, 1 : EDGE + 1, :] = seams.reshape(12, EDGE, CH)
@@ -321,7 +317,7 @@
     parts = []
     for side in range(4):
         rows = slice(side * tiles * EDGE, (side + 1) * tiles * EDGE)
-        parts.append(dot(line_cols_ref[rows, :], early_ref[: 3 * CH, lanes(side)]))
+        parts.append(dot(line_cols_ref[rows, :], sides_ref[: 3 * CH, lanes(side)]))
     add_sides(pre_ref, jnp.concatenate(parts, axis=0))
     fill_pad(pad_ref, gelu(pre_ref[...]).astype(BF16).astype(F32))
     put_seams(pad_ref, dot(turn, gelu(strip_pre_ref[...]).astype(BF16)))
@@ -348,8 +344,9 @@
 def gradient_kernel(
     index_ref, turn_ref, early_ref, late_ref, pre_ref, strip_pre_ref, seam_ref, cols2_ref, strip_ref, down_cols_ref, delta_ref, line_ref,
     grad_ref, rest_ref,
-    pad_ref, cols_ref, cols3_ref, split_ref, line_cols_ref,
+    pad_ref, cols_ref, cols3_ref, split_ref, line_cols_ref, sides_ref,
 ):
+    side_weights(late_ref, W2_BACK, sides_ref, 1, True)
     tiles = 3
     core = lax.axis_index("c")
 
@@ -380,7 +377,7 @@
     rims = []
     for side in range(4):
         rows = slice(side * tiles * EDGE, (side + 1) * tiles * EDGE)
-        rims.append(dot(line_cols_ref[rows, :], late_ref[: 3 * CH, lanes(2 + side)]))
+        rims.append(dot(line_cols_ref[rows, :], sides_ref[:, lanes(side)]))
     sent = turned(turn, jnp.concatenate(rims, axis=0))
     rest_ref[768:, lanes(0)] = strip_pre_ref[...]
     rest_ref[768:, lanes(1)] = sent
@@ -389,7 +386,7 @@
         chosen = pl.ds(pl.multiple_of(index_ref[near_at(n) + 2] * CH, CH), CH)
         split_ref[strip(n), chosen] = sent_delta[strip(n)]
     sent_grad = dot(across_rows(split_ref[...]), strip_ref[...])
-    fill_pad(pad_ref, early_ref[:768, X].astype(F32))
+    fill_pad(pad_ref, late_ref[:768, X].astype(F32))
     put_seams(pad_ref, seam_ref[...])
     windows(pad_ref, cols_ref)
     first_grad = dot(across_rows(inner_delta), cols_ref[...])
@@ -408,8 +405,10 @@
     index_ref, turn_ref, mine_ref, other_ref, late_ref, rest_ref,
     out_ref, flag_ref,
     pad_ref, cols_ref, line_ref, deep_ref, line_cols_ref, deep_cols_ref, ends_ref, wide_ref,
-    strip_wide_ref, cot_ref, cells_ref,
+    strip_wide_ref, cot_ref, cells_ref, sides_ref, sides2_ref,
 ):
+    side_weights(late_ref, W1_BACK, sides_ref, 1, True)
+    side_weights(late_ref, W2_BACK, sides2_ref, 2, True)
     flag_ref[...] = jnp.zeros_like(flag_ref)
     turn = turn_ref[...]
     line_ref[...] = jnp.zeros_like(line_ref)
@@ -431,9 +430,9 @@
     triples(line_ref, line_cols_ref, (2, 1, 0))
     line_cols_ref[strip_rows:, :] = ends_ref[...].astype(BF16)
     triples(deep_ref, deep_cols_ref, (2, 1, 0))
-    wide_ref[...] = dot(line_cols_ref[...], late_ref[: 3 * CH, ADJOINT])
-    strip_wide_ref[...] = dot(deep_cols_ref[...], late_ref[: 3 * CH, ADJOINT]) + dot(
-        line_cols_ref[:strip_rows, :], late_ref[3 * CH : 6 * CH, ADJOINT]
+    wide_ref[...] = dot(line_cols_ref[...], sides2_ref[: 3 * CH])
+    strip_wide_ref[...] = dot(deep_cols_ref[...], sides2_ref[: 3 * CH]) + dot(
+        line_cols_ref[:strip_rows, :], sides2_ref[3 * CH :]
     )
     cot_ref[...] = rest_ref[768:, lanes(1)]
     rims = []
@@ -455,7 +454,7 @@
     strip_delta = (gelu_slope(rest_ref[768:, lanes(0)]) * cot_ref[...]).astype(BF16).astype(F32)
     line_ref[:, 1 : EDGE + 1, :] = strip_delta.reshape(12, EDGE, CH)
     triples(line_ref, deep_cols_ref, (2, 1, 0))
-    strip_wide_ref[...] = dot(deep_cols_ref[...], late_ref[6 * CH :, ADJOINT])
+    strip_wide_ref[...] = dot(deep_cols_ref[...], sides_ref[...])
     rims = []
     for n in range(12):
         rims.append(pick(strip_wide_ref, n * EDGE, EDGE, index_ref[near_at(n) + 2]))
@@ -497,6 +496,10 @@
 ):
     spread_sum(pieces_ref, copies_ref)
     table_kernel(own_ref, one_ref, two_ref, three_ref, table_ref)
+
+
+def keep_kernel(grads_ref, got_ref, kept_ref):
+    kept_ref[...] = (grads_ref[0] + got_ref[...]).astype(BF16)
 
 
 def hold_kernel(block_ref, flag_ref, out_ref):
@@ -589,8 +592,8 @@
         room=60,
     )
     staged = (
-        shape((9 * CH, 7 * CH), BF16),
-        shape((9 * CH, 6 * CH), BF16),
+        shape((9 * CH, 3 * CH), BF16),
+        shape((9 * CH, 3 * CH), BF16),
         shape((cells, 2 * CH), F32),
     )
     ready, early, late, staged_cells = call(
@@ -603,7 +606,7 @@
         specs=[smem] + [hbm] * 6,
         out_specs=(smem,) + (hbm,) * 3,
         cost=100,
-        room=60,
+        room=50,
     )
     near_rings = [own_ring] + [swap_apart(own_ring, "y", apart) for apart in (1, 2, 3)]
     far_rings = [across] + [swap_apart(across, "y", apart) for apart in (1, 2, 3)]
@@ -642,6 +645,7 @@
             shape(x.shape, F32),
             cell_rows,
             shape((strips, 3 * CH), BF16),
+            shape((9 * CH, 4 * CH), BF16),
         ],
         specs=[smem] + [vmem] * 5,
         cost=2,
@@ -659,11 +663,12 @@
             all_cols,
             shape((strips, 4 * CH), BF16),
             shape((strips, 3 * CH), BF16),
+            shape((3 * CH, 4 * CH), BF16),
         ],
         specs=[smem] + [vmem] * 11,
         cost=4,
     )
-    kept = (grads[0] + swap_core(grads[1])).astype(BF16)
+    kept = call(keep_kernel, shape(grads.shape[1:], BF16), [grads, swap_core(grads[1])])
     part = kept.shape[0] // plane
     across = swap_apart(delta_ring, "z", 1)
     pieces = lax.all_to_all(kept.reshape(plane, part, CH), PLANE, 0, 0)
@@ -697,6 +702,8 @@
             wide,
             strip_rows,
             cell_rows,
+            shape((3 * CH, 4 * CH), BF16),
+            shape((6 * CH, 4 * CH), BF16),
         ],
         specs=[smem] + [vmem] * 5,
         cost=100,

time: 98.3 us -> 94.6 us (0.962)
  local copies, waits for them, and re-layouts: 4.48 us -> 1.69 us
  waiting for transfers between devices: 23.7 us -> 25.8 us
  starting transfers between devices: 45.7 us -> 44.6 us
    unnamed x18 -> x20, local copies, waits for them, and re-layouts: 4.43 us -> 1.64 us
    all_to_all x1, waiting for transfers between devices: 3.83 us -> 4.86 us  [shards(): summed = lax.all_to_all(copies, PLANE, 0, 0).reshape(-1, CH)]
    all_to_all x1, starting transfers between devices: 6.63 us -> 5.6 us  [shards(): pieces = lax.all_to_all(kept.reshape(plane, part, CH), PLANE, 0, 0)]
    pallas_call x13 -> x14, Pallas kernels: 22.2 us -> 21.3 us  [call(): pl.pallas_call(kernel, out_shape=outs, in_specs=specs or [vmem] * len(ope...]
  transfers between devices with their start and end apart: 18 -> 18, of which waited for: 7 -> 8; matrix products, arithmetic and copies ran while one was open for 1% -> 0% of each run, Pallas kernels for 12% -> 12%
where the time goes in v6:
time: 94.6 us; the launch traced here: 94.2 us
  starting transfers between devices  44.6 us (47%)
  waiting for transfers between devices  25.8 us (27%)
  Pallas kernels  21.3 us (23%)
  local copies, waits for them, and re-layouts  1.69 us (2%)
    ppermute x11, starting transfers between devices, swap_apart(): return lax.ppermute(block, axis, [(i, i ^ apart) for i in range(number)])  21.8 us
    pallas_call x14, Pallas kernels, call(): pl.pallas_call(kernel, out_shape=outs, in_specs=specs or [vmem] * len(ope...  21.3 us
    ppermute x4, starting transfers between devices, swap_core(): return lax.ppermute(block, 'c', [(0, 1), (1, 0)])  9.23 us
    all_to_all x1, waiting for transfers between devices, shards(): pieces = lax.all_to_all(kept.reshape(plane, part, CH), PLANE, 0, 0)  8.02 us
    ppermute x11, waiting for transfers between devices, swap_apart(): return lax.ppermute(block, axis, [(i, i ^ apart) for i in range(number)])  6.04 us
    all_to_all x1, starting transfers between devices, shards(): pieces = lax.all_to_all(kept.reshape(plane, part, CH), PLANE, 0, 0)  5.6 us
    all_to_all x1, waiting for transfers between devices, shards(): summed = lax.all_to_all(copies, PLANE, 0, 0).reshape(-1, CH)  4.86 us
    all_to_all x1, starting transfers between devices, shards(): pieces = lax.all_to_all(copies, DEPTH, 0, 0)  4.44 us
  transfers between devices with their start and end apart: 18, of which 8 were waited for; matrix products, arithmetic and copies ran while one was open for 0% of the time, Pallas kernels for 12%

profile of v6, /device:TPU:1, one launch (start us, length us, event | category | flops | bytes accessed | tf_op | source)
XLA Modules:
  0.0 94.2 jit_solution(4033938058750020197)
XLA Ops:
  0.6 0.0 copy-start.5
  0.6 0.9 copy-done.5
  1.6 0.1 shard_map.129.refs_0_
  1.6 7.8 %collective-permute-start.3 = (bf16[3,4,2,16,128]{4,3,2,1,0:T(8,128)(2,1)S(1)}, bf16[3,4,2,16,128]{4,3,2,1,0:T(8,128)(2,1)S(1)}, u32[]{:S(2)}, u32[]{:S(2)}) collective-permute-start(bf16[3,4,2,16,128]{4,3,2,1,0:T(8,128)(2,1)S(1)} %shard_map.129.refs_0_), channel_id=1, source_target_pairs={{0,32},{32,0},{1,33},{33,1},{2,34},{34,2},{3,35},{35,3},{4,36},{36... | collective-permute-start | bytes 294920 | tf_op jit(solution)/shard_map/ppermute | solution.py:28
  9.4 1.3 %collective-permute-start = (bf16[3,4,2,16,128]{4,3,2,1,0:T(8,128)(2,1)S(1)}, bf16[3,4,2,16,128]{4,3,2,1,0:T(8,128)(2,1)S(1)}, u32[]{:S(2)}, u32[]{:S(2)}) collective-permute-start(bf16[3,4,2,16,128]{4,3,2,1,0:T(8,128)(2,1)S(1)} %shard_map.129.refs_0_), channel_id=1, source_target_pairs={{0,64},{64,0},{128,192},{192,128},{1,65},{65,1},{129,193},{193,129... | collective-permute-start | bytes 294920 | tf_op jit(solution)/shard_map/ppermute | solution.py:28
  10.7 2.6 %collective-permute-start.1 = (bf16[3,4,2,16,128]{4,3,2,1,0:T(8,128)(2,1)S(1)}, bf16[3,4,2,16,128]{4,3,2,1,0:T(8,128)(2,1)S(1)}, u32[]{:S(2)}, u32[]{:S(2)}) collective-permute-start(bf16[3,4,2,16,128]{4,3,2,1,0:T(8,128)(2,1)S(1)} %shard_map.129.refs_0_), channel_id=1, source_target_pairs={{0,128},{64,192},{128,0},{192,64},{1,129},{65,193},{129,1},{193,65... | collective-permute-start | bytes 294920 | tf_op jit(solution)/shard_map/ppermute | solution.py:28
  13.4 0.0 collective-permute-start.2
  13.4 0.0 copy-start.7
  13.4 0.0 copy-start.8
  13.4 0.0 copy-start.9
  13.4 2.6 %shard_map.128 = (s32[296]{0:T(512)}, bf16[192,192]{1,0:T(8,128)(2,1)}) custom-call(s32[4,48]{1,0:T(4,128)} %bitcast.32, s32[4,48]{1,0:T(4,128)} %bitcast.33, s32[48]{0:T(128)} %slot_ref.1), custom_call_target="tpu_custom_call" | custom-call | flops 905969664 | bytes 2097152 | tf_op jit(solution)/shard_map/pallas_call | solution.py:555
  16.0 0.0 collective-permute-done.3.refs_4_
  16.0 0.1 collective-permute-start.4
  16.1 3.8 %collective-permute-start.5 = (bf16[3,4,2,16,128]{4,3,2,1,0:T(8,128)(2,1)S(1)}, bf16[3,4,2,16,128]{4,3,2,1,0:T(8,128)(2,1)S(1)}, u32[]{:S(2)}, u32[]{:S(2)}) collective-permute-start(bf16[3,4,2,16,128]{4,3,2,1,0:T(8,128)(2,1)S(1)} %collective-permute-done.3.refs_4_), channel_id=1, source_target_pairs={{0,128},{64,192},{128,0},{192,64},{1,129},{65,193},{129,1},{193,65... | collective-permute-start | bytes 294920 | tf_op jit(solution)/shard_map/ppermute | solution.py:28
  19.9 0.0 collective-permute-done.refs_1_
  19.9 0.0 collective-permute-start.6
  20.0 0.0 copy-start.1
  20.0 0.7 copy-done.1
  20.7 3.8 %shard_map.130 = (s32[8]{0:T(128)S(1)}, bf16[1152,384]{1,0:T(8,128)(2,1)S(1)}, bf16[1152,384]{1,0:T(8,128)(2,1)S(1)}, f32[768,256]{1,0:T(8,128)S(1)}) custom-call(s32[296]{0:T(512)S(1)} %copy-done.1, bf16[3,16,16,128]{3,2,1,0:T(8,128)(2,1)S(1)} %bitcast.27, bf16[3,16,16,128]{3,2,1,0:T(8,128)(2,1)S(1)} %bitcast.28, bf16[192,128]{1,0:T(8,128)(2,1)S(1)} %bitcast.30, ...), custom_call_target="tpu_custom_call" | custom-call | flops 22649241600 | bytes 2097152 | tf_op jit(solution)/shard_map/pallas_call | solution.py:555
  24.5 0.0 copy-start
  24.5 0.0 collective-permute-done.1.refs_2_
  24.6 1.1 %collective-permute-done.6.refs_7_ = bf16[3,4,2,16,128]{4,3,2,1,0:T(8,128)(2,1)S(1)} collective-permute-done((bf16[3,4,2,16,128]{4,3,2,1,0:T(8,128)(2,1)S(1)}, bf16[3,4,2,16,128]{4,3,2,1,0:T(8,128)(2,1)S(1)}, u32[]{:S(2)}, u32[]{:S(2)}) %collective-permute-start.6) | collective-permute-done | bytes 98336 | tf_op jit(solution)/shard_map/ppermute | solution.py:28
  25.7 0.6 shard_map.131
  26.3 2.5 %collective-permute-start.7 = (bf16[4,2,3,4,2,16,128]{6,5,4,3,2,1,0:T(8,128)(2,1)S(1)}, bf16[4,2,3,4,2,16,128]{6,5,4,3,2,1,0:T(8,128)(2,1)S(1)}, u32[]{:S(2)}, u32[]{:S(2)}) collective-permute-start(bf16[4,2,3,4,2,16,128]{6,5,4,3,2,1,0:T(8,128)(2,1)S(1)} %shard_map.131), channel_id=1, source_target_pairs={{0,16},{16,0},{1,17},{17,1},{2,18},{18,2},{3,19},{19,3},{4,20},{20... | collective-permute-start | bytes 2359304 | tf_op jit(solution)/shard_map/ppermute | solution.py:23
  28.8 1.9 %collective-permute-done.7 = bf16[4,2,3,4,2,16,128]{6,5,4,3,2,1,0:T(8,128)(2,1)S(1)} collective-permute-done((bf16[4,2,3,4,2,16,128]{6,5,4,3,2,1,0:T(8,128)(2,1)S(1)}, bf16[4,2,3,4,2,16,128]{6,5,4,3,2,1,0:T(8,128)(2,1)S(1)}, u32[]{:S(2)}, u32[]{:S(2)}) %collective-permute-start.7) | collective-permute-done | bytes 786464 | tf_op jit(solution)/shard_map/ppermute | solution.py:23
  30.7 3.3 %shard_map.132 = (bf16[192,128]{1,0:T(8,128)(2,1)}, bf16[3,4,2,16,128]{4,3,2,1,0:T(8,128)(2,1)S(1)}, f32[768,128]{1,0:T(8,128)S(1)}, f32[192,128]{1,0:T(8,128)S(...) custom-call(s32[296]{0:T(512)S(1)} %copy-done.1, ...), custom_call_target="tpu_custom_call" | custom-call | flops 452984832 | bytes 2097152 | tf_op jit(solution)/shard_map/pallas_call | solution.py:555
  34.0 3.0 %shard_map.133 = (f32[2,1408,128]{2,1,0:T(8,128)S(1)}, f32[960,256]{1,0:T(8,128)S(1)}) custom-call(s32[296]{0:T(512)S(1)} %copy-done.1, bf16[192,192]{1,0:T(8,128)(2,1)S(1)} %copy-done, bf16[1152,384]{1,0:T(8,128)(2,1)S(1)} %get-tuple-element.35.early_ref, bf16[1152,384]{1,0:T(8,128)(2,1)S(1)} %get-tuple-element.38.late_ref, ...), custom_call_target="tpu_custom_call" | custom-call | flops 905969664 | bytes 2097152 | tf_op jit(solution)/shard_map/pallas_call | solution.py:555
  37.0 0.4 collective-permute-start.8
  37.5 2.2 %collective-permute-start.9 = (bf16[3,4,2,16,128]{4,3,2,1,0:T(8,128)(2,1)S(1)}, bf16[3,4,2,16,128]{4,3,2,1,0:T(8,128)(2,1)S(1)}, u32[]{:S(2)}, u32[]{:S(2)}) collective-permute-start(bf16[3,4,2,16,128]{4,3,2,1,0:T(8,128)(2,1)S(1)} %get-tuple-element.48.own_ref), channel_id=1, source_target_pairs={{0,32},{32,0},{1,33},{33,1},{2,34},{34,2},{3,35},{35,3},{4,36},{36... | collective-permute-start | bytes 294920 | tf_op jit(solution)/shard_map/ppermute | solution.py:28
  39.7 0.8 shard_map.134
  40.5 5.6 %all-to-all-start = ((bf16[16,88,128]{2,1,0:T(8,128)(2,1)}), bf16[16,88,128]{2,1,0:T(8,128)(2,1)S(1)}, u32[]{:S(2)}, u32[]{:S(2)}) async-start(bf16[16,88,128]{2,1,0:T(8,128)(2,1)} %bitcast.12), calls=%async_computation | async-start | bytes 720896 | tf_op jit(solution)/shard_map/all_to_all | solution.py:674
  46.1 8.0 %all-to-all-done.pieces_ref = bf16[16,88,128]{2,1,0:T(8,128)(2,1)S(1)} async-done(((bf16[16,88,128]{2,1,0:T(8,128)(2,1)}), bf16[16,88,128]{2,1,0:T(8,128)(2,1)S(1)}, u32[]{:S(2)}, u32[]{:S(2)}) %all-to-all-start) | async-done | bytes 360480 | tf_op jit(solution)/shard_map/all_to_all | solution.py:674
  54.2 0.7 shard_map.136
  54.9 0.4 collective-permute-start.10
  55.3 2.3 %collective-permute-start.11 = (bf16[2,3,4,2,16,128]{5,4,3,2,1,0:T(8,128)(2,1)S(1)}, bf16[2,3,4,2,16,128]{5,4,3,2,1,0:T(8,128)(2,1)S(1)}, u32[]{:S(2)}, u32[]{:S(2)}) collective-permute-start(bf16[2,3,4,2,16,128]{5,4,3,2,1,0:T(8,128)(2,1)S(1)} %get-tuple-element.50.own_ref), channel_id=1, source_target_pairs={{0,128},{64,192},{128,0},{192,64},{1,129},{65,193},{129,1},{193,65... | collective-permute-start | bytes 589832 | tf_op jit(solution)/shard_map/ppermute | solution.py:28
  57.5 1.2 %collective-permute-start.12 = (bf16[2,3,4,2,16,128]{5,4,3,2,1,0:T(8,128)(2,1)S(1)}, bf16[2,3,4,2,16,128]{5,4,3,2,1,0:T(8,128)(2,1)S(1)}, u32[]{:S(2)}, u32[]{:S(2)}) collective-permute-start(bf16[2,3,4,2,16,128]{5,4,3,2,1,0:T(8,128)(2,1)S(1)} %get-tuple-element.50.own_ref), channel_id=1, source_target_pairs={{0,192},{64,128},{128,64},{192,0},{1,193},{65,129},{129,65},{193,1... | collective-permute-start | bytes 589832 | tf_op jit(solution)/shard_map/ppermute | solution.py:28
  58.8 4.4 %all-to-all-start.1 = ((bf16[8,88,128]{2,1,0:T(8,128)(2,1)}), bf16[8,88,128]{2,1,0:T(8,128)(2,1)S(1)}, u32[]{:S(2)}, u32[]{:S(2)}) async-start(bf16[8,88,128]{2,1,0:T(8,128)(2,1)} %get-tuple-element.49), calls=%async_computation.1 | async-start | bytes 360448 | tf_op jit(solution)/shard_map/all_to_all | solution.py:681
  63.2 1.5 %collective-permute-done.11.refs_1_.two_ref = bf16[2,3,4,2,16,128]{5,4,3,2,1,0:T(8,128)(2,1)S(1)} collective-permute-done((bf16[2,3,4,2,16,128]{5,4,3,2,1,0:T(8,128)(2,1)S(1)}, bf16[2,3,4,2,16,128]{5,4,3,2,1,0:T(8,128)(2,1)S(1)}, u32[]{:S(2)}, u32[]{:S(2)}) %collective-permute-start.11) | collective-permute-done | bytes 196640 | tf_op jit(solution)/shard_map/ppermute | solution.py:28
  64.7 3.4 %collective-permute-done.12.refs_2_.three_ref = bf16[2,3,4,2,16,128]{5,4,3,2,1,0:T(8,128)(2,1)S(1)} collective-permute-done((bf16[2,3,4,2,16,128]{5,4,3,2,1,0:T(8,128)(2,1)S(1)}, bf16[2,3,4,2,16,128]{5,4,3,2,1,0:T(8,128)(2,1)S(1)}, u32[]{:S(2)}, u32[]{:S(2)}) %collective-permute-start.12) | collective-permute-done | bytes 196640 | tf_op jit(solution)/shard_map/ppermute | solution.py:28
  68.2 3.6 %all-to-all-done.1.pieces_ref = bf16[8,88,128]{2,1,0:T(8,128)(2,1)S(1)} async-done(((bf16[8,88,128]{2,1,0:T(8,128)(2,1)}), bf16[8,88,128]{2,1,0:T(8,128)(2,1)S(1)}, u32[]{:S(2)}, u32[]{:S(2)}) %all-to-all-start.1) | async-done | bytes 180256 | tf_op jit(solution)/shard_map/all_to_all | solution.py:681
  71.8 1.1 %shard_map.138 = (bf16[16,88,128]{2,1,0:T(8,128)(2,1)}, bf16[4,2,3,4,2,16,128]{6,5,4,3,2,1,0:T(8,128)(2,1)}) custom-call(bf16[8,88,128]{2,1,0:T(8,128)(2,1)S(1)} %all-to-all-done.1.pieces_ref, f32[8,128]{1,0:T(8,128)S(1)} %shard_map.137.flag_ref, bf16[2,3,4,2,16,128]{5,4,3,2,1,0:T(8,128)(2,1)S(1)} %get-tuple-element.50.own_ref, ...), custom_call_target="tpu_custom_call" | custom-call | flops 226492416 | bytes 2097152 | tf_op jit(solution)/shard_map/pallas_call | solution.py:555
  72.8 4.6 %collective-permute-start.13 = (bf16[4,2,3,4,2,16,128]{6,5,4,3,2,1,0:T(8,128)(2,1)}, bf16[4,2,3,4,2,16,128]{6,5,4,3,2,1,0:T(8,128)(2,1)}, u32[]{:S(2)}, u32[]{:S(2)}) collective-permute-start(bf16[4,2,3,4,2,16,128]{6,5,4,3,2,1,0:T(8,128)(2,1)} %get-tuple-element.51), channel_id=1, source_target_pairs={{0,16},{16,0},{1,17},{17,1},{2,18},{18,2},{3,19},{19,3},{4,20},{20... | collective-permute-start | bytes 2359304 | tf_op jit(solution)/shard_map/ppermute | solution.py:23
  77.4 3.5 %all-to-all-start.2 = ((bf16[16,88,128]{2,1,0:T(8,128)(2,1)}), bf16[16,88,128]{2,1,0:T(8,128)(2,1)S(1)}, u32[]{:S(2)}, u32[]{:S(2)}) async-start(bf16[16,88,128]{2,1,0:T(8,128)(2,1)} %get-tuple-element.54), calls=%async_computation.2 | async-start | bytes 720896 | tf_op jit(solution)/shard_map/all_to_all | solution.py:688
  81.0 4.0 %shard_map.139 = (bf16[3,16,16,128]{3,2,1,0:T(8,128)(2,1)}, f32[8,128]{1,0:T(8,128)S(1)}) custom-call(s32[296]{0:T(512)S(1)} %copy-done.2, bf16[192,192]{1,0:T(8,128)(2,1)S(1)} %copy-done, bf16[24,4,2,16,128]{4,3,2,1,0:T(8,128)(2,1)} %bitcast.13.mine_ref, bf16[24,4,2,16,128]{4,3,2,1,0:T(8,128)(2,1)} %bitcast.14.other_ref, ...), custom_call_target="tpu_custom_call" | custom-call | flops 22649241600 | bytes 2097152 | tf_op jit(solution)/shard_map/pallas_call | solution.py:555
  85.0 4.9 %all-to-all-done.2 = bf16[16,88,128]{2,1,0:T(8,128)(2,1)S(1)} async-done(((bf16[16,88,128]{2,1,0:T(8,128)(2,1)}), bf16[16,88,128]{2,1,0:T(8,128)(2,1)S(1)}, u32[]{:S(2)}, u32[]{:S(2)}) %all-to-all-start.2) | async-done | bytes 360480 | tf_op jit(solution)/shard_map/all_to_all | solution.py:688
  89.9 1.7 %collective-permute-start.14 = (bf16[1408,128]{1,0:T(8,128)(2,1)S(1)}, bf16[1408,128]{1,0:T(8,128)(2,1)S(1)}, u32[]{:S(2)}, u32[]{:S(2)}) collective-permute-start(bf16[1408,128]{1,0:T(8,128)(2,1)S(1)} %shard_map.140.mine_ref), channel_id=1, source_target_pairs={{0,16},{16,0},{1,17},{17,1},{2,18},{18,2},{3,19},{19,3},{4,20},{20... | collective-permute-start | bytes 1081352 | tf_op jit(solution)/shard_map/ppermute | solution.py:23
  91.6 1.3 %collective-permute-done.14.other_ref = bf16[1408,128]{1,0:T(8,128)(2,1)S(1)} collective-permute-done((bf16[1408,128]{1,0:T(8,128)(2,1)S(1)}, bf16[1408,128]{1,0:T(8,128)(2,1)S(1)}, u32[]{:S(2)}, u32[]{:S(2)}) %collective-permute-start.14) | collective-permute-done | bytes 360480 | tf_op jit(solution)/shard_map/ppermute | solution.py:23
  92.9 1.3 %shard_map.141 = (f32[9,128,128]{2,1,0:T(8,128)}, f32[9,128,128]{2,1,0:T(8,128)}, f32[4,128,128]{2,1,0:T(8,128)}) custom-call(bf16[1408,128]{1,0:T(8,128)(2,1)S(1)} %shard_map.140.mine_ref, bf16[1408,128]{1,0:T(8,128)(2,1)S(1)} %collective-permute-done.14.other_ref), custom_call_target="tpu_custom_call" | custom-call | flops 226492416 | bytes 2097152 | tf_op jit(solution)/shard_map/pallas_call | solution.py:555
  (23 shorter events, 0.1 us)
Async XLA Ops:
  0.6 0.9 copy-start.5
  1.6 14.4 %collective-permute-start.3 = (bf16[3,4,2,16,128]{4,3,2,1,0:T(8,128)(2,1)S(1)}, bf16[3,4,2,16,128]{4,3,2,1,0:T(8,128)(2,1)S(1)}, u32[]{:S(2)}, u32[]{:S(2)}) collective-permute-start(bf16[3,4,2,16,128]{4,3,2,1,0:T(8,128)(2,1)S(1)} %shard_map.129.refs_0_), channel_id=1, source_target_pairs={{0,32},{32,0},{1,33},{33,1},{2,34},{34,2},{3,35},{35,3},{4,36},{36... | collective-permute-start | bytes 294920 | tf_op jit(solution)/shard_map/ppermute | solution.py:28
  9.4 10.5 %collective-permute-start = (bf16[3,4,2,16,128]{4,3,2,1,0:T(8,128)(2,1)S(1)}, bf16[3,4,2,16,128]{4,3,2,1,0:T(8,128)(2,1)S(1)}, u32[]{:S(2)}, u32[]{:S(2)}) collective-permute-start(bf16[3,4,2,16,128]{4,3,2,1,0:T(8,128)(2,1)S(1)} %shard_map.129.refs_0_), channel_id=1, source_target_pairs={{0,64},{64,0},{128,192},{192,128},{1,65},{65,1},{129,193},{193,129... | collective-permute-start | bytes 294920 | tf_op jit(solution)/shard_map/ppermute | solution.py:28
  10.7 13.8 %collective-permute-start.1 = (bf16[3,4,2,16,128]{4,3,2,1,0:T(8,128)(2,1)S(1)}, bf16[3,4,2,16,128]{4,3,2,1,0:T(8,128)(2,1)S(1)}, u32[]{:S(2)}, u32[]{:S(2)}) collective-permute-start(bf16[3,4,2,16,128]{4,3,2,1,0:T(8,128)(2,1)S(1)} %shard_map.129.refs_0_), channel_id=1, source_target_pairs={{0,128},{64,192},{128,0},{192,64},{1,129},{65,193},{129,1},{193,65... | collective-permute-start | bytes 294920 | tf_op jit(solution)/shard_map/ppermute | solution.py:28
  13.4 11.2 %collective-permute-start.2 = (bf16[3,4,2,16,128]{4,3,2,1,0:T(8,128)(2,1)S(1)}, bf16[3,4,2,16,128]{4,3,2,1,0:T(8,128)(2,1)S(1)}, u32[]{:S(2)}, u32[]{:S(2)}) collective-permute-start(bf16[3,4,2,16,128]{4,3,2,1,0:T(8,128)(2,1)S(1)} %shard_map.129.refs_0_), channel_id=1, source_target_pairs={{0,192},{64,128},{128,64},{192,0},{1,193},{65,129},{129,65},{193,1... | collective-permute-start | bytes 294920 | tf_op jit(solution)/shard_map/ppermute | solution.py:28
  13.4 6.6 %copy-start.3 = (bf16[3,3,128,128]{3,2,1,0:T(8,128)(2,1)S(1)}, bf16[3,3,128,128]{3,2,1,0:T(8,128)(2,1)}, u32[]{:S(2)}) copy-start(bf16[3,3,128,128]{3,2,1,0:T(8,128)(2,1)} %param.10) | copy-start | bytes 884740
  13.4 6.6 %copy-start.4 = (bf16[3,3,128,128]{3,2,1,0:T(8,128)(2,1)S(1)}, bf16[3,3,128,128]{3,2,1,0:T(8,128)(2,1)}, u32[]{:S(2)}) copy-start(bf16[3,3,128,128]{3,2,1,0:T(8,128)(2,1)} %param.11) | copy-start | bytes 884740
  13.4 6.6 %copy-start.6 = (bf16[1,3,16,16,128]{4,3,2,1,0:T(8,128)(2,1)S(1)}, bf16[1,3,16,16,128]{4,3,2,1,0:T(8,128)(2,1)}, u32[]{:S(2)}) copy-start(bf16[1,3,16,16,128]{4,3,2,1,0:T(8,128)(2,1)} %param.9) | copy-start | bytes 589828
  13.4 6.6 %copy-start.7 = (bf16[1,3,16,16,128]{4,3,2,1,0:T(8,128)(2,1)S(1)}, bf16[1,3,16,16,128]{4,3,2,1,0:T(8,128)(2,1)}, u32[]{:S(2)}) copy-start(bf16[1,3,16,16,128]{4,3,2,1,0:T(8,128)(2,1)} %param.13) | copy-start | bytes 589828
  13.4 6.6 %copy-start.8 = (bf16[2,2,128,128]{3,2,1,0:T(8,128)(2,1)S(1)}, bf16[2,2,128,128]{3,2,1,0:T(8,128)(2,1)}, u32[]{:S(2)}) copy-start(bf16[2,2,128,128]{3,2,1,0:T(8,128)(2,1)} %param.12) | copy-start | bytes 393220
  13.4 6.6 %copy-start.9 = (bf16[1,3,8,8,128]{4,3,2,1,0:T(8,128)(2,1)S(1)}, bf16[1,3,8,8,128]{4,3,2,1,0:T(8,128)(2,1)}, u32[]{:S(2)}) copy-start(bf16[1,3,8,8,128]{4,3,2,1,0:T(8,128)(2,1)} %param.14) | copy-start | bytes 147460
  16.0 8.6 %collective-permute-start.4 = (bf16[3,4,2,16,128]{4,3,2,1,0:T(8,128)(2,1)S(1)}, bf16[3,4,2,16,128]{4,3,2,1,0:T(8,128)(2,1)S(1)}, u32[]{:S(2)}, u32[]{:S(2)}) collective-permute-start(bf16[3,4,2,16,128]{4,3,2,1,0:T(8,128)(2,1)S(1)} %collective-permute-done.3.refs_4_), channel_id=1, source_target_pairs={{0,64},{64,0},{128,192},{192,128},{1,65},{65,1},{129,193},{193,129... | collective-permute-start | bytes 294920 | tf_op jit(solution)/shard_map/ppermute | solution.py:28
  16.1 8.5 %collective-permute-start.5 = (bf16[3,4,2,16,128]{4,3,2,1,0:T(8,128)(2,1)S(1)}, bf16[3,4,2,16,128]{4,3,2,1,0:T(8,128)(2,1)S(1)}, u32[]{:S(2)}, u32[]{:S(2)}) collective-permute-start(bf16[3,4,2,16,128]{4,3,2,1,0:T(8,128)(2,1)S(1)} %collective-permute-done.3.refs_4_), channel_id=1, source_target_pairs={{0,128},{64,192},{128,0},{192,64},{1,129},{65,193},{129,1},{193,65... | collective-permute-start | bytes 294920 | tf_op jit(solution)/shard_map/ppermute | solution.py:28
  19.9 5.7 %collective-permute-start.6 = (bf16[3,4,2,16,128]{4,3,2,1,0:T(8,128)(2,1)S(1)}, bf16[3,4,2,16,128]{4,3,2,1,0:T(8,128)(2,1)S(1)}, u32[]{:S(2)}, u32[]{:S(2)}) collective-permute-start(bf16[3,4,2,16,128]{4,3,2,1,0:T(8,128)(2,1)S(1)} %collective-permute-done.3.refs_4_), channel_id=1, source_target_pairs={{0,192},{64,128},{128,64},{192,0},{1,193},{65,129},{129,65},{193,1... | collective-permute-start | bytes 294920 | tf_op jit(solution)/shard_map/ppermute | solution.py:28
  20.0 0.7 copy-start.1
  24.5 6.2 %copy-start = (bf16[192,192]{1,0:T(8,128)(2,1)S(1)}, bf16[192,192]{1,0:T(8,128)(2,1)}, u32[]{:S(2)}) copy-start(bf16[192,192]{1,0:T(8,128)(2,1)} %get-tuple-element.33.turn_ref) | copy-start | bytes 221188
  26.3 4.5 %collective-permute-start.7 = (bf16[4,2,3,4,2,16,128]{6,5,4,3,2,1,0:T(8,128)(2,1)S(1)}, bf16[4,2,3,4,2,16,128]{6,5,4,3,2,1,0:T(8,128)(2,1)S(1)}, u32[]{:S(2)}, u32[]{:S(2)}) collective-permute-start(bf16[4,2,3,4,2,16,128]{6,5,4,3,2,1,0:T(8,128)(2,1)S(1)} %shard_map.131), channel_id=1, source_target_pairs={{0,16},{16,0},{1,17},{17,1},{2,18},{18,2},{3,19},{19,3},{4,20},{20... | collective-permute-start | bytes 2359304 | tf_op jit(solution)/shard_map/ppermute | solution.py:23
  37.0 2.7 %collective-permute-start.8 = (f32[1408,128]{1,0:T(8,128)S(1)}, f32[1408,128]{1,0:T(8,128)S(1)}, u32[]{:S(2)}, u32[]{:S(2)}) collective-permute-start(f32[1408,128]{1,0:T(8,128)S(1)} %slice_bitcast_fusion), channel_id=1, source_target_pairs={{0,16},{16,0},{1,17},{17,1},{2,18},{18,2},{3,19},{19,3},{4,20},{20... | collective-permute-start | bytes 2162696 | tf_op jit(solution)/shard_map/ppermute | solution.py:23
  37.5 8.7 %collective-permute-start.9 = (bf16[3,4,2,16,128]{4,3,2,1,0:T(8,128)(2,1)S(1)}, bf16[3,4,2,16,128]{4,3,2,1,0:T(8,128)(2,1)S(1)}, u32[]{:S(2)}, u32[]{:S(2)}) collective-permute-start(bf16[3,4,2,16,128]{4,3,2,1,0:T(8,128)(2,1)S(1)} %get-tuple-element.48.own_ref), channel_id=1, source_target_pairs={{0,32},{32,0},{1,33},{33,1},{2,34},{34,2},{3,35},{35,3},{4,36},{36... | collective-permute-start | bytes 294920 | tf_op jit(solution)/shard_map/ppermute | solution.py:28
  40.5 13.7 %all-to-all-start = ((bf16[16,88,128]{2,1,0:T(8,128)(2,1)}), bf16[16,88,128]{2,1,0:T(8,128)(2,1)S(1)}, u32[]{:S(2)}, u32[]{:S(2)}) async-start(bf16[16,88,128]{2,1,0:T(8,128)(2,1)} %bitcast.12), calls=%async_computation | async-start | bytes 720896 | tf_op jit(solution)/shard_map/all_to_all | solution.py:674
  54.9 8.3 %collective-permute-start.10 = (bf16[2,3,4,2,16,128]{5,4,3,2,1,0:T(8,128)(2,1)S(1)}, bf16[2,3,4,2,16,128]{5,4,3,2,1,0:T(8,128)(2,1)S(1)}, u32[]{:S(2)}, u32[]{:S(2)}) collective-permute-start(bf16[2,3,4,2,16,128]{5,4,3,2,1,0:T(8,128)(2,1)S(1)} %get-tuple-element.50.own_ref), channel_id=1, source_target_pairs={{0,64},{64,0},{128,192},{192,128},{1,65},{65,1},{129,193},{193,129... | collective-permute-start | bytes 589832 | tf_op jit(solution)/shard_map/ppermute | solution.py:28
  55.3 9.4 %collective-permute-start.11 = (bf16[2,3,4,2,16,128]{5,4,3,2,1,0:T(8,128)(2,1)S(1)}, bf16[2,3,4,2,16,128]{5,4,3,2,1,0:T(8,128)(2,1)S(1)}, u32[]{:S(2)}, u32[]{:S(2)}) collective-permute-start(bf16[2,3,4,2,16,128]{5,4,3,2,1,0:T(8,128)(2,1)S(1)} %get-tuple-element.50.own_ref), channel_id=1, source_target_pairs={{0,128},{64,192},{128,0},{192,64},{1,129},{65,193},{129,1},{193,65... | collective-permute-start | bytes 589832 | tf_op jit(solution)/shard_map/ppermute | solution.py:28
  57.5 10.6 %collective-permute-start.12 = (bf16[2,3,4,2,16,128]{5,4,3,2,1,0:T(8,128)(2,1)S(1)}, bf16[2,3,4,2,16,128]{5,4,3,2,1,0:T(8,128)(2,1)S(1)}, u32[]{:S(2)}, u32[]{:S(2)}) collective-permute-start(bf16[2,3,4,2,16,128]{5,4,3,2,1,0:T(8,128)(2,1)S(1)} %get-tuple-element.50.own_ref), channel_id=1, source_target_pairs={{0,192},{64,128},{128,64},{192,0},{1,193},{65,129},{129,65},{193,1... | collective-permute-start | bytes 589832 | tf_op jit(solution)/shard_map/ppermute | solution.py:28
  58.8 13.0 %all-to-all-start.1 = ((bf16[8,88,128]{2,1,0:T(8,128)(2,1)}), bf16[8,88,128]{2,1,0:T(8,128)(2,1)S(1)}, u32[]{:S(2)}, u32[]{:S(2)}) async-start(bf16[8,88,128]{2,1,0:T(8,128)(2,1)} %get-tuple-element.49), calls=%async_computation.1 | async-start | bytes 360448 | tf_op jit(solution)/shard_map/all_to_all | solution.py:681
  68.1 12.8 %copy-start.2 = (s32[296]{0:T(512)S(1)}, s32[296]{0:T(512)}, u32[]{:S(2)}) copy-start(s32[296]{0:T(512)} %get-tuple-element.32.index_ref.refs_8_) | copy-start | bytes 3556
  72.8 8.1 %collective-permute-start.13 = (bf16[4,2,3,4,2,16,128]{6,5,4,3,2,1,0:T(8,128)(2,1)}, bf16[4,2,3,4,2,16,128]{6,5,4,3,2,1,0:T(8,128)(2,1)}, u32[]{:S(2)}, u32[]{:S(2)}) collective-permute-start(bf16[4,2,3,4,2,16,128]{6,5,4,3,2,1,0:T(8,128)(2,1)} %get-tuple-element.51), channel_id=1, source_target_pairs={{0,16},{16,0},{1,17},{17,1},{2,18},{18,2},{3,19},{19,3},{4,20},{20... | collective-permute-start | bytes 2359304 | tf_op jit(solution)/shard_map/ppermute | solution.py:23
  77.4 12.4 %all-to-all-start.2 = ((bf16[16,88,128]{2,1,0:T(8,128)(2,1)}), bf16[16,88,128]{2,1,0:T(8,128)(2,1)S(1)}, u32[]{:S(2)}, u32[]{:S(2)}) async-start(bf16[16,88,128]{2,1,0:T(8,128)(2,1)} %get-tuple-element.54), calls=%async_computation.2 | async-start | bytes 720896 | tf_op jit(solution)/shard_map/all_to_all | solution.py:688
  89.9 3.0 %collective-permute-start.14 = (bf16[1408,128]{1,0:T(8,128)(2,1)S(1)}, bf16[1408,128]{1,0:T(8,128)(2,1)S(1)}, u32[]{:S(2)}, u32[]{:S(2)}) collective-permute-start(bf16[1408,128]{1,0:T(8,128)(2,1)S(1)} %shard_map.140.mine_ref), channel_id=1, source_target_pairs={{0,16},{16,0},{1,17},{17,1},{2,18},{18,2},{3,19},{19,3},{4,20},{20... | collective-permute-start | bytes 1081352 | tf_op jit(solution)/shard_map/ppermute | solution.py:23

commit v7 on v6

--- a/solution.py
+++ b/solution.py
@@ -136,7 +136,7 @@
 
 
 def ring_kernel(x_ref, ring_ref, cells_ref):
-    cells_ref[...] = as_rows(x_ref[...]).astype(F32)
+    cells_ref[:768] = as_rows(x_ref[...]).astype(F32)
     for n in range(12):
         for depth in range(2):
             rows = cells_ref[side_cells(n % 3, n // 3, depth), :].astype(BF16)
@@ -249,7 +249,8 @@
         for b in range(2):
             part = spread_down[:, lanes(2 * a + b)].reshape(-1, half, half, CH)
             cot_ref[:, pl.ds(a, half, 2), pl.ds(b, half, 2), :] = part
-    cells_ref[:, lanes(1)] = as_rows(cot_ref[...] + skip_ref[...].astype(F32))
+    spread_rows = cot_ref[:, :EDGE, :EDGE, :]
+    cells_ref[:, lanes(1)] = as_rows(spread_rows + skip_ref[...].astype(F32))
     fill_pad(pad_ref, x_rows.astype(F32))
     windows(pad_ref, cols_ref)
     cells_ref[:, lanes(0)] = dot(cols_ref[...], w1_ref[...])
@@ -313,26 +314,28 @@
         strip_pre_ref[strip(n), :] = pick(wide_ref, n * EDGE, EDGE, index_ref[near_at(n) + 2])
     line_ref[:, 1 : EDGE + 1, :] = seams.reshape(12, EDGE, CH)
     triples(line_ref, line_cols_ref, (0, 1, 2))
-    pre_ref[...] = staged_ref[:, lanes(0)]
+    cells_ref[:768] = staged_ref[:, lanes(0)]
     parts = []
     for side in range(4):
         rows = slice(side * tiles * EDGE, (side + 1) * tiles * EDGE)
         parts.append(dot(line_cols_ref[rows, :], sides_ref[: 3 * CH, lanes(side)]))
-    add_sides(pre_ref, jnp.concatenate(parts, axis=0))
-    fill_pad(pad_ref, gelu(pre_ref[...]).astype(BF16).astype(F32))
+    add_sides(cells_ref, jnp.concatenate(parts, axis=0))
+    first_pre = cells_ref[:768]
+    pre_ref[...] = first_pre
+    fill_pad(pad_ref, gelu(first_pre).astype(BF16).astype(F32))
     put_seams(pad_ref, dot(turn, gelu(strip_pre_ref[...]).astype(BF16)))
     windows(pad_ref, cols2_ref)
     second_pre = dot(cols2_ref[...], early_ref[:, W2])
     delta = (gelu_slope(second_pre) * staged_ref[:, lanes(1)]).astype(BF16)
     delta_ref[...] = delta
-    cells_ref[...] = delta.astype(F32)
+    cells_ref[:768] = delta.astype(F32)
     for n in range(12):
         for depth in range(2):
             rows = cells_ref[side_cells(n % tiles, n // tiles, depth), :]
             delta_ring_ref[n % tiles, n // tiles, depth] = rows.astype(BF16)
             if depth == 0:
                 line_ref[n, 1 : EDGE + 1, :] = rows
-    fine_ref[...] = as_cells(gelu(second_pre).astype(BF16).astype(F32))
+    fine_ref[:, :EDGE, :EDGE, :] = as_cells(gelu(second_pre).astype(BF16).astype(F32))
     half = EDGE // 2
     for a in range(2):
         for b in range(2):
@@ -446,9 +449,9 @@
             cot_ref[at : at + 1, :] += pick(
                 wide_ref, strip_rows + j, 1, index_ref[lateral_at(j) + 2]
             )
-    cells_ref[...] = rest_ref[:768, lanes(1)]
+    cells_ref[:768] = rest_ref[:768, lanes(1)]
     add_sides(cells_ref, turned(turn, jnp.concatenate(rims, axis=0)))
-    delta = gelu_slope(rest_ref[:768, lanes(0)]) * cells_ref[...]
+    delta = gelu_slope(rest_ref[:768, lanes(0)]) * cells_ref[:768]
     fill_pad(pad_ref, delta.astype(BF16).astype(F32))
     windows(pad_ref, cols_ref)
     strip_delta = (gelu_slope(rest_ref[768:, lanes(0)]) * cot_ref[...]).astype(BF16).astype(F32)
@@ -458,9 +461,9 @@
     rims = []
     for n in range(12):
         rims.append(pick(strip_wide_ref, n * EDGE, EDGE, index_ref[near_at(n) + 2]))
-    cells_ref[...] = dot(cols_ref[...], late_ref[:, W1_BACK])
+    cells_ref[:768] = dot(cols_ref[...], late_ref[:, W1_BACK])
     add_sides(cells_ref, turned(turn, jnp.concatenate(rims, axis=0)))
-    out_ref[...] = as_cells(cells_ref[...]).astype(BF16)
+    out_ref[...] = as_cells(cells_ref[:768]).astype(BF16)
 
 
 def first_table_kernel(*refs):
@@ -568,8 +571,9 @@
     all_cols = shape((cells, 9 * CH), BF16)
     cell_rows = shape((cells, CH), F32)
     strip_rows = shape((strips, CH), F32)
+    roomy_rows = shape((cells + EDGE * EDGE, CH), F32)
     flag = shape((8, CH), F32)
-    own_ring = call(ring_kernel, ring, [x], [cell_rows])
+    own_ring = call(ring_kernel, ring, [x], [roomy_rows])
     across = swap_apart(own_ring, "z", 1)
     operands = [
         x,
@@ -601,7 +605,7 @@
         (shape((8,), jnp.int32),) + staged,
         [index] + operands,
         tuple(operands) + staged
-        + (pad, shape(x.shape, F32), all_cols, shape((CH, 4 * CH), BF16)),
+        + (pad, pad, all_cols, shape((CH, 4 * CH), BF16)),
         (len(operands), len(staged)),
         specs=[smem] + [hbm] * 6,
         out_specs=(smem,) + (hbm,) * 3,
@@ -642,8 +646,8 @@
             pad,
             shape((4 * tiles, 3, EDGE + 8, CH), F32),
             wide,
-            shape(x.shape, F32),
-            cell_rows,
+            pad,
+            roomy_rows,
             shape((strips, 3 * CH), BF16),
             shape((9 * CH, 4 * CH), BF16),
         ],
@@ -701,7 +705,7 @@
             shape((strips + 32, 4 * CH), F32),
             wide,
             strip_rows,
-            cell_rows,
+            roomy_rows,
             shape((3 * CH, 4 * CH), BF16),
             shape((6 * CH, 4 * CH), BF16),
         ],

time: 94.6 us -> 94.6 us (level)
  no operation moved by 1% of the time
where the time goes in v7:
time: 94.6 us; the launch traced here: 94.2 us
  starting transfers between devices  44.6 us (47%)
  waiting for transfers between devices  25.8 us (27%)
  Pallas kernels  21.3 us (23%)
  local copies, waits for them, and re-layouts  1.69 us (2%)
    ppermute x11, starting transfers between devices, swap_apart(): return lax.ppermute(block, axis, [(i, i ^ apart) for i in range(number)])  21.8 us
    pallas_call x14, Pallas kernels, call(): pl.pallas_call(kernel, out_shape=outs, in_specs=specs or [vmem] * len(ope...  21.3 us
    ppermute x4, starting transfers between devices, swap_core(): return lax.ppermute(block, 'c', [(0, 1), (1, 0)])  9.23 us
    all_to_all x1, waiting for transfers between devices, shards(): pieces = lax.all_to_all(kept.reshape(plane, part, CH), PLANE, 0, 0)  8.03 us
    ppermute x11, waiting for transfers between devices, swap_apart(): return lax.ppermute(block, axis, [(i, i ^ apart) for i in range(number)])  6 us
    all_to_all x1, starting transfers between devices, shards(): pieces = lax.all_to_all(kept.reshape(plane, part, CH), PLANE, 0, 0)  5.62 us
    all_to_all x1, waiting for transfers between devices, shards(): summed = lax.all_to_all(copies, PLANE, 0, 0).reshape(-1, CH)  4.86 us
    all_to_all x1, starting transfers between devices, shards(): pieces = lax.all_to_all(copies, DEPTH, 0, 0)  4.44 us
  transfers between devices with their start and end apart: 18, of which 8 were waited for; matrix products, arithmetic and copies ran while one was open for 0% of the time, Pallas kernels for 12%

profile of v7, /device:TPU:1, one launch (start us, length us, event | category | flops | bytes accessed | tf_op | source)
XLA Modules:
  0.0 94.2 jit_solution(3245471241862648206)
XLA Ops:
  0.6 0.0 copy-start.5
  0.6 0.9 copy-done.5
  1.6 0.1 shard_map.129.refs_0_
  1.6 7.8 %collective-permute-start.3 = (bf16[3,4,2,16,128]{4,3,2,1,0:T(8,128)(2,1)S(1)}, bf16[3,4,2,16,128]{4,3,2,1,0:T(8,128)(2,1)S(1)}, u32[]{:S(2)}, u32[]{:S(2)}) collective-permute-start(bf16[3,4,2,16,128]{4,3,2,1,0:T(8,128)(2,1)S(1)} %shard_map.129.refs_0_), channel_id=1, source_target_pairs={{0,32},{32,0},{1,33},{33,1},{2,34},{34,2},{3,35},{35,3},{4,36},{36... | collective-permute-start | bytes 294920 | tf_op jit(solution)/shard_map/ppermute | solution.py:28
  9.4 1.3 %collective-permute-start = (bf16[3,4,2,16,128]{4,3,2,1,0:T(8,128)(2,1)S(1)}, bf16[3,4,2,16,128]{4,3,2,1,0:T(8,128)(2,1)S(1)}, u32[]{:S(2)}, u32[]{:S(2)}) collective-permute-start(bf16[3,4,2,16,128]{4,3,2,1,0:T(8,128)(2,1)S(1)} %shard_map.129.refs_0_), channel_id=1, source_target_pairs={{0,64},{64,0},{128,192},{192,128},{1,65},{65,1},{129,193},{193,129... | collective-permute-start | bytes 294920 | tf_op jit(solution)/shard_map/ppermute | solution.py:28
  10.7 2.6 %collective-permute-start.1 = (bf16[3,4,2,16,128]{4,3,2,1,0:T(8,128)(2,1)S(1)}, bf16[3,4,2,16,128]{4,3,2,1,0:T(8,128)(2,1)S(1)}, u32[]{:S(2)}, u32[]{:S(2)}) collective-permute-start(bf16[3,4,2,16,128]{4,3,2,1,0:T(8,128)(2,1)S(1)} %shard_map.129.refs_0_), channel_id=1, source_target_pairs={{0,128},{64,192},{128,0},{192,64},{1,129},{65,193},{129,1},{193,65... | collective-permute-start | bytes 294920 | tf_op jit(solution)/shard_map/ppermute | solution.py:28
  13.4 0.0 collective-permute-start.2
  13.4 0.0 copy-start.7
  13.4 0.0 copy-start.8
  13.4 0.0 copy-start.9
  13.4 2.6 %shard_map.128 = (s32[296]{0:T(512)}, bf16[192,192]{1,0:T(8,128)(2,1)}) custom-call(s32[4,48]{1,0:T(4,128)} %bitcast.32, s32[4,48]{1,0:T(4,128)} %bitcast.33, s32[48]{0:T(128)} %slot_ref.1), custom_call_target="tpu_custom_call" | custom-call | flops 905969664 | bytes 2097152 | tf_op jit(solution)/shard_map/pallas_call | solution.py:558
  16.0 0.0 collective-permute-done.3.refs_4_
  16.0 0.1 collective-permute-start.4
  16.1 3.8 %collective-permute-start.5 = (bf16[3,4,2,16,128]{4,3,2,1,0:T(8,128)(2,1)S(1)}, bf16[3,4,2,16,128]{4,3,2,1,0:T(8,128)(2,1)S(1)}, u32[]{:S(2)}, u32[]{:S(2)}) collective-permute-start(bf16[3,4,2,16,128]{4,3,2,1,0:T(8,128)(2,1)S(1)} %collective-permute-done.3.refs_4_), channel_id=1, source_target_pairs={{0,128},{64,192},{128,0},{192,64},{1,129},{65,193},{129,1},{193,65... | collective-permute-start | bytes 294920 | tf_op jit(solution)/shard_map/ppermute | solution.py:28
  19.9 0.0 collective-permute-done.refs_1_
  19.9 0.0 collective-permute-start.6
  20.0 0.0 copy-start.1
  20.0 0.7 copy-done.1
  20.7 3.9 %shard_map.130 = (s32[8]{0:T(128)S(1)}, bf16[1152,384]{1,0:T(8,128)(2,1)S(1)}, bf16[1152,384]{1,0:T(8,128)(2,1)S(1)}, f32[768,256]{1,0:T(8,128)S(1)}) custom-call(s32[296]{0:T(512)S(1)} %copy-done.1, bf16[3,16,16,128]{3,2,1,0:T(8,128)(2,1)S(1)} %bitcast.27, bf16[3,16,16,128]{3,2,1,0:T(8,128)(2,1)S(1)} %bitcast.28, bf16[192,128]{1,0:T(8,128)(2,1)S(1)} %bitcast.30, ...), custom_call_target="tpu_custom_call" | custom-call | flops 22649241600 | bytes 2097152 | tf_op jit(solution)/shard_map/pallas_call | solution.py:558
  24.5 0.0 copy-start
  24.5 0.0 collective-permute-done.1.refs_2_
  24.6 1.1 %collective-permute-done.6.refs_7_ = bf16[3,4,2,16,128]{4,3,2,1,0:T(8,128)(2,1)S(1)} collective-permute-done((bf16[3,4,2,16,128]{4,3,2,1,0:T(8,128)(2,1)S(1)}, bf16[3,4,2,16,128]{4,3,2,1,0:T(8,128)(2,1)S(1)}, u32[]{:S(2)}, u32[]{:S(2)}) %collective-permute-start.6) | collective-permute-done | bytes 98336 | tf_op jit(solution)/shard_map/ppermute | solution.py:28
  25.7 0.6 shard_map.131
  26.3 2.5 %collective-permute-start.7 = (bf16[4,2,3,4,2,16,128]{6,5,4,3,2,1,0:T(8,128)(2,1)S(1)}, bf16[4,2,3,4,2,16,128]{6,5,4,3,2,1,0:T(8,128)(2,1)S(1)}, u32[]{:S(2)}, u32[]{:S(2)}) collective-permute-start(bf16[4,2,3,4,2,16,128]{6,5,4,3,2,1,0:T(8,128)(2,1)S(1)} %shard_map.131), channel_id=1, source_target_pairs={{0,16},{16,0},{1,17},{17,1},{2,18},{18,2},{3,19},{19,3},{4,20},{20... | collective-permute-start | bytes 2359304 | tf_op jit(solution)/shard_map/ppermute | solution.py:23
  28.8 1.9 %collective-permute-done.7 = bf16[4,2,3,4,2,16,128]{6,5,4,3,2,1,0:T(8,128)(2,1)S(1)} collective-permute-done((bf16[4,2,3,4,2,16,128]{6,5,4,3,2,1,0:T(8,128)(2,1)S(1)}, bf16[4,2,3,4,2,16,128]{6,5,4,3,2,1,0:T(8,128)(2,1)S(1)}, u32[]{:S(2)}, u32[]{:S(2)}) %collective-permute-start.7) | collective-permute-done | bytes 786464 | tf_op jit(solution)/shard_map/ppermute | solution.py:23
  30.7 3.3 %shard_map.132 = (bf16[192,128]{1,0:T(8,128)(2,1)}, bf16[3,4,2,16,128]{4,3,2,1,0:T(8,128)(2,1)S(1)}, f32[768,128]{1,0:T(8,128)S(1)}, f32[192,128]{1,0:T(8,128)S(...) custom-call(s32[296]{0:T(512)S(1)} %copy-done.1, ...), custom_call_target="tpu_custom_call" | custom-call | flops 452984832 | bytes 2097152 | tf_op jit(solution)/shard_map/pallas_call | solution.py:558
  34.0 3.0 %shard_map.133 = (f32[2,1408,128]{2,1,0:T(8,128)S(1)}, f32[960,256]{1,0:T(8,128)S(1)}) custom-call(s32[296]{0:T(512)S(1)} %copy-done.1, bf16[192,192]{1,0:T(8,128)(2,1)S(1)} %copy-done, bf16[1152,384]{1,0:T(8,128)(2,1)S(1)} %get-tuple-element.35.early_ref, bf16[1152,384]{1,0:T(8,128)(2,1)S(1)} %get-tuple-element.38.late_ref, ...), custom_call_target="tpu_custom_call" | custom-call | flops 905969664 | bytes 2097152 | tf_op jit(solution)/shard_map/pallas_call | solution.py:558
  37.0 0.5 collective-permute-start.8
  37.5 2.2 %collective-permute-start.9 = (bf16[3,4,2,16,128]{4,3,2,1,0:T(8,128)(2,1)S(1)}, bf16[3,4,2,16,128]{4,3,2,1,0:T(8,128)(2,1)S(1)}, u32[]{:S(2)}, u32[]{:S(2)}) collective-permute-start(bf16[3,4,2,16,128]{4,3,2,1,0:T(8,128)(2,1)S(1)} %get-tuple-element.48.own_ref), channel_id=1, source_target_pairs={{0,32},{32,0},{1,33},{33,1},{2,34},{34,2},{3,35},{35,3},{4,36},{36... | collective-permute-start | bytes 294920 | tf_op jit(solution)/shard_map/ppermute | solution.py:28
  39.7 0.8 shard_map.134
  40.5 5.6 %all-to-all-start = ((bf16[16,88,128]{2,1,0:T(8,128)(2,1)}), bf16[16,88,128]{2,1,0:T(8,128)(2,1)S(1)}, u32[]{:S(2)}, u32[]{:S(2)}) async-start(bf16[16,88,128]{2,1,0:T(8,128)(2,1)} %bitcast.12), calls=%async_computation | async-start | bytes 720896 | tf_op jit(solution)/shard_map/all_to_all | solution.py:678
  46.2 8.0 %all-to-all-done.pieces_ref = bf16[16,88,128]{2,1,0:T(8,128)(2,1)S(1)} async-done(((bf16[16,88,128]{2,1,0:T(8,128)(2,1)}), bf16[16,88,128]{2,1,0:T(8,128)(2,1)S(1)}, u32[]{:S(2)}, u32[]{:S(2)}) %all-to-all-start) | async-done | bytes 360480 | tf_op jit(solution)/shard_map/all_to_all | solution.py:678
  54.2 0.7 shard_map.136
  54.9 0.3 collective-permute-start.10
  55.3 2.3 %collective-permute-start.11 = (bf16[2,3,4,2,16,128]{5,4,3,2,1,0:T(8,128)(2,1)S(1)}, bf16[2,3,4,2,16,128]{5,4,3,2,1,0:T(8,128)(2,1)S(1)}, u32[]{:S(2)}, u32[]{:S(2)}) collective-permute-start(bf16[2,3,4,2,16,128]{5,4,3,2,1,0:T(8,128)(2,1)S(1)} %get-tuple-element.50.own_ref), channel_id=1, source_target_pairs={{0,128},{64,192},{128,0},{192,64},{1,129},{65,193},{129,1},{193,65... | collective-permute-start | bytes 589832 | tf_op jit(solution)/shard_map/ppermute | solution.py:28
  57.5 1.3 %collective-permute-start.12 = (bf16[2,3,4,2,16,128]{5,4,3,2,1,0:T(8,128)(2,1)S(1)}, bf16[2,3,4,2,16,128]{5,4,3,2,1,0:T(8,128)(2,1)S(1)}, u32[]{:S(2)}, u32[]{:S(2)}) collective-permute-start(bf16[2,3,4,2,16,128]{5,4,3,2,1,0:T(8,128)(2,1)S(1)} %get-tuple-element.50.own_ref), channel_id=1, source_target_pairs={{0,192},{64,128},{128,64},{192,0},{1,193},{65,129},{129,65},{193,1... | collective-permute-start | bytes 589832 | tf_op jit(solution)/shard_map/ppermute | solution.py:28
  58.8 4.4 %all-to-all-start.1 = ((bf16[8,88,128]{2,1,0:T(8,128)(2,1)}), bf16[8,88,128]{2,1,0:T(8,128)(2,1)S(1)}, u32[]{:S(2)}, u32[]{:S(2)}) async-start(bf16[8,88,128]{2,1,0:T(8,128)(2,1)} %get-tuple-element.49), calls=%async_computation.1 | async-start | bytes 360448 | tf_op jit(solution)/shard_map/all_to_all | solution.py:685
  63.2 1.5 %collective-permute-done.11.refs_1_.two_ref = bf16[2,3,4,2,16,128]{5,4,3,2,1,0:T(8,128)(2,1)S(1)} collective-permute-done((bf16[2,3,4,2,16,128]{5,4,3,2,1,0:T(8,128)(2,1)S(1)}, bf16[2,3,4,2,16,128]{5,4,3,2,1,0:T(8,128)(2,1)S(1)}, u32[]{:S(2)}, u32[]{:S(2)}) %collective-permute-start.11) | collective-permute-done | bytes 196640 | tf_op jit(solution)/shard_map/ppermute | solution.py:28
  64.7 3.4 %collective-permute-done.12.refs_2_.three_ref = bf16[2,3,4,2,16,128]{5,4,3,2,1,0:T(8,128)(2,1)S(1)} collective-permute-done((bf16[2,3,4,2,16,128]{5,4,3,2,1,0:T(8,128)(2,1)S(1)}, bf16[2,3,4,2,16,128]{5,4,3,2,1,0:T(8,128)(2,1)S(1)}, u32[]{:S(2)}, u32[]{:S(2)}) %collective-permute-start.12) | collective-permute-done | bytes 196640 | tf_op jit(solution)/shard_map/ppermute | solution.py:28
  68.1 3.6 %all-to-all-done.1.pieces_ref = bf16[8,88,128]{2,1,0:T(8,128)(2,1)S(1)} async-done(((bf16[8,88,128]{2,1,0:T(8,128)(2,1)}), bf16[8,88,128]{2,1,0:T(8,128)(2,1)S(1)}, u32[]{:S(2)}, u32[]{:S(2)}) %all-to-all-start.1) | async-done | bytes 180256 | tf_op jit(solution)/shard_map/all_to_all | solution.py:685
  71.8 1.1 %shard_map.138 = (bf16[16,88,128]{2,1,0:T(8,128)(2,1)}, bf16[4,2,3,4,2,16,128]{6,5,4,3,2,1,0:T(8,128)(2,1)}) custom-call(bf16[8,88,128]{2,1,0:T(8,128)(2,1)S(1)} %all-to-all-done.1.pieces_ref, f32[8,128]{1,0:T(8,128)S(1)} %shard_map.137.flag_ref, bf16[2,3,4,2,16,128]{5,4,3,2,1,0:T(8,128)(2,1)S(1)} %get-tuple-element.50.own_ref, ...), custom_call_target="tpu_custom_call" | custom-call | flops 226492416 | bytes 2097152 | tf_op jit(solution)/shard_map/pallas_call | solution.py:558
  72.9 4.6 %collective-permute-start.13 = (bf16[4,2,3,4,2,16,128]{6,5,4,3,2,1,0:T(8,128)(2,1)}, bf16[4,2,3,4,2,16,128]{6,5,4,3,2,1,0:T(8,128)(2,1)}, u32[]{:S(2)}, u32[]{:S(2)}) collective-permute-start(bf16[4,2,3,4,2,16,128]{6,5,4,3,2,1,0:T(8,128)(2,1)} %get-tuple-element.51), channel_id=1, source_target_pairs={{0,16},{16,0},{1,17},{17,1},{2,18},{18,2},{3,19},{19,3},{4,20},{20... | collective-permute-start | bytes 2359304 | tf_op jit(solution)/shard_map/ppermute | solution.py:23
  77.4 3.5 %all-to-all-start.2 = ((bf16[16,88,128]{2,1,0:T(8,128)(2,1)}), bf16[16,88,128]{2,1,0:T(8,128)(2,1)S(1)}, u32[]{:S(2)}, u32[]{:S(2)}) async-start(bf16[16,88,128]{2,1,0:T(8,128)(2,1)} %get-tuple-element.54), calls=%async_computation.2 | async-start | bytes 720896 | tf_op jit(solution)/shard_map/all_to_all | solution.py:692
  81.0 4.0 %shard_map.139 = (bf16[3,16,16,128]{3,2,1,0:T(8,128)(2,1)}, f32[8,128]{1,0:T(8,128)S(1)}) custom-call(s32[296]{0:T(512)S(1)} %copy-done.2, bf16[192,192]{1,0:T(8,128)(2,1)S(1)} %copy-done, bf16[24,4,2,16,128]{4,3,2,1,0:T(8,128)(2,1)} %bitcast.13.mine_ref, bf16[24,4,2,16,128]{4,3,2,1,0:T(8,128)(2,1)} %bitcast.14.other_ref, ...), custom_call_target="tpu_custom_call" | custom-call | flops 22649241600 | bytes 2097152 | tf_op jit(solution)/shard_map/pallas_call | solution.py:558
  85.0 4.9 %all-to-all-done.2 = bf16[16,88,128]{2,1,0:T(8,128)(2,1)S(1)} async-done(((bf16[16,88,128]{2,1,0:T(8,128)(2,1)}), bf16[16,88,128]{2,1,0:T(8,128)(2,1)S(1)}, u32[]{:S(2)}, u32[]{:S(2)}) %all-to-all-start.2) | async-done | bytes 360480 | tf_op jit(solution)/shard_map/all_to_all | solution.py:692
  89.9 1.7 %collective-permute-start.14 = (bf16[1408,128]{1,0:T(8,128)(2,1)S(1)}, bf16[1408,128]{1,0:T(8,128)(2,1)S(1)}, u32[]{:S(2)}, u32[]{:S(2)}) collective-permute-start(bf16[1408,128]{1,0:T(8,128)(2,1)S(1)} %shard_map.140.mine_ref), channel_id=1, source_target_pairs={{0,16},{16,0},{1,17},{17,1},{2,18},{18,2},{3,19},{19,3},{4,20},{20... | collective-permute-start | bytes 1081352 | tf_op jit(solution)/shard_map/ppermute | solution.py:23
  91.6 1.3 %collective-permute-done.14.other_ref = bf16[1408,128]{1,0:T(8,128)(2,1)S(1)} collective-permute-done((bf16[1408,128]{1,0:T(8,128)(2,1)S(1)}, bf16[1408,128]{1,0:T(8,128)(2,1)S(1)}, u32[]{:S(2)}, u32[]{:S(2)}) %collective-permute-start.14) | collective-permute-done | bytes 360480 | tf_op jit(solution)/shard_map/ppermute | solution.py:23
  92.9 1.3 %shard_map.141 = (f32[9,128,128]{2,1,0:T(8,128)}, f32[9,128,128]{2,1,0:T(8,128)}, f32[4,128,128]{2,1,0:T(8,128)}) custom-call(bf16[1408,128]{1,0:T(8,128)(2,1)S(1)} %shard_map.140.mine_ref, bf16[1408,128]{1,0:T(8,128)(2,1)S(1)} %collective-permute-done.14.other_ref), custom_call_target="tpu_custom_call" | custom-call | flops 226492416 | bytes 2097152 | tf_op jit(solution)/shard_map/pallas_call | solution.py:558
  (23 shorter events, 0.1 us)
Async XLA Ops:
  0.6 0.9 copy-start.5
  1.6 14.4 %collective-permute-start.3 = (bf16[3,4,2,16,128]{4,3,2,1,0:T(8,128)(2,1)S(1)}, bf16[3,4,2,16,128]{4,3,2,1,0:T(8,128)(2,1)S(1)}, u32[]{:S(2)}, u32[]{:S(2)}) collective-permute-start(bf16[3,4,2,16,128]{4,3,2,1,0:T(8,128)(2,1)S(1)} %shard_map.129.refs_0_), channel_id=1, source_target_pairs={{0,32},{32,0},{1,33},{33,1},{2,34},{34,2},{3,35},{35,3},{4,36},{36... | collective-permute-start | bytes 294920 | tf_op jit(solution)/shard_map/ppermute | solution.py:28
  9.4 10.5 %collective-permute-start = (bf16[3,4,2,16,128]{4,3,2,1,0:T(8,128)(2,1)S(1)}, bf16[3,4,2,16,128]{4,3,2,1,0:T(8,128)(2,1)S(1)}, u32[]{:S(2)}, u32[]{:S(2)}) collective-permute-start(bf16[3,4,2,16,128]{4,3,2,1,0:T(8,128)(2,1)S(1)} %shard_map.129.refs_0_), channel_id=1, source_target_pairs={{0,64},{64,0},{128,192},{192,128},{1,65},{65,1},{129,193},{193,129... | collective-permute-start | bytes 294920 | tf_op jit(solution)/shard_map/ppermute | solution.py:28
  10.7 13.8 %collective-permute-start.1 = (bf16[3,4,2,16,128]{4,3,2,1,0:T(8,128)(2,1)S(1)}, bf16[3,4,2,16,128]{4,3,2,1,0:T(8,128)(2,1)S(1)}, u32[]{:S(2)}, u32[]{:S(2)}) collective-permute-start(bf16[3,4,2,16,128]{4,3,2,1,0:T(8,128)(2,1)S(1)} %shard_map.129.refs_0_), channel_id=1, source_target_pairs={{0,128},{64,192},{128,0},{192,64},{1,129},{65,193},{129,1},{193,65... | collective-permute-start | bytes 294920 | tf_op jit(solution)/shard_map/ppermute | solution.py:28
  13.4 11.2 %collective-permute-start.2 = (bf16[3,4,2,16,128]{4,3,2,1,0:T(8,128)(2,1)S(1)}, bf16[3,4,2,16,128]{4,3,2,1,0:T(8,128)(2,1)S(1)}, u32[]{:S(2)}, u32[]{:S(2)}) collective-permute-start(bf16[3,4,2,16,128]{4,3,2,1,0:T(8,128)(2,1)S(1)} %shard_map.129.refs_0_), channel_id=1, source_target_pairs={{0,192},{64,128},{128,64},{192,0},{1,193},{65,129},{129,65},{193,1... | collective-permute-start | bytes 294920 | tf_op jit(solution)/shard_map/ppermute | solution.py:28
  13.4 6.6 %copy-start.3 = (bf16[3,3,128,128]{3,2,1,0:T(8,128)(2,1)S(1)}, bf16[3,3,128,128]{3,2,1,0:T(8,128)(2,1)}, u32[]{:S(2)}) copy-start(bf16[3,3,128,128]{3,2,1,0:T(8,128)(2,1)} %param.10) | copy-start | bytes 884740
  13.4 6.6 %copy-start.4 = (bf16[3,3,128,128]{3,2,1,0:T(8,128)(2,1)S(1)}, bf16[3,3,128,128]{3,2,1,0:T(8,128)(2,1)}, u32[]{:S(2)}) copy-start(bf16[3,3,128,128]{3,2,1,0:T(8,128)(2,1)} %param.11) | copy-start | bytes 884740
  13.4 6.6 %copy-start.6 = (bf16[1,3,16,16,128]{4,3,2,1,0:T(8,128)(2,1)S(1)}, bf16[1,3,16,16,128]{4,3,2,1,0:T(8,128)(2,1)}, u32[]{:S(2)}) copy-start(bf16[1,3,16,16,128]{4,3,2,1,0:T(8,128)(2,1)} %param.9) | copy-start | bytes 589828
  13.4 6.6 %copy-start.7 = (bf16[1,3,16,16,128]{4,3,2,1,0:T(8,128)(2,1)S(1)}, bf16[1,3,16,16,128]{4,3,2,1,0:T(8,128)(2,1)}, u32[]{:S(2)}) copy-start(bf16[1,3,16,16,128]{4,3,2,1,0:T(8,128)(2,1)} %param.13) | copy-start | bytes 589828
  13.4 6.6 %copy-start.8 = (bf16[2,2,128,128]{3,2,1,0:T(8,128)(2,1)S(1)}, bf16[2,2,128,128]{3,2,1,0:T(8,128)(2,1)}, u32[]{:S(2)}) copy-start(bf16[2,2,128,128]{3,2,1,0:T(8,128)(2,1)} %param.12) | copy-start | bytes 393220
  13.4 6.6 %copy-start.9 = (bf16[1,3,8,8,128]{4,3,2,1,0:T(8,128)(2,1)S(1)}, bf16[1,3,8,8,128]{4,3,2,1,0:T(8,128)(2,1)}, u32[]{:S(2)}) copy-start(bf16[1,3,8,8,128]{4,3,2,1,0:T(8,128)(2,1)} %param.14) | copy-start | bytes 147460
  16.0 8.6 %collective-permute-start.4 = (bf16[3,4,2,16,128]{4,3,2,1,0:T(8,128)(2,1)S(1)}, bf16[3,4,2,16,128]{4,3,2,1,0:T(8,128)(2,1)S(1)}, u32[]{:S(2)}, u32[]{:S(2)}) collective-permute-start(bf16[3,4,2,16,128]{4,3,2,1,0:T(8,128)(2,1)S(1)} %collective-permute-done.3.refs_4_), channel_id=1, source_target_pairs={{0,64},{64,0},{128,192},{192,128},{1,65},{65,1},{129,193},{193,129... | collective-permute-start | bytes 294920 | tf_op jit(solution)/shard_map/ppermute | solution.py:28
  16.1 8.5 %collective-permute-start.5 = (bf16[3,4,2,16,128]{4,3,2,1,0:T(8,128)(2,1)S(1)}, bf16[3,4,2,16,128]{4,3,2,1,0:T(8,128)(2,1)S(1)}, u32[]{:S(2)}, u32[]{:S(2)}) collective-permute-start(bf16[3,4,2,16,128]{4,3,2,1,0:T(8,128)(2,1)S(1)} %collective-permute-done.3.refs_4_), channel_id=1, source_target_pairs={{0,128},{64,192},{128,0},{192,64},{1,129},{65,193},{129,1},{193,65... | collective-permute-start | bytes 294920 | tf_op jit(solution)/shard_map/ppermute | solution.py:28
  19.9 5.7 %collective-permute-start.6 = (bf16[3,4,2,16,128]{4,3,2,1,0:T(8,128)(2,1)S(1)}, bf16[3,4,2,16,128]{4,3,2,1,0:T(8,128)(2,1)S(1)}, u32[]{:S(2)}, u32[]{:S(2)}) collective-permute-start(bf16[3,4,2,16,128]{4,3,2,1,0:T(8,128)(2,1)S(1)} %collective-permute-done.3.refs_4_), channel_id=1, source_target_pairs={{0,192},{64,128},{128,64},{192,0},{1,193},{65,129},{129,65},{193,1... | collective-permute-start | bytes 294920 | tf_op jit(solution)/shard_map/ppermute | solution.py:28
  20.0 0.7 copy-start.1
  24.5 6.2 %copy-start = (bf16[192,192]{1,0:T(8,128)(2,1)S(1)}, bf16[192,192]{1,0:T(8,128)(2,1)}, u32[]{:S(2)}) copy-start(bf16[192,192]{1,0:T(8,128)(2,1)} %get-tuple-element.33.turn_ref) | copy-start | bytes 221188
  26.3 4.5 %collective-permute-start.7 = (bf16[4,2,3,4,2,16,128]{6,5,4,3,2,1,0:T(8,128)(2,1)S(1)}, bf16[4,2,3,4,2,16,128]{6,5,4,3,2,1,0:T(8,128)(2,1)S(1)}, u32[]{:S(2)}, u32[]{:S(2)}) collective-permute-start(bf16[4,2,3,4,2,16,128]{6,5,4,3,2,1,0:T(8,128)(2,1)S(1)} %shard_map.131), channel_id=1, source_target_pairs={{0,16},{16,0},{1,17},{17,1},{2,18},{18,2},{3,19},{19,3},{4,20},{20... | collective-permute-start | bytes 2359304 | tf_op jit(solution)/shard_map/ppermute | solution.py:23
  37.0 2.7 %collective-permute-start.8 = (f32[1408,128]{1,0:T(8,128)S(1)}, f32[1408,128]{1,0:T(8,128)S(1)}, u32[]{:S(2)}, u32[]{:S(2)}) collective-permute-start(f32[1408,128]{1,0:T(8,128)S(1)} %slice_bitcast_fusion), channel_id=1, source_target_pairs={{0,16},{16,0},{1,17},{17,1},{2,18},{18,2},{3,19},{19,3},{4,20},{20... | collective-permute-start | bytes 2162696 | tf_op jit(solution)/shard_map/ppermute | solution.py:23
  37.5 8.7 %collective-permute-start.9 = (bf16[3,4,2,16,128]{4,3,2,1,0:T(8,128)(2,1)S(1)}, bf16[3,4,2,16,128]{4,3,2,1,0:T(8,128)(2,1)S(1)}, u32[]{:S(2)}, u32[]{:S(2)}) collective-permute-start(bf16[3,4,2,16,128]{4,3,2,1,0:T(8,128)(2,1)S(1)} %get-tuple-element.48.own_ref), channel_id=1, source_target_pairs={{0,32},{32,0},{1,33},{33,1},{2,34},{34,2},{3,35},{35,3},{4,36},{36... | collective-permute-start | bytes 294920 | tf_op jit(solution)/shard_map/ppermute | solution.py:28
  40.5 13.7 %all-to-all-start = ((bf16[16,88,128]{2,1,0:T(8,128)(2,1)}), bf16[16,88,128]{2,1,0:T(8,128)(2,1)S(1)}, u32[]{:S(2)}, u32[]{:S(2)}) async-start(bf16[16,88,128]{2,1,0:T(8,128)(2,1)} %bitcast.12), calls=%async_computation | async-start | bytes 720896 | tf_op jit(solution)/shard_map/all_to_all | solution.py:678
  54.9 8.3 %collective-permute-start.10 = (bf16[2,3,4,2,16,128]{5,4,3,2,1,0:T(8,128)(2,1)S(1)}, bf16[2,3,4,2,16,128]{5,4,3,2,1,0:T(8,128)(2,1)S(1)}, u32[]{:S(2)}, u32[]{:S(2)}) collective-permute-start(bf16[2,3,4,2,16,128]{5,4,3,2,1,0:T(8,128)(2,1)S(1)} %get-tuple-element.50.own_ref), channel_id=1, source_target_pairs={{0,64},{64,0},{128,192},{192,128},{1,65},{65,1},{129,193},{193,129... | collective-permute-start | bytes 589832 | tf_op jit(solution)/shard_map/ppermute | solution.py:28
  55.3 9.4 %collective-permute-start.11 = (bf16[2,3,4,2,16,128]{5,4,3,2,1,0:T(8,128)(2,1)S(1)}, bf16[2,3,4,2,16,128]{5,4,3,2,1,0:T(8,128)(2,1)S(1)}, u32[]{:S(2)}, u32[]{:S(2)}) collective-permute-start(bf16[2,3,4,2,16,128]{5,4,3,2,1,0:T(8,128)(2,1)S(1)} %get-tuple-element.50.own_ref), channel_id=1, source_target_pairs={{0,128},{64,192},{128,0},{192,64},{1,129},{65,193},{129,1},{193,65... | collective-permute-start | bytes 589832 | tf_op jit(solution)/shard_map/ppermute | solution.py:28
  57.5 10.6 %collective-permute-start.12 = (bf16[2,3,4,2,16,128]{5,4,3,2,1,0:T(8,128)(2,1)S(1)}, bf16[2,3,4,2,16,128]{5,4,3,2,1,0:T(8,128)(2,1)S(1)}, u32[]{:S(2)}, u32[]{:S(2)}) collective-permute-start(bf16[2,3,4,2,16,128]{5,4,3,2,1,0:T(8,128)(2,1)S(1)} %get-tuple-element.50.own_ref), channel_id=1, source_target_pairs={{0,192},{64,128},{128,64},{192,0},{1,193},{65,129},{129,65},{193,1... | collective-permute-start | bytes 589832 | tf_op jit(solution)/shard_map/ppermute | solution.py:28
  58.8 13.0 %all-to-all-start.1 = ((bf16[8,88,128]{2,1,0:T(8,128)(2,1)}), bf16[8,88,128]{2,1,0:T(8,128)(2,1)S(1)}, u32[]{:S(2)}, u32[]{:S(2)}) async-start(bf16[8,88,128]{2,1,0:T(8,128)(2,1)} %get-tuple-element.49), calls=%async_computation.1 | async-start | bytes 360448 | tf_op jit(solution)/shard_map/all_to_all | solution.py:685
  68.1 12.9 %copy-start.2 = (s32[296]{0:T(512)S(1)}, s32[296]{0:T(512)}, u32[]{:S(2)}) copy-start(s32[296]{0:T(512)} %get-tuple-element.32.index_ref.refs_8_) | copy-start | bytes 3556
  72.9 8.1 %collective-permute-start.13 = (bf16[4,2,3,4,2,16,128]{6,5,4,3,2,1,0:T(8,128)(2,1)}, bf16[4,2,3,4,2,16,128]{6,5,4,3,2,1,0:T(8,128)(2,1)}, u32[]{:S(2)}, u32[]{:S(2)}) collective-permute-start(bf16[4,2,3,4,2,16,128]{6,5,4,3,2,1,0:T(8,128)(2,1)} %get-tuple-element.51), channel_id=1, source_target_pairs={{0,16},{16,0},{1,17},{17,1},{2,18},{18,2},{3,19},{19,3},{4,20},{20... | collective-permute-start | bytes 2359304 | tf_op jit(solution)/shard_map/ppermute | solution.py:23
  77.4 12.4 %all-to-all-start.2 = ((bf16[16,88,128]{2,1,0:T(8,128)(2,1)}), bf16[16,88,128]{2,1,0:T(8,128)(2,1)S(1)}, u32[]{:S(2)}, u32[]{:S(2)}) async-start(bf16[16,88,128]{2,1,0:T(8,128)(2,1)} %get-tuple-element.54), calls=%async_computation.2 | async-start | bytes 720896 | tf_op jit(solution)/shard_map/all_to_all | solution.py:692
  89.9 3.0 %collective-permute-start.14 = (bf16[1408,128]{1,0:T(8,128)(2,1)S(1)}, bf16[1408,128]{1,0:T(8,128)(2,1)S(1)}, u32[]{:S(2)}, u32[]{:S(2)}) collective-permute-start(bf16[1408,128]{1,0:T(8,128)(2,1)S(1)} %shard_map.140.mine_ref), channel_id=1, source_target_pairs={{0,16},{16,0},{1,17},{17,1},{2,18},{18,2},{3,19},{19,3},{4,20},{20... | collective-permute-start | bytes 1081352 | tf_op jit(solution)/shard_map/ppermute | solution.py:23

commit v8 on v7

--- a/solution.py
+++ b/solution.py
@@ -509,7 +509,11 @@
     out_ref[...] = block_ref[...]
 
 
-def finish_kernel(scale, mine_ref, other_ref, first_ref, second_ref, down_ref):
+def finish_kernel(
+    scale, mine_ref, other_ref, first_hbm, second_hbm, down_hbm, first_ref, second_ref, down_ref,
+    sems,
+):
+    copies = []
     core = lax.axis_index("c")
     for at in range(22):
         half = at // 11
@@ -517,6 +521,11 @@
         block = jnp.where(core == half, mine_ref[rows, :], other_ref[rows, :])
         out_ref, base = ((first_ref, 0), (second_ref, 9), (down_ref, 18))[at // 9]
         out_ref[at - base] = block.astype(F32) * scale
+        if at in (8, 17, 21):
+            out_hbm = (first_hbm, second_hbm, down_hbm)[at // 9]
+            copies.append(pltpu.make_async_copy(out_ref, out_hbm, sems.at[at // 9]))
+            copies[-1].start()
+    finish(copies)
 
 
 def whole(space):
@@ -718,6 +727,9 @@
         functools.partial(finish_kernel, scale),
         tuple(shape((count, CH, CH), F32) for count in (9, 9, 4)),
         [summed, swap_core(summed)],
+        [shape((count, CH, CH), F32) for count in (9, 9, 4)],
+        (3,),
+        out_specs=(hbm,) * 3,
     )
     return (
         coarse.reshape((1, tiles, half, half, CH)),

time: 94.6 us -> 94.7 us (level)
  no operation moved by 1% of the time
where the time goes in v8:
time: 94.7 us; the launch traced here: 94.3 us
  starting transfers between devices  44.6 us (47%)
  waiting for transfers between devices  25.8 us (27%)
  Pallas kernels  21.2 us (22%)
  local copies, waits for them, and re-layouts  1.69 us (2%)
  between operations  1.02 us (1%)
    ppermute x11, starting transfers between devices, swap_apart(): return lax.ppermute(block, axis, [(i, i ^ apart) for i in range(number)])  21.8 us
    pallas_call x14, Pallas kernels, call(): pl.pallas_call(kernel, out_shape=outs, in_specs=specs or [vmem] * len(ope...  21.2 us
    ppermute x4, starting transfers between devices, swap_core(): return lax.ppermute(block, 'c', [(0, 1), (1, 0)])  9.24 us
    all_to_all x1, waiting for transfers between devices, shards(): pieces = lax.all_to_all(kept.reshape(plane, part, CH), PLANE, 0, 0)  8.03 us
    ppermute x11, waiting for transfers between devices, swap_apart(): return lax.ppermute(block, axis, [(i, i ^ apart) for i in range(number)])  6 us
    all_to_all x1, starting transfers between devices, shards(): pieces = lax.all_to_all(kept.reshape(plane, part, CH), PLANE, 0, 0)  5.62 us
    all_to_all x1, waiting for transfers between devices, shards(): summed = lax.all_to_all(copies, PLANE, 0, 0).reshape(-1, CH)  4.86 us
    all_to_all x1, starting transfers between devices, shards(): pieces = lax.all_to_all(copies, DEPTH, 0, 0)  4.44 us
  transfers between devices with their start and end apart: 18, of which 8 were waited for; matrix products, arithmetic and copies ran while one was open for 0% of the time, Pallas kernels for 12%

profile of v8, /device:TPU:1, one launch (start us, length us, event | category | flops | bytes accessed | tf_op | source)
XLA Modules:
  0.0 94.3 jit_solution(17890580891407014451)
XLA Ops:
  0.6 0.0 copy-start.5
  0.6 0.9 copy-done.5
  1.6 0.1 shard_map.129.refs_0_
  1.6 7.8 %collective-permute-start.3 = (bf16[3,4,2,16,128]{4,3,2,1,0:T(8,128)(2,1)S(1)}, bf16[3,4,2,16,128]{4,3,2,1,0:T(8,128)(2,1)S(1)}, u32[]{:S(2)}, u32[]{:S(2)}) collective-permute-start(bf16[3,4,2,16,128]{4,3,2,1,0:T(8,128)(2,1)S(1)} %shard_map.129.refs_0_), channel_id=1, source_target_pairs={{0,32},{32,0},{1,33},{33,1},{2,34},{34,2},{3,35},{35,3},{4,36},{36... | collective-permute-start | bytes 294920 | tf_op jit(solution)/shard_map/ppermute | solution.py:28
  9.4 1.3 %collective-permute-start = (bf16[3,4,2,16,128]{4,3,2,1,0:T(8,128)(2,1)S(1)}, bf16[3,4,2,16,128]{4,3,2,1,0:T(8,128)(2,1)S(1)}, u32[]{:S(2)}, u32[]{:S(2)}) collective-permute-start(bf16[3,4,2,16,128]{4,3,2,1,0:T(8,128)(2,1)S(1)} %shard_map.129.refs_0_), channel_id=1, source_target_pairs={{0,64},{64,0},{128,192},{192,128},{1,65},{65,1},{129,193},{193,129... | collective-permute-start | bytes 294920 | tf_op jit(solution)/shard_map/ppermute | solution.py:28
  10.7 2.6 %collective-permute-start.1 = (bf16[3,4,2,16,128]{4,3,2,1,0:T(8,128)(2,1)S(1)}, bf16[3,4,2,16,128]{4,3,2,1,0:T(8,128)(2,1)S(1)}, u32[]{:S(2)}, u32[]{:S(2)}) collective-permute-start(bf16[3,4,2,16,128]{4,3,2,1,0:T(8,128)(2,1)S(1)} %shard_map.129.refs_0_), channel_id=1, source_target_pairs={{0,128},{64,192},{128,0},{192,64},{1,129},{65,193},{129,1},{193,65... | collective-permute-start | bytes 294920 | tf_op jit(solution)/shard_map/ppermute | solution.py:28
  13.4 0.0 copy-start.7
  13.4 0.0 copy-start.8
  13.4 0.0 copy-start.9
  13.4 2.6 %shard_map.128 = (s32[296]{0:T(512)}, bf16[192,192]{1,0:T(8,128)(2,1)}) custom-call(s32[4,48]{1,0:T(4,128)} %bitcast.32, s32[4,48]{1,0:T(4,128)} %bitcast.33, s32[48]{0:T(128)} %slot_ref.1), custom_call_target="tpu_custom_call" | custom-call | flops 905969664 | bytes 2097152 | tf_op jit(solution)/shard_map/pallas_call | solution.py:567
  16.0 0.1 collective-permute-start.4
  16.1 3.8 %collective-permute-start.5 = (bf16[3,4,2,16,128]{4,3,2,1,0:T(8,128)(2,1)S(1)}, bf16[3,4,2,16,128]{4,3,2,1,0:T(8,128)(2,1)S(1)}, u32[]{:S(2)}, u32[]{:S(2)}) collective-permute-start(bf16[3,4,2,16,128]{4,3,2,1,0:T(8,128)(2,1)S(1)} %collective-permute-done.3.refs_4_), channel_id=1, source_target_pairs={{0,128},{64,192},{128,0},{192,64},{1,129},{65,193},{129,1},{193,65... | collective-permute-start | bytes 294920 | tf_op jit(solution)/shard_map/ppermute | solution.py:28
  19.9 0.0 collective-permute-done.refs_1_
  19.9 0.0 collective-permute-start.6
  20.0 0.0 copy-start.1
  20.0 0.7 copy-done.1
  20.7 3.9 %shard_map.130 = (s32[8]{0:T(128)S(1)}, bf16[1152,384]{1,0:T(8,128)(2,1)S(1)}, bf16[1152,384]{1,0:T(8,128)(2,1)S(1)}, f32[768,256]{1,0:T(8,128)S(1)}) custom-call(s32[296]{0:T(512)S(1)} %copy-done.1, bf16[3,16,16,128]{3,2,1,0:T(8,128)(2,1)S(1)} %bitcast.27, bf16[3,16,16,128]{3,2,1,0:T(8,128)(2,1)S(1)} %bitcast.28, bf16[192,128]{1,0:T(8,128)(2,1)S(1)} %bitcast.30, ...), custom_call_target="tpu_custom_call" | custom-call | flops 22649241600 | bytes 2097152 | tf_op jit(solution)/shard_map/pallas_call | solution.py:567
  24.5 0.0 copy-start
  24.5 0.0 collective-permute-done.1.refs_2_
  24.5 0.0 collective-permute-done.2.refs_3_
  24.6 0.0 collective-permute-done.5.refs_6_
  24.6 1.1 %collective-permute-done.6.refs_7_ = bf16[3,4,2,16,128]{4,3,2,1,0:T(8,128)(2,1)S(1)} collective-permute-done((bf16[3,4,2,16,128]{4,3,2,1,0:T(8,128)(2,1)S(1)}, bf16[3,4,2,16,128]{4,3,2,1,0:T(8,128)(2,1)S(1)}, u32[]{:S(2)}, u32[]{:S(2)}) %collective-permute-start.6) | collective-permute-done | bytes 98336 | tf_op jit(solution)/shard_map/ppermute | solution.py:28
  25.7 0.6 shard_map.131
  26.3 2.5 %collective-permute-start.7 = (bf16[4,2,3,4,2,16,128]{6,5,4,3,2,1,0:T(8,128)(2,1)S(1)}, bf16[4,2,3,4,2,16,128]{6,5,4,3,2,1,0:T(8,128)(2,1)S(1)}, u32[]{:S(2)}, u32[]{:S(2)}) collective-permute-start(bf16[4,2,3,4,2,16,128]{6,5,4,3,2,1,0:T(8,128)(2,1)S(1)} %shard_map.131), channel_id=1, source_target_pairs={{0,16},{16,0},{1,17},{17,1},{2,18},{18,2},{3,19},{19,3},{4,20},{20... | collective-permute-start | bytes 2359304 | tf_op jit(solution)/shard_map/ppermute | solution.py:23
  28.8 1.9 %collective-permute-done.7 = bf16[4,2,3,4,2,16,128]{6,5,4,3,2,1,0:T(8,128)(2,1)S(1)} collective-permute-done((bf16[4,2,3,4,2,16,128]{6,5,4,3,2,1,0:T(8,128)(2,1)S(1)}, bf16[4,2,3,4,2,16,128]{6,5,4,3,2,1,0:T(8,128)(2,1)S(1)}, u32[]{:S(2)}, u32[]{:S(2)}) %collective-permute-start.7) | collective-permute-done | bytes 786464 | tf_op jit(solution)/shard_map/ppermute | solution.py:23
  30.7 3.3 %shard_map.132 = (bf16[192,128]{1,0:T(8,128)(2,1)}, bf16[3,4,2,16,128]{4,3,2,1,0:T(8,128)(2,1)S(1)}, f32[768,128]{1,0:T(8,128)S(1)}, f32[192,128]{1,0:T(8,128)S(...) custom-call(s32[296]{0:T(512)S(1)} %copy-done.1, ...), custom_call_target="tpu_custom_call" | custom-call | flops 452984832 | bytes 2097152 | tf_op jit(solution)/shard_map/pallas_call | solution.py:567
  34.0 2.9 %shard_map.133 = (f32[2,1408,128]{2,1,0:T(8,128)S(1)}, f32[960,256]{1,0:T(8,128)S(1)}) custom-call(s32[296]{0:T(512)S(1)} %copy-done.1, bf16[192,192]{1,0:T(8,128)(2,1)S(1)} %copy-done, bf16[1152,384]{1,0:T(8,128)(2,1)S(1)} %get-tuple-element.35.early_ref, bf16[1152,384]{1,0:T(8,128)(2,1)S(1)} %get-tuple-element.38.late_ref, ...), custom_call_target="tpu_custom_call" | custom-call | flops 905969664 | bytes 2097152 | tf_op jit(solution)/shard_map/pallas_call | solution.py:567
  37.0 0.5 collective-permute-start.8
  37.5 2.2 %collective-permute-start.9 = (bf16[3,4,2,16,128]{4,3,2,1,0:T(8,128)(2,1)S(1)}, bf16[3,4,2,16,128]{4,3,2,1,0:T(8,128)(2,1)S(1)}, u32[]{:S(2)}, u32[]{:S(2)}) collective-permute-start(bf16[3,4,2,16,128]{4,3,2,1,0:T(8,128)(2,1)S(1)} %get-tuple-element.48.own_ref), channel_id=1, source_target_pairs={{0,32},{32,0},{1,33},{33,1},{2,34},{34,2},{3,35},{35,3},{4,36},{36... | collective-permute-start | bytes 294920 | tf_op jit(solution)/shard_map/ppermute | solution.py:28
  39.7 0.8 shard_map.134
  40.5 5.6 %all-to-all-start = ((bf16[16,88,128]{2,1,0:T(8,128)(2,1)}), bf16[16,88,128]{2,1,0:T(8,128)(2,1)S(1)}, u32[]{:S(2)}, u32[]{:S(2)}) async-start(bf16[16,88,128]{2,1,0:T(8,128)(2,1)} %bitcast.12), calls=%async_computation | async-start | bytes 720896 | tf_op jit(solution)/shard_map/all_to_all | solution.py:687
  46.2 8.0 %all-to-all-done.pieces_ref = bf16[16,88,128]{2,1,0:T(8,128)(2,1)S(1)} async-done(((bf16[16,88,128]{2,1,0:T(8,128)(2,1)}), bf16[16,88,128]{2,1,0:T(8,128)(2,1)S(1)}, u32[]{:S(2)}, u32[]{:S(2)}) %all-to-all-start) | async-done | bytes 360480 | tf_op jit(solution)/shard_map/all_to_all | solution.py:687
  54.2 0.7 shard_map.136
  54.9 0.3 collective-permute-start.10
  55.3 2.3 %collective-permute-start.11 = (bf16[2,3,4,2,16,128]{5,4,3,2,1,0:T(8,128)(2,1)S(1)}, bf16[2,3,4,2,16,128]{5,4,3,2,1,0:T(8,128)(2,1)S(1)}, u32[]{:S(2)}, u32[]{:S(2)}) collective-permute-start(bf16[2,3,4,2,16,128]{5,4,3,2,1,0:T(8,128)(2,1)S(1)} %get-tuple-element.50.own_ref), channel_id=1, source_target_pairs={{0,128},{64,192},{128,0},{192,64},{1,129},{65,193},{129,1},{193,65... | collective-permute-start | bytes 589832 | tf_op jit(solution)/shard_map/ppermute | solution.py:28
  57.5 1.3 %collective-permute-start.12 = (bf16[2,3,4,2,16,128]{5,4,3,2,1,0:T(8,128)(2,1)S(1)}, bf16[2,3,4,2,16,128]{5,4,3,2,1,0:T(8,128)(2,1)S(1)}, u32[]{:S(2)}, u32[]{:S(2)}) collective-permute-start(bf16[2,3,4,2,16,128]{5,4,3,2,1,0:T(8,128)(2,1)S(1)} %get-tuple-element.50.own_ref), channel_id=1, source_target_pairs={{0,192},{64,128},{128,64},{192,0},{1,193},{65,129},{129,65},{193,1... | collective-permute-start | bytes 589832 | tf_op jit(solution)/shard_map/ppermute | solution.py:28
  58.8 4.4 %all-to-all-start.1 = ((bf16[8,88,128]{2,1,0:T(8,128)(2,1)}), bf16[8,88,128]{2,1,0:T(8,128)(2,1)S(1)}, u32[]{:S(2)}, u32[]{:S(2)}) async-start(bf16[8,88,128]{2,1,0:T(8,128)(2,1)} %get-tuple-element.49), calls=%async_computation.1 | async-start | bytes 360448 | tf_op jit(solution)/shard_map/all_to_all | solution.py:694
  63.2 1.5 %collective-permute-done.11.refs_1_.two_ref = bf16[2,3,4,2,16,128]{5,4,3,2,1,0:T(8,128)(2,1)S(1)} collective-permute-done((bf16[2,3,4,2,16,128]{5,4,3,2,1,0:T(8,128)(2,1)S(1)}, bf16[2,3,4,2,16,128]{5,4,3,2,1,0:T(8,128)(2,1)S(1)}, u32[]{:S(2)}, u32[]{:S(2)}) %collective-permute-start.11) | collective-permute-done | bytes 196640 | tf_op jit(solution)/shard_map/ppermute | solution.py:28
  64.7 3.4 %collective-permute-done.12.refs_2_.three_ref = bf16[2,3,4,2,16,128]{5,4,3,2,1,0:T(8,128)(2,1)S(1)} collective-permute-done((bf16[2,3,4,2,16,128]{5,4,3,2,1,0:T(8,128)(2,1)S(1)}, bf16[2,3,4,2,16,128]{5,4,3,2,1,0:T(8,128)(2,1)S(1)}, u32[]{:S(2)}, u32[]{:S(2)}) %collective-permute-start.12) | collective-permute-done | bytes 196640 | tf_op jit(solution)/shard_map/ppermute | solution.py:28
  68.1 3.6 %all-to-all-done.1.pieces_ref = bf16[8,88,128]{2,1,0:T(8,128)(2,1)S(1)} async-done(((bf16[8,88,128]{2,1,0:T(8,128)(2,1)}), bf16[8,88,128]{2,1,0:T(8,128)(2,1)S(1)}, u32[]{:S(2)}, u32[]{:S(2)}) %all-to-all-start.1) | async-done | bytes 180256 | tf_op jit(solution)/shard_map/all_to_all | solution.py:694
  71.8 1.1 %shard_map.138 = (bf16[16,88,128]{2,1,0:T(8,128)(2,1)}, bf16[4,2,3,4,2,16,128]{6,5,4,3,2,1,0:T(8,128)(2,1)}) custom-call(bf16[8,88,128]{2,1,0:T(8,128)(2,1)S(1)} %all-to-all-done.1.pieces_ref, f32[8,128]{1,0:T(8,128)S(1)} %shard_map.137.flag_ref, bf16[2,3,4,2,16,128]{5,4,3,2,1,0:T(8,128)(2,1)S(1)} %get-tuple-element.50.own_ref, ...), custom_call_target="tpu_custom_call" | custom-call | flops 226492416 | bytes 2097152 | tf_op jit(solution)/shard_map/pallas_call | solution.py:567
  72.9 4.6 %collective-permute-start.13 = (bf16[4,2,3,4,2,16,128]{6,5,4,3,2,1,0:T(8,128)(2,1)}, bf16[4,2,3,4,2,16,128]{6,5,4,3,2,1,0:T(8,128)(2,1)}, u32[]{:S(2)}, u32[]{:S(2)}) collective-permute-start(bf16[4,2,3,4,2,16,128]{6,5,4,3,2,1,0:T(8,128)(2,1)} %get-tuple-element.51), channel_id=1, source_target_pairs={{0,16},{16,0},{1,17},{17,1},{2,18},{18,2},{3,19},{19,3},{4,20},{20... | collective-permute-start | bytes 2359304 | tf_op jit(solution)/shard_map/ppermute | solution.py:23
  77.4 3.5 %all-to-all-start.2 = ((bf16[16,88,128]{2,1,0:T(8,128)(2,1)}), bf16[16,88,128]{2,1,0:T(8,128)(2,1)S(1)}, u32[]{:S(2)}, u32[]{:S(2)}) async-start(bf16[16,88,128]{2,1,0:T(8,128)(2,1)} %get-tuple-element.54), calls=%async_computation.2 | async-start | bytes 720896 | tf_op jit(solution)/shard_map/all_to_all | solution.py:701
  81.0 4.0 %shard_map.139 = (bf16[3,16,16,128]{3,2,1,0:T(8,128)(2,1)}, f32[8,128]{1,0:T(8,128)S(1)}) custom-call(s32[296]{0:T(512)S(1)} %copy-done.2, bf16[192,192]{1,0:T(8,128)(2,1)S(1)} %copy-done, bf16[24,4,2,16,128]{4,3,2,1,0:T(8,128)(2,1)} %bitcast.13.mine_ref, bf16[24,4,2,16,128]{4,3,2,1,0:T(8,128)(2,1)} %bitcast.14.other_ref, ...), custom_call_target="tpu_custom_call" | custom-call | flops 22649241600 | bytes 2097152 | tf_op jit(solution)/shard_map/pallas_call | solution.py:567
  85.0 4.9 %all-to-all-done.2 = bf16[16,88,128]{2,1,0:T(8,128)(2,1)S(1)} async-done(((bf16[16,88,128]{2,1,0:T(8,128)(2,1)}), bf16[16,88,128]{2,1,0:T(8,128)(2,1)S(1)}, u32[]{:S(2)}, u32[]{:S(2)}) %all-to-all-start.2) | async-done | bytes 360480 | tf_op jit(solution)/shard_map/all_to_all | solution.py:701
  89.9 1.7 %collective-permute-start.14 = (bf16[1408,128]{1,0:T(8,128)(2,1)S(1)}, bf16[1408,128]{1,0:T(8,128)(2,1)S(1)}, u32[]{:S(2)}, u32[]{:S(2)}) collective-permute-start(bf16[1408,128]{1,0:T(8,128)(2,1)S(1)} %shard_map.140.mine_ref), channel_id=1, source_target_pairs={{0,16},{16,0},{1,17},{17,1},{2,18},{18,2},{3,19},{19,3},{4,20},{20... | collective-permute-start | bytes 1081352 | tf_op jit(solution)/shard_map/ppermute | solution.py:23
  91.6 1.3 %collective-permute-done.14.other_ref = bf16[1408,128]{1,0:T(8,128)(2,1)S(1)} collective-permute-done((bf16[1408,128]{1,0:T(8,128)(2,1)S(1)}, bf16[1408,128]{1,0:T(8,128)(2,1)S(1)}, u32[]{:S(2)}, u32[]{:S(2)}) %collective-permute-start.14) | collective-permute-done | bytes 360480 | tf_op jit(solution)/shard_map/ppermute | solution.py:23
  92.9 1.2 %shard_map.141 = (f32[9,128,128]{2,1,0:T(8,128)}, f32[9,128,128]{2,1,0:T(8,128)}, f32[4,128,128]{2,1,0:T(8,128)}) custom-call(bf16[1408,128]{1,0:T(8,128)(2,1)S(1)} %shard_map.140.mine_ref, bf16[1408,128]{1,0:T(8,128)(2,1)S(1)} %collective-permute-done.14.other_ref), custom_call_target="tpu_custom_call" | custom-call | flops 226492416 | bytes 2097152 | tf_op jit(solution)/shard_map/pallas_call | solution.py:567
  (23 shorter events, 0.1 us)
Async XLA Ops:
  0.6 0.9 copy-start.5
  1.6 14.4 %collective-permute-start.3 = (bf16[3,4,2,16,128]{4,3,2,1,0:T(8,128)(2,1)S(1)}, bf16[3,4,2,16,128]{4,3,2,1,0:T(8,128)(2,1)S(1)}, u32[]{:S(2)}, u32[]{:S(2)}) collective-permute-start(bf16[3,4,2,16,128]{4,3,2,1,0:T(8,128)(2,1)S(1)} %shard_map.129.refs_0_), channel_id=1, source_target_pairs={{0,32},{32,0},{1,33},{33,1},{2,34},{34,2},{3,35},{35,3},{4,36},{36... | collective-permute-start | bytes 294920 | tf_op jit(solution)/shard_map/ppermute | solution.py:28
  9.4 10.5 %collective-permute-start = (bf16[3,4,2,16,128]{4,3,2,1,0:T(8,128)(2,1)S(1)}, bf16[3,4,2,16,128]{4,3,2,1,0:T(8,128)(2,1)S(1)}, u32[]{:S(2)}, u32[]{:S(2)}) collective-permute-start(bf16[3,4,2,16,128]{4,3,2,1,0:T(8,128)(2,1)S(1)} %shard_map.129.refs_0_), channel_id=1, source_target_pairs={{0,64},{64,0},{128,192},{192,128},{1,65},{65,1},{129,193},{193,129... | collective-permute-start | bytes 294920 | tf_op jit(solution)/shard_map/ppermute | solution.py:28
  10.7 13.8 %collective-permute-start.1 = (bf16[3,4,2,16,128]{4,3,2,1,0:T(8,128)(2,1)S(1)}, bf16[3,4,2,16,128]{4,3,2,1,0:T(8,128)(2,1)S(1)}, u32[]{:S(2)}, u32[]{:S(2)}) collective-permute-start(bf16[3,4,2,16,128]{4,3,2,1,0:T(8,128)(2,1)S(1)} %shard_map.129.refs_0_), channel_id=1, source_target_pairs={{0,128},{64,192},{128,0},{192,64},{1,129},{65,193},{129,1},{193,65... | collective-permute-start | bytes 294920 | tf_op jit(solution)/shard_map/ppermute | solution.py:28
  13.4 11.2 %collective-permute-start.2 = (bf16[3,4,2,16,128]{4,3,2,1,0:T(8,128)(2,1)S(1)}, bf16[3,4,2,16,128]{4,3,2,1,0:T(8,128)(2,1)S(1)}, u32[]{:S(2)}, u32[]{:S(2)}) collective-permute-start(bf16[3,4,2,16,128]{4,3,2,1,0:T(8,128)(2,1)S(1)} %shard_map.129.refs_0_), channel_id=1, source_target_pairs={{0,192},{64,128},{128,64},{192,0},{1,193},{65,129},{129,65},{193,1... | collective-permute-start | bytes 294920 | tf_op jit(solution)/shard_map/ppermute | solution.py:28
  13.4 6.6 %copy-start.3 = (bf16[3,3,128,128]{3,2,1,0:T(8,128)(2,1)S(1)}, bf16[3,3,128,128]{3,2,1,0:T(8,128)(2,1)}, u32[]{:S(2)}) copy-start(bf16[3,3,128,128]{3,2,1,0:T(8,128)(2,1)} %param.10) | copy-start | bytes 884740
  13.4 6.6 %copy-start.4 = (bf16[3,3,128,128]{3,2,1,0:T(8,128)(2,1)S(1)}, bf16[3,3,128,128]{3,2,1,0:T(8,128)(2,1)}, u32[]{:S(2)}) copy-start(bf16[3,3,128,128]{3,2,1,0:T(8,128)(2,1)} %param.11) | copy-start | bytes 884740
  13.4 6.6 %copy-start.6 = (bf16[1,3,16,16,128]{4,3,2,1,0:T(8,128)(2,1)S(1)}, bf16[1,3,16,16,128]{4,3,2,1,0:T(8,128)(2,1)}, u32[]{:S(2)}) copy-start(bf16[1,3,16,16,128]{4,3,2,1,0:T(8,128)(2,1)} %param.9) | copy-start | bytes 589828
  13.4 6.6 %copy-start.7 = (bf16[1,3,16,16,128]{4,3,2,1,0:T(8,128)(2,1)S(1)}, bf16[1,3,16,16,128]{4,3,2,1,0:T(8,128)(2,1)}, u32[]{:S(2)}) copy-start(bf16[1,3,16,16,128]{4,3,2,1,0:T(8,128)(2,1)} %param.13) | copy-start | bytes 589828
  13.4 6.6 %copy-start.8 = (bf16[2,2,128,128]{3,2,1,0:T(8,128)(2,1)S(1)}, bf16[2,2,128,128]{3,2,1,0:T(8,128)(2,1)}, u32[]{:S(2)}) copy-start(bf16[2,2,128,128]{3,2,1,0:T(8,128)(2,1)} %param.12) | copy-start | bytes 393220
  13.4 6.6 %copy-start.9 = (bf16[1,3,8,8,128]{4,3,2,1,0:T(8,128)(2,1)S(1)}, bf16[1,3,8,8,128]{4,3,2,1,0:T(8,128)(2,1)}, u32[]{:S(2)}) copy-start(bf16[1,3,8,8,128]{4,3,2,1,0:T(8,128)(2,1)} %param.14) | copy-start | bytes 147460
  16.0 8.6 %collective-permute-start.4 = (bf16[3,4,2,16,128]{4,3,2,1,0:T(8,128)(2,1)S(1)}, bf16[3,4,2,16,128]{4,3,2,1,0:T(8,128)(2,1)S(1)}, u32[]{:S(2)}, u32[]{:S(2)}) collective-permute-start(bf16[3,4,2,16,128]{4,3,2,1,0:T(8,128)(2,1)S(1)} %collective-permute-done.3.refs_4_), channel_id=1, source_target_pairs={{0,64},{64,0},{128,192},{192,128},{1,65},{65,1},{129,193},{193,129... | collective-permute-start | bytes 294920 | tf_op jit(solution)/shard_map/ppermute | solution.py:28
  16.1 8.5 %collective-permute-start.5 = (bf16[3,4,2,16,128]{4,3,2,1,0:T(8,128)(2,1)S(1)}, bf16[3,4,2,16,128]{4,3,2,1,0:T(8,128)(2,1)S(1)}, u32[]{:S(2)}, u32[]{:S(2)}) collective-permute-start(bf16[3,4,2,16,128]{4,3,2,1,0:T(8,128)(2,1)S(1)} %collective-permute-done.3.refs_4_), channel_id=1, source_target_pairs={{0,128},{64,192},{128,0},{192,64},{1,129},{65,193},{129,1},{193,65... | collective-permute-start | bytes 294920 | tf_op jit(solution)/shard_map/ppermute | solution.py:28
  19.9 5.7 %collective-permute-start.6 = (bf16[3,4,2,16,128]{4,3,2,1,0:T(8,128)(2,1)S(1)}, bf16[3,4,2,16,128]{4,3,2,1,0:T(8,128)(2,1)S(1)}, u32[]{:S(2)}, u32[]{:S(2)}) collective-permute-start(bf16[3,4,2,16,128]{4,3,2,1,0:T(8,128)(2,1)S(1)} %collective-permute-done.3.refs_4_), channel_id=1, source_target_pairs={{0,192},{64,128},{128,64},{192,0},{1,193},{65,129},{129,65},{193,1... | collective-permute-start | bytes 294920 | tf_op jit(solution)/shard_map/ppermute | solution.py:28
  20.0 0.7 copy-start.1
  24.5 6.2 %copy-start = (bf16[192,192]{1,0:T(8,128)(2,1)S(1)}, bf16[192,192]{1,0:T(8,128)(2,1)}, u32[]{:S(2)}) copy-start(bf16[192,192]{1,0:T(8,128)(2,1)} %get-tuple-element.33.turn_ref) | copy-start | bytes 221188
  26.3 4.5 %collective-permute-start.7 = (bf16[4,2,3,4,2,16,128]{6,5,4,3,2,1,0:T(8,128)(2,1)S(1)}, bf16[4,2,3,4,2,16,128]{6,5,4,3,2,1,0:T(8,128)(2,1)S(1)}, u32[]{:S(2)}, u32[]{:S(2)}) collective-permute-start(bf16[4,2,3,4,2,16,128]{6,5,4,3,2,1,0:T(8,128)(2,1)S(1)} %shard_map.131), channel_id=1, source_target_pairs={{0,16},{16,0},{1,17},{17,1},{2,18},{18,2},{3,19},{19,3},{4,20},{20... | collective-permute-start | bytes 2359304 | tf_op jit(solution)/shard_map/ppermute | solution.py:23
  37.0 2.7 %collective-permute-start.8 = (f32[1408,128]{1,0:T(8,128)S(1)}, f32[1408,128]{1,0:T(8,128)S(1)}, u32[]{:S(2)}, u32[]{:S(2)}) collective-permute-start(f32[1408,128]{1,0:T(8,128)S(1)} %slice_bitcast_fusion), channel_id=1, source_target_pairs={{0,16},{16,0},{1,17},{17,1},{2,18},{18,2},{3,19},{19,3},{4,20},{20... | collective-permute-start | bytes 2162696 | tf_op jit(solution)/shard_map/ppermute | solution.py:23
  37.5 8.7 %collective-permute-start.9 = (bf16[3,4,2,16,128]{4,3,2,1,0:T(8,128)(2,1)S(1)}, bf16[3,4,2,16,128]{4,3,2,1,0:T(8,128)(2,1)S(1)}, u32[]{:S(2)}, u32[]{:S(2)}) collective-permute-start(bf16[3,4,2,16,128]{4,3,2,1,0:T(8,128)(2,1)S(1)} %get-tuple-element.48.own_ref), channel_id=1, source_target_pairs={{0,32},{32,0},{1,33},{33,1},{2,34},{34,2},{3,35},{35,3},{4,36},{36... | collective-permute-start | bytes 294920 | tf_op jit(solution)/shard_map/ppermute | solution.py:28
  40.5 13.7 %all-to-all-start = ((bf16[16,88,128]{2,1,0:T(8,128)(2,1)}), bf16[16,88,128]{2,1,0:T(8,128)(2,1)S(1)}, u32[]{:S(2)}, u32[]{:S(2)}) async-start(bf16[16,88,128]{2,1,0:T(8,128)(2,1)} %bitcast.12), calls=%async_computation | async-start | bytes 720896 | tf_op jit(solution)/shard_map/all_to_all | solution.py:687
  54.9 8.3 %collective-permute-start.10 = (bf16[2,3,4,2,16,128]{5,4,3,2,1,0:T(8,128)(2,1)S(1)}, bf16[2,3,4,2,16,128]{5,4,3,2,1,0:T(8,128)(2,1)S(1)}, u32[]{:S(2)}, u32[]{:S(2)}) collective-permute-start(bf16[2,3,4,2,16,128]{5,4,3,2,1,0:T(8,128)(2,1)S(1)} %get-tuple-element.50.own_ref), channel_id=1, source_target_pairs={{0,64},{64,0},{128,192},{192,128},{1,65},{65,1},{129,193},{193,129... | collective-permute-start | bytes 589832 | tf_op jit(solution)/shard_map/ppermute | solution.py:28
  55.3 9.4 %collective-permute-start.11 = (bf16[2,3,4,2,16,128]{5,4,3,2,1,0:T(8,128)(2,1)S(1)}, bf16[2,3,4,2,16,128]{5,4,3,2,1,0:T(8,128)(2,1)S(1)}, u32[]{:S(2)}, u32[]{:S(2)}) collective-permute-start(bf16[2,3,4,2,16,128]{5,4,3,2,1,0:T(8,128)(2,1)S(1)} %get-tuple-element.50.own_ref), channel_id=1, source_target_pairs={{0,128},{64,192},{128,0},{192,64},{1,129},{65,193},{129,1},{193,65... | collective-permute-start | bytes 589832 | tf_op jit(solution)/shard_map/ppermute | solution.py:28
  57.5 10.6 %collective-permute-start.12 = (bf16[2,3,4,2,16,128]{5,4,3,2,1,0:T(8,128)(2,1)S(1)}, bf16[2,3,4,2,16,128]{5,4,3,2,1,0:T(8,128)(2,1)S(1)}, u32[]{:S(2)}, u32[]{:S(2)}) collective-permute-start(bf16[2,3,4,2,16,128]{5,4,3,2,1,0:T(8,128)(2,1)S(1)} %get-tuple-element.50.own_ref), channel_id=1, source_target_pairs={{0,192},{64,128},{128,64},{192,0},{1,193},{65,129},{129,65},{193,1... | collective-permute-start | bytes 589832 | tf_op jit(solution)/shard_map/ppermute | solution.py:28
  58.8 13.0 %all-to-all-start.1 = ((bf16[8,88,128]{2,1,0:T(8,128)(2,1)}), bf16[8,88,128]{2,1,0:T(8,128)(2,1)S(1)}, u32[]{:S(2)}, u32[]{:S(2)}) async-start(bf16[8,88,128]{2,1,0:T(8,128)(2,1)} %get-tuple-element.49), calls=%async_computation.1 | async-start | bytes 360448 | tf_op jit(solution)/shard_map/all_to_all | solution.py:694
  68.1 12.9 %copy-start.2 = (s32[296]{0:T(512)S(1)}, s32[296]{0:T(512)}, u32[]{:S(2)}) copy-start(s32[296]{0:T(512)} %get-tuple-element.32.index_ref.refs_8_) | copy-start | bytes 3556
  72.9 8.1 %collective-permute-start.13 = (bf16[4,2,3,4,2,16,128]{6,5,4,3,2,1,0:T(8,128)(2,1)}, bf16[4,2,3,4,2,16,128]{6,5,4,3,2,1,0:T(8,128)(2,1)}, u32[]{:S(2)}, u32[]{:S(2)}) collective-permute-start(bf16[4,2,3,4,2,16,128]{6,5,4,3,2,1,0:T(8,128)(2,1)} %get-tuple-element.51), channel_id=1, source_target_pairs={{0,16},{16,0},{1,17},{17,1},{2,18},{18,2},{3,19},{19,3},{4,20},{20... | collective-permute-start | bytes 2359304 | tf_op jit(solution)/shard_map/ppermute | solution.py:23
  77.4 12.4 %all-to-all-start.2 = ((bf16[16,88,128]{2,1,0:T(8,128)(2,1)}), bf16[16,88,128]{2,1,0:T(8,128)(2,1)S(1)}, u32[]{:S(2)}, u32[]{:S(2)}) async-start(bf16[16,88,128]{2,1,0:T(8,128)(2,1)} %get-tuple-element.54), calls=%async_computation.2 | async-start | bytes 720896 | tf_op jit(solution)/shard_map/all_to_all | solution.py:701
  89.9 3.0 %collective-permute-start.14 = (bf16[1408,128]{1,0:T(8,128)(2,1)S(1)}, bf16[1408,128]{1,0:T(8,128)(2,1)S(1)}, u32[]{:S(2)}, u32[]{:S(2)}) collective-permute-start(bf16[1408,128]{1,0:T(8,128)(2,1)S(1)} %shard_map.140.mine_ref), channel_id=1, source_target_pairs={{0,16},{16,0},{1,17},{17,1},{2,18},{18,2},{3,19},{19,3},{4,20},{20... | collective-permute-start | bytes 1081352 | tf_op jit(solution)/shard_map/ppermute | solution.py:23
